TPU v7x, 32 devices: a whole 2x2x4 slice. The times are simulated.
32 devices in a mesh: wide: 16 (over z, y, core), narrow: 2 (over x).
Axes of the slice: x: 2, y: 2, z: 4, core: 2. Of those that a mesh axis runs over, the one named last changes fastest.
Arguments:
- right_side: float32 [128, 32, 512], P('wide', 'narrow'), may hold values from -18 to 18
- diagonal: float32 [128, 32, 512], P('wide', 'narrow'), may hold values from 0.01 to 2
- coarse_slot: int32 [16, 4, 64], P('wide', 'narrow'), may hold values from 0 to 127, as said below
- coarse_factor: float32 [4096, 2048], P(('wide', 'narrow')), may hold values from -0.125 to 0.125
Outputs:
- solution_field: float32 [128, 32, 512], P('wide', 'narrow')
- residual: float32 [128, 32, 512], P('wide', 'narrow')
Inputs may be any that keep to these rules, and one draw needn't show every extreme that they name: `coarse_slot`: within each device block the slots of its 128 elements, in row-major order over the block's elements, are a permutation of 0 to 127.
All inputs are finite; a program needn't handle non-finite values.
Results may differ from a plain program's by a relative error of at most 0.0003.
Values sent between devices are 32-bit elements; how exact they have to be, the bound alone decides.
No kernel may reach another device: no remote copies, remote signals or barrier semaphores. Data moves between devices by JAX's collectives and lax.ppermute only.
A program may use at most 64 MiB of HBM per device.

v0:
```python
import jax
import jax.numpy as jnp
from jax import lax
from jax.sharding import PartitionSpec as P

ITERS = 2


def padded_2(x, sides, width):
    for axis, dim in sides:
        size, length = (lax.axis_size(axis), x.shape[dim])
        up = [(i, (i + 1) % size) for i in range(size - 1)]
        down = [(j, i) for i, j in up]
        last = lax.slice_in_dim(x, length - width, length, axis=dim)
        initial = lax.slice_in_dim(x, 0, width, axis=dim)
        before = lax.ppermute(last, axis, up)
        after = lax.ppermute(initial, axis, down)
        x = jnp.concatenate([before, x, after], axis=dim)
    return x


def sine_table():
    indices = jnp.arange(10, dtype=jnp.float32)
    sine_basis = jnp.sqrt(2.0 / 11.0) * jnp.sin(
        jnp.pi * (indices[:, None] + 1.0) * (indices[None, :] + 1.0) / 11.0
    )
    values = 2.0 - 2.0 * jnp.cos(jnp.pi * (indices + 1.0) / 11.0)
    return (sine_basis, values)


def front_windows(values_in):
    length = values_in.shape[0] - 2
    count = length // 8
    middle = values_in[1 : length + 1].reshape((count, 8) + values_in.shape[1:])
    before = values_in[0:length:8][:, None]
    after = values_in[9 : length + 2 : 8][:, None]
    return jnp.concatenate([before, middle, after], axis=1)


def schwarz(extended, sigma):
    count_x, count_y, count_z = sigma.shape
    sine_basis, values = sine_table()
    precise = lax.Precision.HIGHEST
    blocks = front_windows(extended)
    blocks = front_windows(jnp.moveaxis(blocks, 2, 0))
    blocks = front_windows(jnp.moveaxis(blocks, 4, 0))
    blocks = blocks.transpose(5, 3, 1, 4, 2, 0).reshape(10, 10, 10, -1)
    spectra = jnp.einsum("ia,ijke->ajke", sine_basis, blocks, precision=precise)
    spectra = jnp.einsum("jb,ajke->abke", sine_basis, spectra, precision=precise)
    spectra = jnp.einsum("kc,abke->abce", sine_basis, spectra, precision=precise)
    spread = values[:, None, None] + values[None, :, None] + values[None, None, :]
    spectra = spectra / (spread[:, :, :, None] + sigma.reshape(-1)[None, None, None, :])
    interior_basis = sine_basis[1:9]
    nodal = jnp.einsum("ia,abce->ibce", interior_basis, spectra, precision=precise)
    nodal = jnp.einsum("jb,ibce->ijce", interior_basis, nodal, precision=precise)
    nodal = jnp.einsum("kc,ijce->ijke", interior_basis, nodal, precision=precise)
    nodal = nodal.reshape(8, 8, 8, count_x, count_y, count_z).transpose(3, 0, 4, 1, 5, 2)
    return nodal.reshape(8 * count_x, 8 * count_y, 8 * count_z)


def element_sums(field_values):
    size_x, size_y, size_z = field_values.shape
    return field_values.reshape(size_x // 8, 8, size_y // 8, 8, size_z // 8, 8).sum(axis=(1, 3, 5))


def expand(element_values):
    count_x, count_y, count_z = element_values.shape
    spread_out = jnp.broadcast_to(
        element_values[:, None, :, None, :, None], (count_x, 8, count_y, 8, count_z, 8)
    )
    return spread_out.reshape(8 * count_x, 8 * count_y, 8 * count_z)


def operate(padded, coefficient):
    centre = padded[1:-1, 1:-1, 1:-1]
    beside = padded[2:, 1:-1, 1:-1] + padded[:-2, 1:-1, 1:-1]
    beside = beside + padded[1:-1, 2:, 1:-1] + padded[1:-1, :-2, 1:-1]
    beside = beside + padded[1:-1, 1:-1, 2:] + padded[1:-1, 1:-1, :-2]
    return (6.0 + coefficient) * centre - beside


def pad_depth(field_values):
    return jnp.pad(field_values, ((0, 0), (0, 0), (1, 1)))


def fine_solve(extended_rows, sigma):
    return schwarz(pad_depth(extended_rows), sigma)


def global_sum(local_value):
    return lax.psum(local_value, ("wide", "narrow"))


def coarse_term(residual, slot_list, coarse_factor):
    groups = lax.axis_size("narrow")
    totals = element_sums(residual) / 16.0
    elem_count = slot_list.shape[0]
    owner_share = elem_count // groups
    outgoing = (
        jnp.zeros((elem_count,), jnp.float32)
        .at[slot_list]
        .set(totals.reshape(-1))
        .reshape(groups, owner_share)
    )
    owned_rows = lax.all_to_all(outgoing, "narrow", split_axis=0, concat_axis=0, tiled=True)
    precise = lax.Precision.HIGHEST
    partial_proj = jnp.dot(owned_rows.reshape(-1), coarse_factor, precision=precise)
    slab_proj = lax.psum(partial_proj, "wide")
    projected = lax.psum(slab_proj, "narrow")
    corrected = jnp.dot(coarse_factor, projected, precision=precise).reshape(groups, owner_share)
    returned = lax.all_to_all(corrected, "narrow", split_axis=0, concat_axis=0, tiled=True)
    return expand(returned.reshape(-1)[slot_list].reshape(totals.shape) / 16.0)


def residual_solve(residual, sigma, slot_list, coarse_factor):
    extended_rows = padded_2(residual, (("wide", 0), ("narrow", 1)), 1)
    return fine_solve(extended_rows, sigma) + coarse_term(residual, slot_list, coarse_factor)


def apply_operator(direction, diagonal):
    extended_rows = padded_2(direction, (("wide", 0), ("narrow", 1)), 1)
    return operate(pad_depth(extended_rows), diagonal)


def body(right_side, diagonal, coarse_slot, coarse_factor):
    sigma = element_sums(diagonal) / 512.0
    slot_list = coarse_slot.reshape(-1)
    solution = jnp.zeros_like(right_side)
    residual = right_side
    search = residual_solve(residual, sigma, slot_list, coarse_factor)
    product_now = global_sum(jnp.sum(residual * search))
    direction = search
    for sweep in range(ITERS):
        image_field = apply_operator(direction, diagonal)
        step_size = product_now / global_sum(jnp.sum(direction * image_field))
        solution = solution + step_size * direction
        residual = residual - step_size * image_field
        if sweep + 1 < ITERS:
            search = residual_solve(residual, sigma, slot_list, coarse_factor)
            product_next = global_sum(jnp.sum(residual * search))
            direction = search + product_next / product_now * direction
            product_now = product_next
    return (solution, residual)


def solution(mesh):
    in_specs = (
        P("wide", "narrow", None),
        P("wide", "narrow", None),
        P("wide", "narrow", None),
        P(("wide", "narrow"), None),
    )
    out_specs = (P("wide", "narrow", None), P("wide", "narrow", None))
    return jax.shard_map(body, mesh=mesh, in_specs=in_specs, out_specs=out_specs, check_vma=False)
```

profile of v0, /device:TPU:0, one launch (start us, length us, event | category | flops | bytes accessed | tf_op | source)
XLA Modules:
  0.0 362.5 jit_solution(13324696848276107061)
XLA Ops:
  1.5 1.3 collective-permute-start.1
  2.8 3.0 collective-permute-start
  6.8 1.0 reduce_sum.68
  8.5 1.0 fusion.81
  10.0 1.0 scatter_custom_fusion
  11.6 4.2 %all-to-all-start = ((f32[2,1,64]{2,1,0:T(1,128)}), f32[2,1,64]{2,1,0:T(1,128)S(1)}, u32[]{:S(2)}, u32[]{:S(2)}) async-start(f32[2,1,64]{2,1,0:T(1,128)} %bitcast.26), calls=%async_computation | async-start | bytes 2048 | tf_op jit(solution)/shard_map/all_to_all | solution.py:105
  15.8 3.7 %all-to-all-done = f32[2,1,64]{2,1,0:T(1,128)S(1)} async-done(((f32[2,1,64]{2,1,0:T(1,128)}), f32[2,1,64]{2,1,0:T(1,128)S(1)}, u32[]{:S(2)}, u32[]{:S(2)}) %all-to-all-start) | async-done | bytes 544 | tf_op jit(solution)/shard_map/all_to_all | solution.py:105
  21.4 32.8 %psum.56 = f32[2048]{0:T(1024)S(1)} all-reduce(f32[2048]{0:T(1024)S(1)} %bitcast.156), channel_id=1, replica_groups=mesh['wide'=16,'narrow'=2] {'wide'}, use_global_device_ids=true, to_apply=%region_5.6 | all-reduce | flops 2048 | bytes 16384 | tf_op jit(solution)/shard_map/psum | solution.py:108
  54.2 5.0 %psum.57 = f32[2048]{0:T(1024)S(1)} all-reduce(f32[2048]{0:T(1024)S(1)} %psum.56), channel_id=1, replica_groups=mesh['wide'=16,'narrow'=2] {'narrow'}, use_global_device_ids=true, to_apply=%region_6.7 | all-reduce | flops 2048 | bytes 16384 | tf_op jit(solution)/shard_map/psum | solution.py:109
  59.2 0.9 convolution_bitcast_fusion.9
  60.8 3.2 all-to-all-start.1
  64.0 3.9 %collective-permute-start.2 = (f32[10,1,512]{2,1,0:T(1,128)S(1)}, f32[10,1,512]{2,1,0:T(1,128)S(1)}, u32[]{:S(2)}, u32[]{:S(2)}) collective-permute-start(f32[10,1,512]{2,1,0:T(1,128)S(1)} %get-tuple-element.21), channel_id=1, source_target_pairs={{0,1},{2,3},{4,5},{6,7},{8,9},{10,11},{12,13},{14,15},{16,17},{18,... | collective-permute-start | bytes 61448 | tf_op jit(solution)/shard_map/ppermute | solution.py:16
  67.9 1.5 collective-permute-start.3
  70.2 1.2 gather_fusion
  71.9 1.7 collective-permute-done.3
  74.9 3.1 slice.195
  78.0 3.1 slice.193
  81.5 5.4 %reshape.237 = f32[64,8,2,10,1,10]{1,0,2,5,3,4:T(8,128)} reshape(f32[512,2,10,1,10]{0,1,4,2,3:T(2,128)S(1)} %slice.240) | data formatting | bytes 819200 | tf_op jit(solution)/shard_map/reshape | solution.py:34
  87.0 4.5 %copy.92 = f32[64,8,2,10,1,10]{0,2,5,4,3,1:T(2,128)S(1)} copy(f32[64,8,2,10,1,10]{1,0,2,5,3,4:T(8,128)} %reshape.237) | data formatting | bytes 819200 | tf_op jit(solution)/shard_map/reshape | solution.py:34
  92.6 1.0 fusion.4
  93.6 1.3 convolution_bitcast_fusion.3
  94.9 1.1 fusion.1
  98.4 2.6 copy.104
  101.0 4.0 %reshape.240 = f32[8,16,512]{2,1,0:T(8,128)S(1)} reshape(f32[1,8,2,8,64,8]{5,4,3,2,1,0:T(8,128)} %bitcast.146) | data formatting | bytes 524288 | tf_op jit(solution)/shard_map/reshape | solution.py:58
  105.0 1.3 collective-permute-start.5
  106.3 1.3 collective-permute-start.4
  107.6 1.8 collective-permute-done.4
  109.5 2.8 collective-permute-start.7
  112.3 1.3 collective-permute-start.6
  113.8 4.2 %collective-permute-done.6 = f32[10,1,512]{2,1,0:T(1,128)S(1)} collective-permute-done((f32[10,1,512]{2,1,0:T(1,128)S(1)}, f32[10,1,512]{2,1,0:T(1,128)S(1)}, u32[]{:S(2)}, u32[]{:S(2)}) %collective-permute-start.6) | collective-permute-done | bytes 20512 | tf_op jit(solution)/shard_map/ppermute | solution.py:17
  118.3 0.9 multiply_reduce_fusion.2
  119.3 37.1 %all-reduce.4 = (f32[]{:T(128)}, f32[]{:T(128)}) all-reduce(f32[]{:T(128)} %get-tuple-element.3, f32[]{:T(128)} %get-tuple-element.2), channel_id=1, replica_groups=mesh['wide'=16,'narrow'=2] {'wide','narrow'}, use_global_device_ids=true, to_apply=%region_8.9 | all-reduce | flops 2 | bytes 16 | tf_op jit(solution)/shard_map/psum | solution.py:91
  158.3 1.0 scatter_custom_fusion.1
  159.9 3.5 all-to-all-start.2
  163.4 1.3 collective-permute-start.8
  164.7 1.3 collective-permute-start.9
  166.0 1.1 all-to-all-done.2
  168.5 34.2 %psum.60 = f32[2048]{0:T(1024)S(1)} all-reduce(f32[2048]{0:T(1024)S(1)} %bitcast.158), channel_id=1, replica_groups=mesh['wide'=16,'narrow'=2] {'wide'}, use_global_device_ids=true, to_apply=%region_14.15 | all-reduce | flops 2048 | bytes 16384 | tf_op jit(solution)/shard_map/psum | solution.py:108
  202.6 5.0 %psum.61 = f32[2048]{0:T(1024)S(1)} all-reduce(f32[2048]{0:T(1024)S(1)} %psum.60), channel_id=1, replica_groups=mesh['wide'=16,'narrow'=2] {'narrow'}, use_global_device_ids=true, to_apply=%region_15.16 | all-reduce | flops 2048 | bytes 16384 | tf_op jit(solution)/shard_map/psum | solution.py:109
  207.6 0.9 convolution_bitcast_fusion.8
  208.6 6.8 %all_to_all.36 = f32[2,1,64]{2,1,0:T(1,128)S(1)} all-to-all(f32[2,1,64]{2,1,0:T(1,128)S(1)} %bitcast.160), channel_id=1, replica_groups=mesh['wide'=16,'narrow'=2] {'narrow'}, dimensions={0} | all-to-all | bytes 1024 | tf_op jit(solution)/shard_map/all_to_all | solution.py:111
  216.2 1.2 gather_fusion.1
  217.5 1.9 collective-permute-start.10
  219.4 1.3 collective-permute-start.11
  221.2 3.9 %collective-permute-done.11 = f32[10,1,512]{2,1,0:T(1,128)S(1)} collective-permute-done((f32[10,1,512]{2,1,0:T(1,128)S(1)}, f32[10,1,512]{2,1,0:T(1,128)S(1)}, u32[]{:S(2)}, u32[]{:S(2)}) %collective-permute-start.11) | collective-permute-done | bytes 20512 | tf_op jit(solution)/shard_map/ppermute | solution.py:17
  226.6 3.1 slice.218
  229.7 3.1 slice.216
  233.3 5.4 %reshape.246 = f32[64,8,2,10,1,10]{1,0,2,5,3,4:T(8,128)} reshape(f32[512,2,10,1,10]{0,1,4,2,3:T(2,128)S(1)} %slice.251) | data formatting | bytes 819200 | tf_op jit(solution)/shard_map/reshape | solution.py:34
  238.7 5.4 %copy.111 = f32[64,8,2,10,1,10]{0,2,5,4,3,1:T(2,128)} copy(f32[64,8,2,10,1,10]{1,0,2,5,3,4:T(8,128)} %reshape.246) | data formatting | bytes 819200 | tf_op jit(solution)/shard_map/reshape | solution.py:34
  244.1 1.7 maximum_bitcast_fusion.1
  245.8 1.5 reshape.301
  247.3 2.1 fusion.2
  249.4 1.3 convolution_bitcast_fusion.1
  250.7 1.1 fusion
  254.1 2.6 copy.123
  256.7 4.0 %reshape.249 = f32[8,16,512]{2,1,0:T(8,128)S(1)} reshape(f32[1,8,2,8,64,8]{5,4,3,2,1,0:T(8,128)} %bitcast.147) | data formatting | bytes 524288 | tf_op jit(solution)/shard_map/reshape | solution.py:58
  261.4 37.1 %psum.62 = f32[]{:T(128)} all-reduce(f32[]{:T(128)} %multiply_reduce_fusion.1), channel_id=1, replica_groups=mesh['wide'=16,'narrow'=2] {'wide','narrow'}, use_global_device_ids=true, to_apply=%region_17.18 | all-reduce | flops 1 | bytes 8 | tf_op jit(solution)/shard_map/psum | solution.py:91
  299.8 1.3 collective-permute-start.13
  301.1 1.3 collective-permute-start.12
  302.4 4.5 %collective-permute-done.12 = f32[1,16,512]{2,1,0:T(8,128)S(1)} collective-permute-done((f32[1,16,512]{2,1,0:T(8,128)S(1)}, f32[1,16,512]{2,1,0:T(8,128)S(1)}, u32[]{:S(2)}, u32[]{:S(2)}) %collective-permute-start.12) | collective-permute-done | bytes 32800 | tf_op jit(solution)/shard_map/ppermute | solution.py:17
  307.0 1.9 collective-permute-start.15
  308.9 1.3 collective-permute-start.14
  310.4 4.2 %collective-permute-done.14 = f32[10,1,512]{2,1,0:T(1,128)S(1)} collective-permute-done((f32[10,1,512]{2,1,0:T(1,128)S(1)}, f32[10,1,512]{2,1,0:T(1,128)S(1)}, u32[]{:S(2)}, u32[]{:S(2)}) %collective-permute-start.14) | collective-permute-done | bytes 20512 | tf_op jit(solution)/shard_map/ppermute | solution.py:17
  315.8 43.9 %psum.63 = f32[]{:T(128)} all-reduce(f32[]{:T(128)} %get-tuple-element.6), channel_id=1, replica_groups=mesh['wide'=16,'narrow'=2] {'wide','narrow'}, use_global_device_ids=true, to_apply=%region_19.20 | all-reduce | flops 1 | bytes 8 | tf_op jit(solution)/shard_map/psum | solution.py:91
  (109 shorter events, 24.9 us)
Async XLA Ops:
  0.6 20.1 %copy-start = (f32[128,2048]{1,0:T(8,128)S(1)}, f32[128,2048]{1,0:T(8,128)}, u32[]{:S(2)}) copy-start(f32[128,2048]{1,0:T(8,128)} %param.7) | copy-start | bytes 3145732
  1.5 14.3 %collective-permute-start.1 = (f32[1,16,512]{2,1,0:T(8,128)S(1)}, f32[1,16,512]{2,1,0:T(8,128)S(1)}, u32[]{:S(2)}, u32[]{:S(2)}) collective-permute-start(f32[1,16,512]{2,1,0:T(8,128)S(1)} %get-tuple-element.31), channel_id=1, source_target_pairs={{2,0},{4,2},{6,4},{8,6},{10,8},{12,10},{14,12},{16,14},{18,16},{20... | collective-permute-start | bytes 98312 | tf_op jit(solution)/shard_map/ppermute | solution.py:17
  2.8 5.7 %collective-permute-start = (f32[1,16,512]{2,1,0:T(8,128)S(1)}, f32[1,16,512]{2,1,0:T(8,128)S(1)}, u32[]{:S(2)}, u32[]{:S(2)}) collective-permute-start(f32[1,16,512]{2,1,0:T(8,128)S(1)} %get-tuple-element.32), channel_id=1, source_target_pairs={{0,2},{2,4},{4,6},{6,8},{8,10},{10,12},{12,14},{14,16},{16,18},{18... | collective-permute-start | bytes 98312 | tf_op jit(solution)/shard_map/ppermute | solution.py:16
  11.6 7.9 %all-to-all-start = ((f32[2,1,64]{2,1,0:T(1,128)}), f32[2,1,64]{2,1,0:T(1,128)S(1)}, u32[]{:S(2)}, u32[]{:S(2)}) async-start(f32[2,1,64]{2,1,0:T(1,128)} %bitcast.26), calls=%async_computation | async-start | bytes 2048 | tf_op jit(solution)/shard_map/all_to_all | solution.py:105
  60.8 8.6 %all-to-all-start.1 = ((f32[2,1,64]{2,1,0:T(1,128)}), f32[2,1,64]{2,1,0:T(1,128)S(1)}, u32[]{:S(2)}, u32[]{:S(2)}) async-start(f32[2,1,64]{2,1,0:T(1,128)} %bitcast.30), calls=%async_computation.1 | async-start | bytes 2048 | tf_op jit(solution)/shard_map/all_to_all | solution.py:111
  64.0 7.9 %collective-permute-start.2 = (f32[10,1,512]{2,1,0:T(1,128)S(1)}, f32[10,1,512]{2,1,0:T(1,128)S(1)}, u32[]{:S(2)}, u32[]{:S(2)}) collective-permute-start(f32[10,1,512]{2,1,0:T(1,128)S(1)} %get-tuple-element.21), channel_id=1, source_target_pairs={{0,1},{2,3},{4,5},{6,7},{8,9},{10,11},{12,13},{14,15},{16,17},{18,... | collective-permute-start | bytes 61448 | tf_op jit(solution)/shard_map/ppermute | solution.py:16
  67.9 5.7 %collective-permute-start.3 = (f32[10,1,512]{2,1,0:T(1,128)S(1)}, f32[10,1,512]{2,1,0:T(1,128)S(1)}, u32[]{:S(2)}, u32[]{:S(2)}) collective-permute-start(f32[10,1,512]{2,1,0:T(1,128)S(1)} %get-tuple-element.22), channel_id=1, source_target_pairs={{1,0},{3,2},{5,4},{7,6},{9,8},{11,10},{13,12},{15,14},{17,16},{19,... | collective-permute-start | bytes 61448 | tf_op jit(solution)/shard_map/ppermute | solution.py:17
  97.5 20.8 %copy-start.1 = (f32[8,16,512]{2,1,0:T(8,128)S(1)}, f32[8,16,512]{2,1,0:T(8,128)}, u32[]{:S(2)}) copy-start(f32[8,16,512]{2,1,0:T(8,128)} %param.4) | copy-start | bytes 786436
  97.5 20.8 %copy-start.2 = (f32[8,16,512]{2,1,0:T(8,128)S(1)}, f32[8,16,512]{2,1,0:T(8,128)}, u32[]{:S(2)}) copy-start(f32[8,16,512]{2,1,0:T(8,128)} %param.5) | copy-start | bytes 786436
  105.0 2.6 collective-permute-start.5
  106.3 3.1 collective-permute-start.4
  109.5 4.3 %collective-permute-start.7 = (f32[10,1,512]{2,1,0:T(1,128)S(1)}, f32[10,1,512]{2,1,0:T(1,128)S(1)}, u32[]{:S(2)}, u32[]{:S(2)}) collective-permute-start(f32[10,1,512]{2,1,0:T(1,128)S(1)} %get-tuple-element.19), channel_id=1, source_target_pairs={{0,1},{2,3},{4,5},{6,7},{8,9},{10,11},{12,13},{14,15},{16,17},{18,... | collective-permute-start | bytes 61448 | tf_op jit(solution)/shard_map/ppermute | solution.py:16
  112.3 5.7 %collective-permute-start.6 = (f32[10,1,512]{2,1,0:T(1,128)S(1)}, f32[10,1,512]{2,1,0:T(1,128)S(1)}, u32[]{:S(2)}, u32[]{:S(2)}) collective-permute-start(f32[10,1,512]{2,1,0:T(1,128)S(1)} %get-tuple-element.20), channel_id=1, source_target_pairs={{1,0},{3,2},{5,4},{7,6},{9,8},{11,10},{13,12},{15,14},{17,16},{19,... | collective-permute-start | bytes 61448 | tf_op jit(solution)/shard_map/ppermute | solution.py:17
  159.9 7.2 %all-to-all-start.2 = ((f32[2,1,64]{2,1,0:T(1,128)}), f32[2,1,64]{2,1,0:T(1,128)S(1)}, u32[]{:S(2)}, u32[]{:S(2)}) async-start(f32[2,1,64]{2,1,0:T(1,128)} %bitcast.55), calls=%async_computation.2 | async-start | bytes 2048 | tf_op jit(solution)/shard_map/all_to_all | solution.py:105
  163.4 54.0 %collective-permute-start.8 = (f32[1,16,512]{2,1,0:T(8,128)S(1)}, f32[1,16,512]{2,1,0:T(8,128)S(1)}, u32[]{:S(2)}, u32[]{:S(2)}) collective-permute-start(f32[1,16,512]{2,1,0:T(8,128)S(1)} %get-tuple-element.25), channel_id=1, source_target_pairs={{0,2},{2,4},{4,6},{6,8},{8,10},{10,12},{12,14},{14,16},{16,18},{18... | collective-permute-start | bytes 98312 | tf_op jit(solution)/shard_map/ppermute | solution.py:16
  164.7 52.7 %collective-permute-start.9 = (f32[1,16,512]{2,1,0:T(8,128)S(1)}, f32[1,16,512]{2,1,0:T(8,128)S(1)}, u32[]{:S(2)}, u32[]{:S(2)}) collective-permute-start(f32[1,16,512]{2,1,0:T(8,128)S(1)} %get-tuple-element.26), channel_id=1, source_target_pairs={{2,0},{4,2},{6,4},{8,6},{10,8},{12,10},{14,12},{16,14},{18,16},{20... | collective-permute-start | bytes 98312 | tf_op jit(solution)/shard_map/ppermute | solution.py:17
  217.5 3.7 %collective-permute-start.10 = (f32[10,1,512]{2,1,0:T(1,128)S(1)}, f32[10,1,512]{2,1,0:T(1,128)S(1)}, u32[]{:S(2)}, u32[]{:S(2)}) collective-permute-start(f32[10,1,512]{2,1,0:T(1,128)S(1)} %get-tuple-element.17), channel_id=1, source_target_pairs={{0,1},{2,3},{4,5},{6,7},{8,9},{10,11},{12,13},{14,15},{16,17},{18,... | collective-permute-start | bytes 61448 | tf_op jit(solution)/shard_map/ppermute | solution.py:16
  219.4 5.7 %collective-permute-start.11 = (f32[10,1,512]{2,1,0:T(1,128)S(1)}, f32[10,1,512]{2,1,0:T(1,128)S(1)}, u32[]{:S(2)}, u32[]{:S(2)}) collective-permute-start(f32[10,1,512]{2,1,0:T(1,128)S(1)} %get-tuple-element.18), channel_id=1, source_target_pairs={{1,0},{3,2},{5,4},{7,6},{9,8},{11,10},{13,12},{15,14},{17,16},{19,... | collective-permute-start | bytes 61448 | tf_op jit(solution)/shard_map/ppermute | solution.py:17
  299.8 2.6 collective-permute-start.13
  301.1 5.8 %collective-permute-start.12 = (f32[1,16,512]{2,1,0:T(8,128)S(1)}, f32[1,16,512]{2,1,0:T(8,128)S(1)}, u32[]{:S(2)}, u32[]{:S(2)}) collective-permute-start(f32[1,16,512]{2,1,0:T(8,128)S(1)} %get-tuple-element.24), channel_id=1, source_target_pairs={{2,0},{4,2},{6,4},{8,6},{10,8},{12,10},{14,12},{16,14},{18,16},{20... | collective-permute-start | bytes 98312 | tf_op jit(solution)/shard_map/ppermute | solution.py:17
  307.0 3.4 collective-permute-start.15
  308.9 5.7 %collective-permute-start.14 = (f32[10,1,512]{2,1,0:T(1,128)S(1)}, f32[10,1,512]{2,1,0:T(1,128)S(1)}, u32[]{:S(2)}, u32[]{:S(2)}) collective-permute-start(f32[10,1,512]{2,1,0:T(1,128)S(1)} %get-tuple-element.16), channel_id=1, source_target_pairs={{1,0},{3,2},{5,4},{7,6},{9,8},{11,10},{13,12},{15,14},{17,16},{19,... | collective-permute-start | bytes 61448 | tf_op jit(solution)/shard_map/ppermute | solution.py:17
where the time goes:
time: 364 us; the launch traced here: 363 us
  blocking collectives  202 us (55%)
  local copies, waits for them, and re-layouts  62.4 us (17%)
  starting transfers between devices  38.9 us (11%)
  waiting for transfers between devices  25.4 us (7%)
  matrix products  14.8 us (4%)
  other arithmetic  13.7 us (4%)
  between operations  5.35 us (1%)
    psum x3, blocking collectives, global_sum(): return lax.psum(local_value, ('wide', 'narrow'))  118 us
    psum x2, blocking collectives, coarse_term(): slab_proj = lax.psum(partial_proj, 'wide')  67 us
    reshape x10, local copies, waits for them, and re-layouts, front_windows(): middle = values_in[1:length + 1].reshape((count, 8) + values_in.shape[1:])  21.3 us
    ppermute x8, waiting for transfers between devices, padded_2(): after = lax.ppermute(initial, axis, down)  20.3 us
    ppermute x8, starting transfers between devices, padded_2(): before = lax.ppermute(last, axis, up)  17.5 us
    ppermute x8, starting transfers between devices, padded_2(): after = lax.ppermute(initial, axis, down)  10.5 us
    psum x2, blocking collectives, coarse_term(): projected = lax.psum(slab_proj, 'narrow')  10 us
    reshape x2, local copies, waits for them, and re-layouts, schwarz(): return nodal.reshape(8 * count_x, 8 * count_y, 8 * count_z)  7.94 us
  transfers between devices with their start and end apart: 19, of which 10 were waited for; matrix products, arithmetic and copies ran while one was open for 3% of the time, Pallas kernels for 0%

commit v1 on v0

v1 whole, which is shorter than its diff:
```python
import functools

import jax
import jax.numpy as jnp
import numpy as np
from jax import lax
from jax.experimental import pallas as pl
from jax.experimental.pallas import tpu as pltpu
from jax.sharding import PartitionSpec as P

F32 = jnp.float32
BF16 = jnp.bfloat16
BX, BY, BZ = 8, 16, 512
EY, EZ = 2, 64
ELEMS = EY * EZ
YR = 24
YW = YR * (BX + 2)
AB = 208
KCOL = 2048
WIDTH = KCOL + 128
AXES = ("wide", "narrow")


def split_const(values):
    high = values.astype(jnp.bfloat16)
    low = (values - high.astype(np.float64)).astype(jnp.bfloat16)
    return high, low


@functools.lru_cache(maxsize=None)
def tables():
    index = np.arange(10, dtype=np.float64)
    basis = np.sqrt(2.0 / 11.0) * np.sin(np.pi * (index[:, None] + 1.0) * (index[None, :] + 1.0) / 11.0)
    values = 2.0 - 2.0 * np.cos(np.pi * (index + 1.0) / 11.0)
    to_z = np.zeros((BZ, 10 * EZ))
    from_z = np.zeros((10 * EZ, BZ))
    for e in range(EZ):
        for k in range(10):
            z = 8 * e + k - 1
            if 0 <= z < BZ:
                to_z[z, e::EZ] = basis[k]
            if 1 <= k <= 8:
                from_z[e::EZ, z] = basis[k]
    to_xy = np.zeros((10, EY, 10, 10, YR))
    from_xy = np.zeros((BX, BY, 10, EY, 10))
    for e in range(EY):
        for j in range(10):
            y = 8 * e + j - 1
            to_xy[:, e, :, :, y % YR] += basis.T[:, None, :] * basis[j][None, :, None]
            if 1 <= j <= 8:
                from_xy[:, y, :, e, :] = basis[1:9, :, None] * basis[j][None, None, :]
    to_xy = np.pad(to_xy.reshape(200, YW), ((0, AB - 200), (0, 0)))
    from_xy = np.pad(from_xy.reshape(BX * BY, 200), ((0, 0), (0, AB - 200)))
    column = np.zeros((AB, 128), np.float32)
    grid = np.zeros((10, EY, 10, 2))
    grid[..., 0] = values[:, None, None] + values[None, None, :]
    grid[..., 1] = np.arange(EY)[None, :, None]
    column[:200, :2] = grid.reshape(200, 2)
    column[200:, 0] = 1.0
    line = np.repeat(values, EZ)[None, :].astype(np.float32)
    gather = np.zeros((BZ, EY * ELEMS), np.float32)
    spread = np.zeros((ELEMS, EY * BZ), np.float32)
    for e in range(EY):
        for z in range(BZ):
            gather[z, e * ELEMS + e * EZ + z // 8] = 1.0
            spread[e * EZ + z // 8, e * BZ + z] = 1.0
    fine = split_const(to_xy) + split_const(to_z) + split_const(from_xy) + split_const(from_z) + (column, line)
    return fine, gather.astype(jnp.bfloat16), spread.astype(jnp.bfloat16)


def dot(a, b):
    return jnp.dot(a, b, preferred_element_type=F32)


def split2(x):
    high = x.astype(BF16)
    return high, (x - high.astype(F32)).astype(BF16)


def split3(x):
    high = x.astype(BF16)
    rest = x - high.astype(F32)
    middle = rest.astype(BF16)
    return high, middle, (rest - middle.astype(F32)).astype(BF16)


def dot3(a, b):
    return dot(a[0], b[0]) + dot(a[0], b[1]) + dot(a[1], b[0])


def iota(shape, axis):
    return lax.broadcasted_iota(jnp.int32, shape, axis)


def total(x):
    while x.ndim > 2:
        x = jnp.sum(x, axis=0)
    return jnp.sum(jnp.sum(x, axis=0, keepdims=True), axis=1, keepdims=True)


def element_row(field, gather):
    parts = jnp.concatenate(split3(jnp.sum(field, axis=0)), axis=0)
    sums = dot(parts, gather)
    sums = sums[0:16] + sums[16:32] + sums[32:48]
    return jnp.sum(sums[0:8, 0:ELEMS], axis=0, keepdims=True) + jnp.sum(sums[8:16, ELEMS:], axis=0, keepdims=True)


def expand_rows(rows, spread):
    count = rows.shape[0]
    tall = jnp.broadcast_to(rows, (16, ELEMS)) if count == 1 else jnp.concatenate([rows, jnp.zeros((16 - count, ELEMS), F32)], axis=0)
    wide = dot(jnp.concatenate(split3(tall), axis=0), spread)
    return (wide[0:16] + wide[16:32] + wide[32:48])[0:count]


def expand_block(row, spread):
    wide = expand_rows(row, spread)
    low = jnp.broadcast_to(wide[:, 0:BZ], (8, BZ))
    high = jnp.broadcast_to(wide[:, BZ:], (8, BZ))
    return jnp.concatenate([low, high], axis=0)


def row_to_column(row):
    eye = iota((ELEMS, ELEMS), 0) == iota((ELEMS, ELEMS), 1)
    return jnp.sum(jnp.where(eye, row, 0.0), axis=1, keepdims=True)


def slot_mask(slots, offset):
    slot_of_row = lax.rem(iota((ELEMS, ELEMS), 0) + offset, ELEMS)
    return slot_of_row == slots


def to_rows(element_values, slots, offset):
    return jnp.sum(jnp.where(slot_mask(slots, offset), element_values, 0.0), axis=1, keepdims=True)


def to_elements(row_values, slots, offset):
    return jnp.sum(jnp.where(slot_mask(slots, offset), row_values, 0.0), axis=0, keepdims=True)


def project(column, parts):
    out = 0.0
    at = 0
    for part in parts:
        size = part.shape[0]
        out = out + jnp.sum(column[at : at + size] * part[...], axis=0, keepdims=True)
        at += size
    return out


def correct(row, parts):
    out = []
    for part in parts:
        products = part[...] * row
        folded = products[:, 0:128]
        for at in range(128, KCOL, 128):
            folded = folded + products[:, at : at + 128]
        out.append(jnp.sum(folded, axis=1, keepdims=True))
    return jnp.concatenate(out, axis=0)


def store_sum(out_ref, projection, extra):
    count = out_ref.shape[0]
    out_ref[:, 0:KCOL] = jnp.broadcast_to(projection, (count, KCOL))
    out_ref[:, KCOL:WIDTH] = jnp.broadcast_to(extra, (count, WIDTH - KCOL))


def lanes(values):
    at = iota((1, 128), 1)
    row = jnp.zeros((1, 128), F32)
    for i, value in enumerate(values):
        row = jnp.where(at == i, value, row)
    return row


def lane(row, i):
    return jnp.sum(jnp.where(iota(row.shape, 1) == i, row, 0.0), axis=1, keepdims=True)


def odd(index):
    return lax.rem(index, 2) == 1


def pair_out(index, low, high):
    return jnp.where(odd(index), low, high), jnp.where(odd(index), high, low)


def pair_in(index, first, second):
    return jnp.where(odd(index), first, second), jnp.where(odd(index), second, first)


def extend_y(block, low, high, depth):
    at = iota((8, BZ), 0)
    tails = []
    for x in range(block.shape[0]):
        tail = jnp.zeros((8, BZ), F32)
        for i in range(depth):
            tail = jnp.where(at == i, high[i][x : x + 1], tail)
            tail = jnp.where(at == 8 - depth + i, low[i][x : x + 1], tail)
        tails.append(tail)
    return jnp.concatenate([block, jnp.stack(tails)], axis=1)


def roll_sum(x):
    count, rows, _ = x.shape
    beside = pltpu.roll(x, 1, 1) + pltpu.roll(x, rows - 1, 1)
    flat = x.reshape(count * rows, BZ)
    at = iota(flat.shape, 1)
    beside_z = jnp.where(at == 0, 0.0, pltpu.roll(flat, 1, 1)) + jnp.where(at == BZ - 1, 0.0, pltpu.roll(flat, BZ - 1, 1))
    return beside + beside_z.reshape(x.shape)


def fine_solve(rows, sigma, consts):
    wh, wl, th, tl, vh, vl, uh, ul, column, line = [ref[...] for ref in consts]
    sig = jnp.where(column[:, 1:2] == 0.0, tile_lanes(sigma, 0), tile_lanes(sigma, 1))
    inverse = 1.0 / (column[:, 0:1] + line + sig)
    spectra = dot3((wh, wl), split2(rows))
    spectra = dot3(split2(spectra), (th, tl)) * inverse
    nodal = dot3((vh, vl), split2(spectra))
    return dot3(split2(nodal), (uh, ul)).reshape(BX, BY, BZ)


def tile_lanes(sigma, e):
    low = iota((1, ELEMS), 1) < EZ
    rolled = pltpu.roll(sigma, EZ, 1)
    both = jnp.where(low, sigma, rolled) if e == 0 else jnp.where(low, rolled, sigma)
    return jnp.concatenate([both] * 5, axis=1)


def start_kernel(right_ref, diag_ref, slot_ref, gather_ref, c_ref, sigma_ref, ya_ref, yb_ref):
    d = lax.axis_index("narrow")
    gather = gather_ref[...]
    totals = element_row(right_ref[...], gather) * (1.0 / 16.0)
    sigma_ref[...] = element_row(diag_ref[...], gather) * (1.0 / 512.0)
    column = to_rows(totals, slot_ref[...], 0)
    eye = iota((ELEMS, ELEMS), 0) == iota((ELEMS, ELEMS), 1)
    row = jnp.sum(jnp.where(eye, column, 0.0), axis=0, keepdims=True)
    c_ref[...] = row
    for i, ref in enumerate((right_ref, diag_ref)):
        first, second = pair_out(d, ref[:, 0, :], ref[:, BY - 1, :])
        ya_ref[i] = first
        yb_ref[i] = second
    ya_ref[2] = jnp.concatenate([jnp.broadcast_to(row, (8, ELEMS)), jnp.zeros((8, BZ - ELEMS), F32)], axis=1)
    yb_ref[2] = jnp.zeros((8, BZ), F32)


def project_kernel(c_ref, ra_ref, rb_ref, right_ref, diag_ref, xa_ref, xb_ref, swapped, sum_ref, re_ref, de_ref, oa_ref, ob_ref):
    w, d = lax.axis_index("wide"), lax.axis_index("narrow")
    row = c_ref[...]
    if swapped:
        half = ELEMS // 2
        other = pltpu.roll(ra_ref[2, 0:1, 0:ELEMS], half, 1)
        row = jnp.where(iota((1, ELEMS), 1) // half == d, row, other)
    store_sum(sum_ref, project(row_to_column(row), (xa_ref, xb_ref)), jnp.zeros((1, 128), F32))
    for i, (ref, out) in enumerate(((right_ref, re_ref), (diag_ref, de_ref))):
        low, high = pair_in(d, ra_ref[i], rb_ref[i])
        block = extend_y(ref[...], [low], [high], 1)
        out[...] = block
        oa_ref[i], ob_ref[i] = pair_out(w, block[0], block[BX - 1])


def first_fine_kernel(re_ref, ra_ref, rb_ref, sigma_ref, *rest):
    w = lax.axis_index("wide")
    low, high = pair_in(w, ra_ref[0], rb_ref[0])
    rows = jnp.concatenate([low[None], re_ref[...], high[None]], axis=0).reshape(YW, BZ)
    rest[-1][...] = fine_solve(rows, sigma_ref[...], rest[:-1])


def first_coarse_kernel(sum_ref, fine_ref, slot_ref, offset_ref, spread_ref, xa_ref, xb_ref, out_ref, ya_ref, yb_ref):
    d = lax.axis_index("narrow")
    row = jnp.sum(sum_ref[...], axis=0, keepdims=True)
    values = to_elements(correct(row[:, 0:KCOL], (xa_ref, xb_ref)), slot_ref[...], offset_ref[0])
    out_ref[...] = fine_ref[...] + expand_block(values * (1.0 / 16.0), spread_ref[...])[None]
    for i in range(2):
        ya_ref[i], yb_ref[i] = pair_out(d, out_ref[:, i, :], out_ref[:, BY - 2 + i, :])


def extend_kernel(s_ref, ra_ref, rb_ref, se_ref, xa_ref, xb_ref):
    w, d = lax.axis_index("wide"), lax.axis_index("narrow")
    pairs = [pair_in(d, ra_ref[i], rb_ref[i]) for i in range(2)]
    block = extend_y(s_ref[...], [p[0] for p in pairs], [p[1] for p in pairs], 2)
    se_ref[...] = block
    xa_ref[...], xb_ref[...] = pair_out(w, block[0:2], block[BX - 2 : BX])


def operator_kernel(
    sizes, se_ref, sa_ref, sb_ref, right_ref, de_ref, da_ref, db_ref, slot_ref, offset_ref, gather_ref, xa_ref, xb_ref, sum_ref, we_ref
):
    w, d = lax.axis_index("wide"), lax.axis_index("narrow")
    s_low, s_high = pair_in(w, sa_ref[...], sb_ref[...])
    d_low, d_high = pair_in(w, da_ref[1], db_ref[1])
    search = jnp.concatenate([s_low, se_ref[...], s_high], axis=0)
    diagonal = jnp.concatenate([d_low[None], de_ref[...], d_high[None]], axis=0)
    centre = search[1 : BX + 3]
    image = (6.0 + diagonal) * centre - (search[0 : BX + 2] + search[2 : BX + 4] + roll_sum(centre))
    x = iota(image.shape, 0)
    y = iota(image.shape, 1)
    inside = (y < BY) | ((y == BY) & (d < sizes[1] - 1)) | ((y == YR - 1) & (d > 0))
    inside &= ((x > 0) | (w > 0)) & ((x < BX + 1) | (w < sizes[0] - 1))
    image = jnp.where(inside, image, 0.0)
    we_ref[...] = image
    own = image[1 : BX + 1, 0:BY]
    own_search = se_ref[:, 0:BY, :]
    totals = element_row(own, gather_ref[...]) * (1.0 / 16.0)
    column = to_rows(totals, slot_ref[...], offset_ref[0])
    extra = lanes([total(right_ref[...] * own_search), total(own_search * own)])
    store_sum(sum_ref, project(column, (xa_ref, xb_ref)), extra)


def second_fine_kernel(we_ref, sigma_ref, *rest):
    w, d = lax.axis_index("wide"), lax.axis_index("narrow")
    out_ref, ya_ref, yb_ref, xa_ref, xb_ref = rest[-5:]
    out = fine_solve(we_ref[...].reshape(YW, BZ), sigma_ref[...], rest[:-5])
    out_ref[...] = out
    ya_ref[...], yb_ref[...] = pair_out(d, out_ref[:, 0, :], out_ref[:, BY - 1, :])
    xa_ref[...], xb_ref[...] = pair_out(w, out[0], out[BX - 1])


def second_coarse_kernel(
    sum_ref, fine_ref, fya_ref, fyb_ref, fxa_ref, fxb_ref, right_ref, se_ref, sa_ref, sb_ref, we_ref, de_ref,
    slot_ref, offset_ref, spread_ref, xa_ref, xb_ref, s1_ref, t1_ref, last_ref,
):
    w, d = lax.axis_index("wide"), lax.axis_index("narrow")
    row = jnp.sum(sum_ref[...], axis=0, keepdims=True)
    step = lane(row[:, KCOL:WIDTH], 0) / lane(row[:, KCOL:WIDTH], 1)
    values = to_elements(correct(row[:, 0:KCOL], (xa_ref, xb_ref)), slot_ref[...], offset_ref[0])
    coarse = expand_block(values * (1.0 / 16.0), spread_ref[...])[None]
    own_search = se_ref[:, 0:BY, :]
    own_image = we_ref[1 : BX + 1, 0:BY, :]
    search = own_search - step * (fine_ref[...] + coarse)
    s_low, s_high = pair_in(w, sa_ref[...], sb_ref[...])
    f_low, f_high = pair_in(w, fxa_ref[...], fxb_ref[...])
    x_low = s_low[1, 0:BY] - step * f_low
    x_high = s_high[0, 0:BY] - step * f_high
    g_low, g_high = pair_in(d, fya_ref[...], fyb_ref[...])
    y_low = se_ref[:, YR - 1, :] - step * g_low
    y_high = se_ref[:, BY, :] - step * g_high
    block = extend_y(search, [y_low], [y_high], 1)
    beside = roll_sum(block)[:, 0:BY]
    beside = beside + jnp.concatenate([x_low[None], search[0 : BX - 1]], axis=0)
    beside = beside + jnp.concatenate([search[1:BX], x_high[None]], axis=0)
    image = (6.0 + de_ref[:, 0:BY, :]) * search - beside
    s1_ref[...] = search
    t1_ref[...] = image
    residual = right_ref[...] - step * own_image
    edges = total(coarse[0] * (x_low + x_high))
    edges = edges + total(y_low * coarse[0, 0:1]) + total(y_high * coarse[0, BY - 1 : BY])
    extra = lanes([total(residual * search), total(search * image) + step * edges, total(search * own_image)])
    count = last_ref.shape[0]
    last_ref[:, 0:ELEMS] = jnp.broadcast_to(values, (count, ELEMS))
    last_ref[:, ELEMS:] = jnp.broadcast_to(extra, (count, 128))


def last_kernel(sizes, sum_ref, last_ref, right_ref, se_ref, we_ref, s1_ref, t1_ref, spread_ref, x_ref, r_ref):
    w, d = lax.axis_index("wide"), lax.axis_index("narrow")
    groups = sizes[1]
    count = sizes[0] * groups
    product = jnp.sum(sum_ref[:, KCOL:WIDTH], axis=0, keepdims=True)
    product, bottom = lane(product, 0), lane(product, 1)
    step = product / bottom
    z = last_ref[:, 0:ELEMS]
    rows = iota((count, ELEMS), 0)
    at = iota((count, ELEMS), 1)
    faces = jnp.where(rows < count - groups, z * pltpu.roll(z, count - groups, 0), 0.0)
    across = pltpu.roll(pltpu.roll(z, count - 1, 0), EZ, 1)
    faces = faces + jnp.where((lax.rem(rows, groups) < groups - 1) & (at >= EZ), z * across, 0.0)
    sums = jnp.sum(last_ref[:, ELEMS:], axis=0, keepdims=True)
    next_product = lane(sums, 0)
    quadratic = lane(sums, 1) - step * step * 0.5 * total(faces)
    cross = lane(sums, 2)
    me = w * groups + d
    picked = []
    for index, there in ((me - groups, w > 0), (me + groups, w < sizes[0] - 1), (me - 1, d > 0), (me + 1, d < groups - 1)):
        picked.append(jnp.sum(jnp.where((rows == index) & there, z, 0.0), axis=0, keepdims=True))
    wide = expand_rows(jnp.concatenate(picked, axis=0), spread_ref[...]) * (1.0 / 16.0)
    layers = []
    for i in range(2):
        layers.append(
            jnp.concatenate(
                [jnp.broadcast_to(wide[i : i + 1, 0:BZ], (8, BZ)), jnp.broadcast_to(wide[i : i + 1, BZ:], (8, BZ))], axis=0
            )
        )
    shape = (BX, BY, BZ)
    x, y = iota(shape, 0), iota(shape, 1)
    missing = jnp.where(x == 0, layers[0][None], 0.0) + jnp.where(x == BX - 1, layers[1][None], 0.0)
    missing = missing + jnp.where(y == 0, wide[2:3, BZ:][None], 0.0) + jnp.where(y == BY - 1, wide[3:4, 0:BZ][None], 0.0)
    ratio = next_product / product
    curvature = quadratic + 2.0 * ratio * cross + ratio * ratio * bottom
    step_next = next_product / curvature
    own_search = se_ref[:, 0:BY, :]
    own_image = we_ref[1 : BX + 1, 0:BY, :]
    direction = s1_ref[...] + ratio * own_search
    image = t1_ref[...] + step * missing + ratio * own_image
    x_ref[...] = step * own_search + step_next * direction
    r_ref[...] = (right_ref[...] - step * own_image) - step_next * image


def call(kernel, shapes, args, smem=()):
    specs = [pl.BlockSpec(memory_space=pltpu.SMEM if i in smem else pltpu.VMEM) for i in range(len(args))]
    return pl.pallas_call(
        kernel,
        out_shape=[jax.ShapeDtypeStruct(shape, F32) for shape in shapes],
        in_specs=specs,
        out_specs=[pl.BlockSpec(memory_space=pltpu.VMEM)] * len(shapes),
        compiler_params=pltpu.CompilerParams(vmem_limit_bytes=48 * 1024 * 1024),
    )(*args)


def pair_swap(first, second, axis):
    size = lax.axis_size(axis)
    received = []
    for value, begin in ((first, 0), (second, 1)):
        perm = []
        for i in range(begin, size - 1, 2):
            perm += [(i, i + 1), (i + 1, i)]
        received.append(lax.ppermute(value, axis, perm) if perm else jnp.zeros_like(value))
    return received


def everywhere(rows):
    return lax.all_to_all(rows, AXES, split_axis=0, concat_axis=0, tiled=True)


def body(right, diagonal, coarse_slot, factor):
    sizes = (lax.axis_size("wide"), lax.axis_size("narrow"))
    groups = sizes[1]
    count = sizes[0] * groups
    d = lax.axis_index("narrow")
    fine, gather, spread = tables()
    fine = [jnp.asarray(c) for c in fine]
    gather, spread = jnp.asarray(gather), jnp.asarray(spread)
    slots = coarse_slot.reshape(1, ELEMS)
    share = ELEMS // groups
    swapped = groups == 2
    if swapped:
        kept = lax.dynamic_slice_in_dim(factor, d * share, share, 0)
        sent = lax.dynamic_slice_in_dim(factor, (1 - d) * share, share, 0)
        owned = (kept, lax.ppermute(sent, "narrow", [(0, 1), (1, 0)]))
        offset = (d * share).reshape(1).astype(jnp.int32)
        first = (factor,)
    else:
        ours = lax.all_to_all(factor.reshape(groups, share, KCOL), "narrow", split_axis=0, concat_axis=0, tiled=True)
        ours = ours.reshape(ELEMS, KCOL)
        owned = (ours[: ELEMS // 2], ours[ELEMS // 2 :])
        offset = jnp.zeros((1,), jnp.int32)
        first = (ours,)

    block, layer, extended = (BX, BY, BZ), (YR, BZ), (BX, YR, BZ)
    y_shape, x_shape = (3, BX, BZ), (2, YR, BZ)
    c_row, sigma, ya, yb = call(start_kernel, [(1, ELEMS), (1, ELEMS), y_shape, y_shape], [right, diagonal, slots, gather])
    ya, yb = pair_swap(ya, yb, "narrow")

    def project_first(c_ref, ra_ref, rb_ref, right_ref, diag_ref, x_ref, *outs):
        half = ELEMS // 2
        project_kernel(
            c_ref, ra_ref, rb_ref, right_ref, diag_ref, x_ref.at[0:half], x_ref.at[half:ELEMS], swapped, *outs
        )

    sums, right_e, diag_e, xa, xb = call(
        project_first, [(count, WIDTH), extended, extended, x_shape, x_shape], [c_row, ya, yb, right, diagonal, *first]
    )
    sums = everywhere(sums)
    xa, xb = pair_swap(xa, xb, "wide")
    (solved,) = call(first_fine_kernel, [block], [right_e, xa, xb, sigma, *fine])
    search, ya, yb = call(
        first_coarse_kernel, [block, (2, BX, BZ), (2, BX, BZ)], [sums, solved, slots, offset, spread, *owned], (3,)
    )
    ya, yb = pair_swap(ya, yb, "narrow")
    search_e, sa, sb = call(extend_kernel, [extended, (2,) + layer, (2,) + layer], [search, ya, yb])
    sa, sb = pair_swap(sa, sb, "wide")
    sums, image_e = call(
        functools.partial(operator_kernel, sizes),
        [(count, WIDTH), (BX + 2, YR, BZ)],
        [search_e, sa, sb, right, diag_e, xa, xb, slots, offset, gather, *owned],
        (8,),
    )
    sums = everywhere(sums)
    solved, ya, yb, fa, fb = call(
        second_fine_kernel, [block, (BX, BZ), (BX, BZ), (BY, BZ), (BY, BZ)], [image_e, sigma, *fine]
    )
    ya, yb = pair_swap(ya, yb, "narrow")
    fa, fb = pair_swap(fa, fb, "wide")
    search_next, image_next, last = call(
        second_coarse_kernel,
        [block, block, (count, 256)],
        [sums, solved, ya, yb, fa, fb, right, search_e, sa, sb, image_e, diag_e, slots, offset, spread, *owned],
        (13,),
    )
    last = everywhere(last)
    return tuple(
        call(
            functools.partial(last_kernel, sizes),
            [block, block],
            [sums, last, right, search_e, image_e, search_next, image_next, spread],
        )
    )


def solution(mesh):
    in_specs = (
        P("wide", "narrow", None),
        P("wide", "narrow", None),
        P("wide", "narrow", None),
        P(("wide", "narrow"), None),
    )
    out_specs = (P("wide", "narrow", None), P("wide", "narrow", None))
    return jax.shard_map(body, mesh=mesh, in_specs=in_specs, out_specs=out_specs, check_vma=False)
```

time: 364 us -> 90.6 us (0.25)
  blocking collectives: 202 us -> 14.6 us
  local copies, waits for them, and re-layouts: 62.4 us -> 25.6 us
  matrix products: 14.8 us -> 0 us
  other arithmetic: 13.7 us -> 0 us
  waiting for transfers between devices: 25.4 us -> 13 us
  starting transfers between devices: 38.9 us -> 26.6 us
  Pallas kernels: 0 us -> 8.72 us
  between operations: 5.35 us -> 1 us
    psum x7 -> x0, blocking collectives: 195 us -> none  [the longest x3 118 us: global_sum(): return lax.psum(local_value, ('wide', 'narrow'))]
    reshape x23 -> x1, local copies, waits for them, and re-layouts: 38.3 us -> 0.76 us  [body(): slots = coarse_slot.reshape(1, ELEMS)]
    unnamed x7 -> x91, local copies, waits for them, and re-layouts: 0.03 us -> 21.9 us
    ppermute x16 -> x10, starting transfers between devices: 28 us -> 9.77 us  [the longest x9 8.06 us: pair_swap(): lax.ppermute(value, axis, perm)]
    slice x15 -> x0, local copies, waits for them, and re-layouts: 15 us -> none  [the longest x4 6.69 us: front_windows(): after = values_in[9:length + 2:8][:, None]]
    dot_general x16 -> x0, matrix products: 14.8 us -> none  [the longest x2 3.1 us: schwarz(): spectra = jnp.einsum('ia,ijke->ajke', sine_basis, blocks, precision=precise)]
    pallas_call x0 -> x9, Pallas kernels: none -> 8.72 us  [call(): pl.pallas_call(kernel, out_shape=[jax.ShapeDtypeStruct(shape, F32) for sh...]
    all_to_all x1, blocking collectives: 6.82 us -> 14.6 us  [everywhere(): return lax.all_to_all(rows, AXES, split_axis=0, concat_axis=0, tiled=True)]
  transfers between devices with their start and end apart: 19 -> 12, of which waited for: 10 -> 6; matrix products, arithmetic and copies ran while one was open for 3% -> 3% of each run, Pallas kernels for 0% -> 4%
where the time goes in v1:
time: 90.6 us; the launch traced here: 89.5 us
  starting transfers between devices  26.6 us (29%)
  local copies, waits for them, and re-layouts  25.6 us (28%)
  blocking collectives  14.6 us (16%)
  waiting for transfers between devices  13 us (14%)
  Pallas kernels  8.72 us (10%)
  between operations  1 us (1%)
    unnamed x91, local copies, waits for them, and re-layouts  21.9 us
    all_to_all x2, starting transfers between devices, everywhere(): return lax.all_to_all(rows, AXES, split_axis=0, concat_axis=0, tiled=True)  16.9 us
    all_to_all x1, blocking collectives, everywhere(): return lax.all_to_all(rows, AXES, split_axis=0, concat_axis=0, tiled=True)  14.6 us
    pallas_call x9, Pallas kernels, call(): pl.pallas_call(kernel, out_shape=[jax.ShapeDtypeStruct(shape, F32) for sh...  8.72 us
    ppermute x9, starting transfers between devices, pair_swap(): lax.ppermute(value, axis, perm)  8.06 us
    ppermute x9, waiting for transfers between devices, pair_swap(): lax.ppermute(value, axis, perm)  7.59 us
    ppermute x1, waiting for transfers between devices, body(): owned = (kept, lax.ppermute(sent, 'narrow', [(0, 1), (1, 0)]))  5.35 us
    all_to_all x3, local copies, waits for them, and re-layouts, everywhere(): return lax.all_to_all(rows, AXES, split_axis=0, concat_axis=0, tiled=True)  2.04 us
  transfers between devices with their start and end apart: 12, of which 6 were waited for; matrix products, arithmetic and copies ran while one was open for 3% of the time, Pallas kernels for 4%

profile of v1, /device:TPU:0, one launch (start us, length us, event | category | flops | bytes accessed | tf_op | source)
XLA Modules:
  0.0 89.5 jit_solution(13493744577930741285)
XLA Ops:
  0.6 0.8 reshape.16.slot_ref
  1.4 0.9 %copy-done = f32[8,16,512]{2,1,0:T(8,128)S(1)} copy-done((f32[8,16,512]{2,1,0:T(8,128)S(1)}, f32[8,16,512]{2,1,0:T(8,128)}, u32[]{:S(2)}) %copy-start) | copy-done | bytes 262168
  2.3 0.9 %copy-done.15 = bf16[512,256]{1,0:T(8,128)(2,1)S(1)} copy-done((bf16[512,256]{1,0:T(8,128)(2,1)S(1)}, bf16[512,256]{1,0:T(8,128)(2,1)}, u32[]{:S(2)}) %copy-start.15) | copy-done | bytes 262168
  3.3 0.9 %copy-done.17 = f32[8,16,512]{2,1,0:T(8,128)S(1)} copy-done((f32[8,16,512]{2,1,0:T(8,128)S(1)}, f32[8,16,512]{2,1,0:T(8,128)}, u32[]{:S(2)}) %copy-start.17) | copy-done | bytes 262168
  4.2 0.9 shard_map.167
  5.1 2.9 %collective-permute-start = (f32[3,8,512]{2,1,0:T(8,128)S(1)}, f32[3,8,512]{2,1,0:T(8,128)S(1)}, u32[]{:S(2)}, u32[]{:S(2)}) collective-permute-start(f32[3,8,512]{2,1,0:T(8,128)S(1)} %get-tuple-element.25), channel_id=1, source_target_pairs={{0,1},{1,0},{2,3},{3,2},{4,5},{5,4},{6,7},{7,6},{8,9},{9,8},{10,11... | collective-permute-start | bytes 147464 | tf_op jit(solution)/shard_map/ppermute | solution.py:415
  8.1 2.1 %collective-permute-done.ra_ref = f32[3,8,512]{2,1,0:T(8,128)S(1)} collective-permute-done((f32[3,8,512]{2,1,0:T(8,128)S(1)}, f32[3,8,512]{2,1,0:T(8,128)S(1)}, u32[]{:S(2)}, u32[]{:S(2)}) %collective-permute-start) | collective-permute-done | bytes 49184 | tf_op jit(solution)/shard_map/ppermute | solution.py:415
  10.1 0.0 copy-start.2
  10.1 1.2 %copy-done.2 = f32[128,2048]{1,0:T(8,128)S(1)} copy-done((f32[128,2048]{1,0:T(8,128)S(1)}, f32[128,2048]{1,0:T(8,128)}, u32[]{:S(2)}) %copy-start.2) | copy-done | bytes 1048600
  11.4 0.3 shard_map.168
  11.7 0.7 copy-done.12
  12.4 0.8 copy-done.33
  13.2 1.0 %copy.18 = f32[32,1,2176]{2,1,0:T(1,128)} copy(f32[32,1,2176]{2,0,1:T(8,128)S(1)} %bitcast.16) | data formatting | bytes 557056 | tf_op jit(solution)/shard_map/all_to_all | solution.py:420
  14.2 6.5 %all-to-all-start = ((f32[32,1,2176]{2,1,0:T(1,128)}), f32[32,1,2176]{2,1,0:T(1,128)}, u32[]{:S(2)}, u32[]{:S(2)}) async-start(f32[32,1,2176]{2,1,0:T(1,128)} %copy.18), calls=%async_computation | async-start | bytes 557056 | tf_op jit(solution)/shard_map/all_to_all | solution.py:420
  20.7 0.0 copy-start.4
  20.7 0.0 copy-start.5
  20.7 0.0 copy-start.6
  20.8 0.0 copy-start.19
  20.8 0.9 %constant_dynamic-slice_fusion = (f32[64,2048]{1,0:T(8,128)}, f32[64,2048]{1,0:T(8,128)S(1)}) fusion(f32[128,2048]{1,0:T(8,128)S(1)} %copy-done.3, s32[]{:T(128)S(6)} %select_n.7, s32[]{:T(128)S(6)} %select_n.6), kind=kLoop, calls=%fused_computation.3 | loop fusion | bytes 2097160 | tf_op jit(solution)/shard_map/dynamic_slice | solution.py:436
  21.7 1.7 %collective-permute-start.3 = (f32[64,2048]{1,0:T(8,128)}, f32[64,2048]{1,0:T(8,128)S(1)}, u32[]{:S(2)}, u32[]{:S(2)}) collective-permute-start(f32[64,2048]{1,0:T(8,128)} %get-tuple-element.46), channel_id=1, source_target_pairs={{0,1},{1,0},{2,3},{3,2},{4,5},{5,4},{6,7},{7,6},{8,9},{9,8},{10,11... | collective-permute-start | bytes 1572872 | tf_op jit(solution)/shard_map/ppermute | solution.py:437
  23.4 0.8 collective-permute-start.2
  24.2 0.7 collective-permute-done.1.ra_ref.da_ref
  24.9 0.0 copy-start.8
  25.0 1.1 %copy-done.8 = bf16[512,640]{1,0:T(8,128)(2,1)S(1)} copy-done((bf16[512,640]{1,0:T(8,128)(2,1)S(1)}, bf16[512,640]{1,0:T(8,128)(2,1)}, u32[]{:S(2)}) %copy-start.8) | copy-done | bytes 655384
  26.0 1.0 %copy-done.34 = f32[8,24,512]{2,1,0:T(8,128)S(1)} copy-done((f32[8,24,512]{2,1,0:T(8,128)S(1)}, f32[8,24,512]{2,1,0:T(8,128)}, u32[]{:S(2)}) %copy-start.34) | copy-done | bytes 393240
  27.0 0.8 copy-done.35
  27.9 0.8 copy-done.37
  28.7 1.6 %shard_map.169.fine_ref = f32[8,16,512]{2,1,0:T(8,128)S(1)} custom-call(f32[8,24,512]{2,1,0:T(8,128)S(1)} %copy-done.34, f32[2,24,512]{2,1,0:T(8,128)S(1)} %collective-permute-done.1.ra_ref.da_ref, f32[2,24,512]{2,1,0:T(8,128)S(1)} %collective-permute-done.2.rb_ref.db_ref, f32[1,128]{1,0:T(1,128)S(1)} %get-tuple-element.30.sigma_ref, ...), custom_call_target="tpu_custom_call" | custom-call | tf_op jit(solution)/shard_map/pallas_call | solution.py:399
  30.4 0.6 copy-done.29
  31.0 0.6 copy-done.31
  31.6 0.0 all-to-all-done
  31.7 1.0 %copy.28 = f32[32,1,2176]{2,0,1:T(8,128)S(1)} copy(f32[32,1,2176]{2,1,0:T(1,128)} %all-to-all-done) | data formatting | bytes 557056
  32.7 5.3 %collective-permute-done.3.xb_ref = f32[64,2048]{1,0:T(8,128)S(1)} collective-permute-done((f32[64,2048]{1,0:T(8,128)}, f32[64,2048]{1,0:T(8,128)S(1)}, u32[]{:S(2)}, u32[]{:S(2)}) %collective-permute-start.3) | collective-permute-done | bytes 524320 | tf_op jit(solution)/shard_map/ppermute | solution.py:437
  38.0 1.1 %shard_map.170 = (f32[8,16,512]{2,1,0:T(8,128)S(1)}, f32[2,8,512]{2,1,0:T(8,128)S(1)}, f32[2,8,512]{2,1,0:T(8,128)}) custom-call(f32[32,2176]{1,0:T(8,128)S(1)} %bitcast.15, f32[8,16,512]{2,1,0:T(8,128)S(1)} %shard_map.169.fine_ref, s32[1,128]{1,0:T(1,128)S(1)} %reshape.16.slot_ref, s32[1]{0:T(128)} %bitcast.1.offset_ref, bf16[128,1024]{1,0:T(8,128)(2,1)S(1)} %copy-done.10, ...), custom_call_target="tpu_custom_call" | custom-call | tf_op jit(solution)/shard_map/pallas_call | solution.py:399
  39.1 1.0 %collective-permute-start.4 = (f32[2,8,512]{2,1,0:T(8,128)S(1)}, f32[2,8,512]{2,1,0:T(8,128)S(1)}, u32[]{:S(2)}, u32[]{:S(2)}) collective-permute-start(f32[2,8,512]{2,1,0:T(8,128)S(1)} %get-tuple-element.32), channel_id=1, source_target_pairs={{0,1},{1,0},{2,3},{3,2},{4,5},{5,4},{6,7},{7,6},{8,9},{9,8},{10,11... | collective-permute-start | bytes 98312 | tf_op jit(solution)/shard_map/ppermute | solution.py:415
  40.1 2.9 %collective-permute-done.4.ra_ref = f32[2,8,512]{2,1,0:T(8,128)S(1)} collective-permute-done((f32[2,8,512]{2,1,0:T(8,128)S(1)}, f32[2,8,512]{2,1,0:T(8,128)S(1)}, u32[]{:S(2)}, u32[]{:S(2)}) %collective-permute-start.4) | collective-permute-done | bytes 32800 | tf_op jit(solution)/shard_map/ppermute | solution.py:415
  43.0 0.1 shard_map.171
  43.1 0.1 collective-permute-start.5
  43.2 0.7 collective-permute-start.6
  43.8 0.6 collective-permute-done.5.sa_ref
  44.5 0.7 shard_map.172
  45.2 1.0 %copy.19 = f32[32,1,2176]{2,1,0:T(1,128)} copy(f32[32,1,2176]{2,0,1:T(8,128)S(1)} %bitcast.17) | data formatting | bytes 557056 | tf_op jit(solution)/shard_map/all_to_all | solution.py:420
  46.2 10.4 %all-to-all-start.1 = ((f32[32,1,2176]{2,1,0:T(1,128)}), f32[32,1,2176]{2,1,0:T(1,128)}, u32[]{:S(2)}, u32[]{:S(2)}) async-start(f32[32,1,2176]{2,1,0:T(1,128)} %copy.19), calls=%async_computation.1 | async-start | bytes 557056 | tf_op jit(solution)/shard_map/all_to_all | solution.py:420
  56.6 0.0 copy-start.7
  56.6 1.1 %copy-done.7 = bf16[512,640]{1,0:T(8,128)(2,1)S(1)} copy-done((bf16[512,640]{1,0:T(8,128)(2,1)S(1)}, bf16[512,640]{1,0:T(8,128)(2,1)}, u32[]{:S(2)}) %copy-start.7) | copy-done | bytes 655384
  57.7 1.1 %copy-done.9 = bf16[512,640]{1,0:T(8,128)(2,1)S(1)} copy-done((bf16[512,640]{1,0:T(8,128)(2,1)S(1)}, bf16[512,640]{1,0:T(8,128)(2,1)}, u32[]{:S(2)}) %copy-start.9) | copy-done | bytes 655384
  58.8 0.9 copy-done.20
  59.7 0.9 copy-done.22
  60.6 0.9 copy-done.24
  61.5 0.8 copy-done.36
  62.3 0.8 copy-done.38
  63.1 2.3 %shard_map.173 = (f32[8,16,512]{2,1,0:T(8,128)S(1)}, f32[8,512]{1,0:T(8,128)}, f32[8,512]{1,0:T(8,128)}, f32[16,512]{1,0:T(8,128)}, f32[16,512]{1,0:T(8,128)S(1)}) custom-call(f32[10,24,512]{2,1,0:T(8,128)S(1)} %get-tuple-element.38.we_ref, f32[1,128]{1,0:T(1,128)S(1)} %get-tuple-element.30.sigma_ref, bf16[208,240]{1,0:T(8,128)(2,1)S(1)} %copy-done.24, ...), custom_call_target="tpu_custom_call" | custom-call | tf_op jit(solution)/shard_map/pallas_call | solution.py:399
  65.4 0.7 copy-done.39
  66.1 0.2 collective-permute-start.8
  66.3 0.7 collective-permute-start.9
  66.9 0.0 copy-start.11
  67.0 1.7 %collective-permute-start.7 = (f32[8,512]{1,0:T(8,128)}, f32[8,512]{1,0:T(8,128)S(1)}, u32[]{:S(2)}, u32[]{:S(2)}) collective-permute-start(f32[8,512]{1,0:T(8,128)} %get-tuple-element.40), channel_id=1, source_target_pairs={{0,1},{1,0},{2,3},{3,2},{4,5},{5,4},{6,7},{7,6},{8,9},{9,8},{10,11... | collective-permute-start | bytes 49160 | tf_op jit(solution)/shard_map/ppermute | solution.py:415
  68.7 1.0 %copy.27 = f32[32,1,2176]{2,0,1:T(8,128)S(1)} copy(f32[32,1,2176]{2,1,0:T(1,128)} %all-to-all-done.1) | data formatting | bytes 557056
  69.7 1.3 %collective-permute-done.7.fya_ref = f32[8,512]{1,0:T(8,128)S(1)} collective-permute-done((f32[8,512]{1,0:T(8,128)}, f32[8,512]{1,0:T(8,128)S(1)}, u32[]{:S(2)}, u32[]{:S(2)}) %collective-permute-start.7) | collective-permute-done | bytes 16416 | tf_op jit(solution)/shard_map/ppermute | solution.py:415
  71.0 1.0 %copy-done.14 = f32[8,24,512]{2,1,0:T(8,128)S(1)} copy-done((f32[8,24,512]{2,1,0:T(8,128)S(1)}, f32[8,24,512]{2,1,0:T(8,128)}, u32[]{:S(2)}) %copy-start.14) | copy-done | bytes 393240
  72.0 0.9 %copy-done.40 = f32[8,16,512]{2,1,0:T(8,128)S(1)} copy-done((f32[8,16,512]{2,1,0:T(8,128)S(1)}, f32[8,16,512]{2,1,0:T(8,128)}, u32[]{:S(2)}) %copy-start.40) | copy-done | bytes 262168
  73.0 0.8 shard_map.174
  73.8 14.6 %all_to_all.33 = f32[32,1,256]{2,1,0:T(1,128)S(1)} all-to-all(f32[32,1,256]{2,1,0:T(1,128)S(1)} %copy.20), channel_id=1, replica_groups=mesh['wide'=16,'narrow'=2] {'wide','narrow'}, dimensions={0} | all-to-all | bytes 65536 | tf_op jit(solution)/shard_map/all_to_all | solution.py:420
  88.5 1.1 %shard_map.175 = (f32[8,16,512]{2,1,0:T(8,128)}, f32[8,16,512]{2,1,0:T(8,128)}) custom-call(f32[32,2176]{1,0:T(8,128)S(1)} %bitcast.14, f32[32,256]{1,0:T(8,128)S(1)} %bitcast.18, f32[8,16,512]{2,1,0:T(8,128)S(1)} %copy-done.1, f32[8,24,512]{2,1,0:T(8,128)S(1)} %get-tuple-element.33.se_ref, f32[10,24,512]{2,1,0:T(8,128)S(1)} %get-tuple-element.38.we_ref, ...), custom_call_target="tpu_custom_call" | custom-call | tf_op jit(solution)/shard_map/pallas_call | solution.py:399
  (69 shorter events, 0.2 us)
Async XLA Ops:
  1.4 0.9 %copy-start = (f32[8,16,512]{2,1,0:T(8,128)S(1)}, f32[8,16,512]{2,1,0:T(8,128)}, u32[]{:S(2)}) copy-start(f32[8,16,512]{2,1,0:T(8,128)} %right_ref.9) | copy-start | bytes 786436
  2.3 0.9 %copy-start.15 = (bf16[512,256]{1,0:T(8,128)(2,1)S(1)}, bf16[512,256]{1,0:T(8,128)(2,1)}, u32[]{:S(2)}) copy-start(bf16[512,256]{1,0:T(8,128)(2,1)} %constant.50.clone.gather_ref) | copy-start | bytes 786436
  3.3 0.9 %copy-start.17 = (f32[8,16,512]{2,1,0:T(8,128)S(1)}, f32[8,16,512]{2,1,0:T(8,128)}, u32[]{:S(2)}) copy-start(f32[8,16,512]{2,1,0:T(8,128)} %diag_ref.3) | copy-start | bytes 786436
  4.2 5.9 %copy-start.1 = (f32[8,16,512]{2,1,0:T(8,128)S(1)}, f32[8,16,512]{2,1,0:T(8,128)}, u32[]{:S(2)}) copy-start(f32[8,16,512]{2,1,0:T(8,128)} %right_ref.9) | copy-start | bytes 786436
  4.2 5.9 %copy-start.18 = (f32[8,16,512]{2,1,0:T(8,128)S(1)}, f32[8,16,512]{2,1,0:T(8,128)}, u32[]{:S(2)}) copy-start(f32[8,16,512]{2,1,0:T(8,128)} %diag_ref.3) | copy-start | bytes 786436
  5.1 5.0 %collective-permute-start = (f32[3,8,512]{2,1,0:T(8,128)S(1)}, f32[3,8,512]{2,1,0:T(8,128)S(1)}, u32[]{:S(2)}, u32[]{:S(2)}) collective-permute-start(f32[3,8,512]{2,1,0:T(8,128)S(1)} %get-tuple-element.25), channel_id=1, source_target_pairs={{0,1},{1,0},{2,3},{3,2},{4,5},{5,4},{6,7},{7,6},{8,9},{9,8},{10,11... | collective-permute-start | bytes 147464 | tf_op jit(solution)/shard_map/ppermute | solution.py:415
  10.1 1.2 %copy-start.2 = (f32[128,2048]{1,0:T(8,128)S(1)}, f32[128,2048]{1,0:T(8,128)}, u32[]{:S(2)}) copy-start(f32[128,2048]{1,0:T(8,128)} %x_ref.1) | copy-start | bytes 3145732
  11.4 9.3 %copy-start.3 = (f32[128,2048]{1,0:T(8,128)S(1)}, f32[128,2048]{1,0:T(8,128)}, u32[]{:S(2)}) copy-start(f32[128,2048]{1,0:T(8,128)} %x_ref.1) | copy-start | bytes 3145732
  11.7 0.7 copy-start.12
  12.4 0.8 copy-start.33
  13.2 1.0 %copy-start.42 = (f32[2,24,512]{2,1,0:T(8,128)}, f32[2,24,512]{2,1,0:T(8,128)S(1)}, u32[]{:S(2)}) copy-start(f32[2,24,512]{2,1,0:T(8,128)S(1)} %get-tuple-element.29) | copy-start | bytes 294916
  13.2 1.0 %copy-start.43 = (f32[2,24,512]{2,1,0:T(8,128)}, f32[2,24,512]{2,1,0:T(8,128)S(1)}, u32[]{:S(2)}) copy-start(f32[2,24,512]{2,1,0:T(8,128)S(1)} %get-tuple-element.28) | copy-start | bytes 294916
  14.2 10.7 %copy-start.21 = (bf16[208,240]{1,0:T(8,128)(2,1)S(1)}, bf16[208,240]{1,0:T(8,128)(2,1)}, u32[]{:S(2)}) copy-start(bf16[208,240]{1,0:T(8,128)(2,1)} %constant.17.clone.rest_1_) | copy-start | bytes 299524
  14.2 10.7 %copy-start.23 = (bf16[208,240]{1,0:T(8,128)(2,1)S(1)}, bf16[208,240]{1,0:T(8,128)(2,1)}, u32[]{:S(2)}) copy-start(bf16[208,240]{1,0:T(8,128)(2,1)} %constant.16.clone.rest_0_) | copy-start | bytes 299524
  14.2 17.5 %all-to-all-start = ((f32[32,1,2176]{2,1,0:T(1,128)}), f32[32,1,2176]{2,1,0:T(1,128)}, u32[]{:S(2)}, u32[]{:S(2)}) async-start(f32[32,1,2176]{2,1,0:T(1,128)} %copy.18), calls=%async_computation | async-start | bytes 557056 | tf_op jit(solution)/shard_map/all_to_all | solution.py:420
  20.7 4.2 %copy-start.4 = (bf16[640,512]{1,0:T(8,128)(2,1)S(1)}, bf16[640,512]{1,0:T(8,128)(2,1)}, u32[]{:S(2)}) copy-start(bf16[640,512]{1,0:T(8,128)(2,1)} %constant.47.clone.rest_7_) | copy-start | bytes 1966084
  20.7 4.2 %copy-start.5 = (bf16[640,512]{1,0:T(8,128)(2,1)S(1)}, bf16[640,512]{1,0:T(8,128)(2,1)}, u32[]{:S(2)}) copy-start(bf16[640,512]{1,0:T(8,128)(2,1)} %constant.46.clone.rest_6_) | copy-start | bytes 1966084
  20.7 4.2 %copy-start.6 = (bf16[512,640]{1,0:T(8,128)(2,1)S(1)}, bf16[512,640]{1,0:T(8,128)(2,1)}, u32[]{:S(2)}) copy-start(bf16[512,640]{1,0:T(8,128)(2,1)} %constant.43.clone.rest_3_) | copy-start | bytes 1966084
  20.8 4.2 %copy-start.19 = (f32[208,128]{1,0:T(8,128)S(1)}, f32[208,128]{1,0:T(8,128)}, u32[]{:S(2)}) copy-start(f32[208,128]{1,0:T(8,128)} %constant.48.clone.rest_8_) | copy-start | bytes 319492
  21.7 16.3 %collective-permute-start.3 = (f32[64,2048]{1,0:T(8,128)}, f32[64,2048]{1,0:T(8,128)S(1)}, u32[]{:S(2)}, u32[]{:S(2)}) collective-permute-start(f32[64,2048]{1,0:T(8,128)} %get-tuple-element.46), channel_id=1, source_target_pairs={{0,1},{1,0},{2,3},{3,2},{4,5},{5,4},{6,7},{7,6},{8,9},{9,8},{10,11... | collective-permute-start | bytes 1572872 | tf_op jit(solution)/shard_map/ppermute | solution.py:437
  23.4 1.6 %copy-start.41 = (f32[1,640]{1,0:T(1,128)S(1)}, f32[1,640]{1,0:T(1,128)}, u32[]{:S(2)}) copy-start(f32[1,640]{1,0:T(1,128)} %constant.49.clone.rest_9_) | copy-start | bytes 7684
  23.4 1.5 %collective-permute-start.1 = (f32[2,24,512]{2,1,0:T(8,128)}, f32[2,24,512]{2,1,0:T(8,128)S(1)}, u32[]{:S(2)}, u32[]{:S(2)}) collective-permute-start(f32[2,24,512]{2,1,0:T(8,128)} %copy-done.43), channel_id=1, source_target_pairs={{0,2},{2,0},{4,6},{6,4},{8,10},{10,8},{12,14},{14,12},{16,18},{18,... | collective-permute-start | bytes 294920 | tf_op jit(solution)/shard_map/ppermute | solution.py:415
  23.4 1.5 %collective-permute-start.2 = (f32[2,24,512]{2,1,0:T(8,128)}, f32[2,24,512]{2,1,0:T(8,128)S(1)}, u32[]{:S(2)}, u32[]{:S(2)}) collective-permute-start(f32[2,24,512]{2,1,0:T(8,128)} %copy-done.42), channel_id=1, source_target_pairs={{2,4},{4,2},{6,8},{8,6},{10,12},{12,10},{14,16},{16,14},{18,20},{2... | collective-permute-start | bytes 294920 | tf_op jit(solution)/shard_map/ppermute | solution.py:415
  24.9 1.1 %copy-start.8 = (bf16[512,640]{1,0:T(8,128)(2,1)S(1)}, bf16[512,640]{1,0:T(8,128)(2,1)}, u32[]{:S(2)}) copy-start(bf16[512,640]{1,0:T(8,128)(2,1)} %constant.42.clone.rest_2_) | copy-start | bytes 1966084
  26.0 1.0 %copy-start.34 = (f32[8,24,512]{2,1,0:T(8,128)S(1)}, f32[8,24,512]{2,1,0:T(8,128)}, u32[]{:S(2)}) copy-start(f32[8,24,512]{2,1,0:T(8,128)} %copy-done.33) | copy-start | bytes 1179652
  27.0 0.8 copy-start.35
  27.9 0.8 copy-start.37
  30.3 0.6 copy-start.29
  31.0 0.6 copy-start.31
  31.6 6.4 %copy-start.10 = (bf16[128,1024]{1,0:T(8,128)(2,1)S(1)}, bf16[128,1024]{1,0:T(8,128)(2,1)}, u32[]{:S(2)}) copy-start(bf16[128,1024]{1,0:T(8,128)(2,1)} %constant.51.clone.spread_ref) | copy-start | bytes 786436
  38.0 6.4 %copy-start.13 = (f32[8,24,512]{2,1,0:T(8,128)S(1)}, f32[8,24,512]{2,1,0:T(8,128)}, u32[]{:S(2)}) copy-start(f32[8,24,512]{2,1,0:T(8,128)} %copy-done.12) | copy-start | bytes 1179652
  38.0 6.5 %copy-start.32 = (f32[2,24,512]{2,1,0:T(8,128)S(1)}, f32[2,24,512]{2,1,0:T(8,128)}, u32[]{:S(2)}) copy-start(f32[2,24,512]{2,1,0:T(8,128)} %copy-done.31) | copy-start | bytes 294916
  39.1 5.4 %copy-start.16 = (bf16[512,256]{1,0:T(8,128)(2,1)S(1)}, bf16[512,256]{1,0:T(8,128)(2,1)}, u32[]{:S(2)}) copy-start(bf16[512,256]{1,0:T(8,128)(2,1)} %constant.50.clone.gather_ref) | copy-start | bytes 786436
  39.1 3.9 %collective-permute-start.4 = (f32[2,8,512]{2,1,0:T(8,128)S(1)}, f32[2,8,512]{2,1,0:T(8,128)S(1)}, u32[]{:S(2)}, u32[]{:S(2)}) collective-permute-start(f32[2,8,512]{2,1,0:T(8,128)S(1)} %get-tuple-element.32), channel_id=1, source_target_pairs={{0,1},{1,0},{2,3},{3,2},{4,5},{5,4},{6,7},{7,6},{8,9},{9,8},{10,11... | collective-permute-start | bytes 98312 | tf_op jit(solution)/shard_map/ppermute | solution.py:415
  43.0 1.5 %copy-start.30 = (f32[2,24,512]{2,1,0:T(8,128)S(1)}, f32[2,24,512]{2,1,0:T(8,128)}, u32[]{:S(2)}) copy-start(f32[2,24,512]{2,1,0:T(8,128)} %copy-done.29) | copy-start | bytes 294916
  43.1 1.4 %collective-permute-start.5 = (f32[2,24,512]{2,1,0:T(8,128)S(1)}, f32[2,24,512]{2,1,0:T(8,128)S(1)}, u32[]{:S(2)}, u32[]{:S(2)}) collective-permute-start(f32[2,24,512]{2,1,0:T(8,128)S(1)} %get-tuple-element.34), channel_id=1, source_target_pairs={{0,2},{2,0},{4,6},{6,4},{8,10},{10,8},{12,14},{14,12},{16,18},{18,... | collective-permute-start | bytes 294920 | tf_op jit(solution)/shard_map/ppermute | solution.py:415
  43.2 1.3 %collective-permute-start.6 = (f32[2,24,512]{2,1,0:T(8,128)S(1)}, f32[2,24,512]{2,1,0:T(8,128)S(1)}, u32[]{:S(2)}, u32[]{:S(2)}) collective-permute-start(f32[2,24,512]{2,1,0:T(8,128)S(1)} %get-tuple-element.35), channel_id=1, source_target_pairs={{2,4},{4,2},{6,8},{8,6},{10,12},{12,10},{14,16},{16,14},{18,20},{2... | collective-permute-start | bytes 294920 | tf_op jit(solution)/shard_map/ppermute | solution.py:415
  44.5 0.7 copy-start.25
  44.5 0.7 copy-start.27
  46.2 22.5 %all-to-all-start.1 = ((f32[32,1,2176]{2,1,0:T(1,128)}), f32[32,1,2176]{2,1,0:T(1,128)}, u32[]{:S(2)}, u32[]{:S(2)}) async-start(f32[32,1,2176]{2,1,0:T(1,128)} %copy.19), calls=%async_computation.1 | async-start | bytes 557056 | tf_op jit(solution)/shard_map/all_to_all | solution.py:420
  56.6 1.1 %copy-start.7 = (bf16[512,640]{1,0:T(8,128)(2,1)S(1)}, bf16[512,640]{1,0:T(8,128)(2,1)}, u32[]{:S(2)}) copy-start(bf16[512,640]{1,0:T(8,128)(2,1)} %constant.43.clone.rest_3_) | copy-start | bytes 1966084
  57.7 1.1 %copy-start.9 = (bf16[512,640]{1,0:T(8,128)(2,1)S(1)}, bf16[512,640]{1,0:T(8,128)(2,1)}, u32[]{:S(2)}) copy-start(bf16[512,640]{1,0:T(8,128)(2,1)} %constant.42.clone.rest_2_) | copy-start | bytes 1966084
  58.8 0.9 %copy-start.20 = (f32[208,128]{1,0:T(8,128)S(1)}, f32[208,128]{1,0:T(8,128)}, u32[]{:S(2)}) copy-start(f32[208,128]{1,0:T(8,128)} %constant.48.clone.rest_8_) | copy-start | bytes 319492
  59.7 0.9 %copy-start.22 = (bf16[208,240]{1,0:T(8,128)(2,1)S(1)}, bf16[208,240]{1,0:T(8,128)(2,1)}, u32[]{:S(2)}) copy-start(bf16[208,240]{1,0:T(8,128)(2,1)} %constant.17.clone.rest_1_) | copy-start | bytes 299524
  60.6 0.9 %copy-start.24 = (bf16[208,240]{1,0:T(8,128)(2,1)S(1)}, bf16[208,240]{1,0:T(8,128)(2,1)}, u32[]{:S(2)}) copy-start(bf16[208,240]{1,0:T(8,128)(2,1)} %constant.16.clone.rest_0_) | copy-start | bytes 299524
  61.5 0.8 copy-start.36
  62.3 0.8 copy-start.38
  65.4 0.7 copy-start.39
  66.1 4.9 %collective-permute-start.8 = (f32[16,512]{1,0:T(8,128)}, f32[16,512]{1,0:T(8,128)S(1)}, u32[]{:S(2)}, u32[]{:S(2)}) collective-permute-start(f32[16,512]{1,0:T(8,128)} %get-tuple-element.41), channel_id=1, source_target_pairs={{0,2},{2,0},{4,6},{6,4},{8,10},{10,8},{12,14},{14,12},{16,18},{18,... | collective-permute-start | bytes 98312 | tf_op jit(solution)/shard_map/ppermute | solution.py:415
  66.3 4.7 %collective-permute-start.9 = (f32[16,512]{1,0:T(8,128)S(1)}, f32[16,512]{1,0:T(8,128)S(1)}, u32[]{:S(2)}, u32[]{:S(2)}) collective-permute-start(f32[16,512]{1,0:T(8,128)S(1)} %get-tuple-element.42), channel_id=1, source_target_pairs={{2,4},{4,2},{6,8},{8,6},{10,12},{12,10},{14,16},{16,14},{18,20},{2... | collective-permute-start | bytes 98312 | tf_op jit(solution)/shard_map/ppermute | solution.py:415
  66.9 4.1 %copy-start.11 = (bf16[128,1024]{1,0:T(8,128)(2,1)S(1)}, bf16[128,1024]{1,0:T(8,128)(2,1)}, u32[]{:S(2)}) copy-start(bf16[128,1024]{1,0:T(8,128)(2,1)} %constant.51.clone.spread_ref) | copy-start | bytes 786436
  67.0 4.1 %copy-start.26 = (f32[2,24,512]{2,1,0:T(8,128)S(1)}, f32[2,24,512]{2,1,0:T(8,128)}, u32[]{:S(2)}) copy-start(f32[2,24,512]{2,1,0:T(8,128)} %copy-done.25) | copy-start | bytes 294916
  67.0 4.1 %copy-start.28 = (f32[2,24,512]{2,1,0:T(8,128)S(1)}, f32[2,24,512]{2,1,0:T(8,128)}, u32[]{:S(2)}) copy-start(f32[2,24,512]{2,1,0:T(8,128)} %copy-done.27) | copy-start | bytes 294916
  67.0 4.0 %collective-permute-start.7 = (f32[8,512]{1,0:T(8,128)}, f32[8,512]{1,0:T(8,128)S(1)}, u32[]{:S(2)}, u32[]{:S(2)}) collective-permute-start(f32[8,512]{1,0:T(8,128)} %get-tuple-element.40), channel_id=1, source_target_pairs={{0,1},{1,0},{2,3},{3,2},{4,5},{5,4},{6,7},{7,6},{8,9},{9,8},{10,11... | collective-permute-start | bytes 49160 | tf_op jit(solution)/shard_map/ppermute | solution.py:415
  71.0 1.0 %copy-start.14 = (f32[8,24,512]{2,1,0:T(8,128)S(1)}, f32[8,24,512]{2,1,0:T(8,128)}, u32[]{:S(2)}) copy-start(f32[8,24,512]{2,1,0:T(8,128)} %copy-done.12) | copy-start | bytes 1179652
  72.0 0.9 %copy-start.40 = (f32[8,16,512]{2,1,0:T(8,128)S(1)}, f32[8,16,512]{2,1,0:T(8,128)}, u32[]{:S(2)}) copy-start(f32[8,16,512]{2,1,0:T(8,128)} %copy-done.39) | copy-start | bytes 786436

commit v2 on v1

v2 whole, which is shorter than its diff:
```python
import functools

import jax
import jax.numpy as jnp
import numpy as np
from jax import lax
from jax.experimental import pallas as pl
from jax.experimental.pallas import tpu as pltpu
from jax.sharding import PartitionSpec as P

F32 = jnp.float32
BF16 = jnp.bfloat16
BX, BY, BZ = 8, 16, 512
EY, EZ = 2, 64
ELEMS = EY * EZ
YR = 24
YW = YR * (BX + 2)
AB = 208
KCOL = 2048
WIDTH = KCOL + 128
AXES = ("wide", "narrow")


def split_const(values):
    high = values.astype(jnp.bfloat16)
    low = (values - high.astype(np.float64)).astype(jnp.bfloat16)
    return high, low


@functools.lru_cache(maxsize=None)
def tables():
    index = np.arange(10, dtype=np.float64)
    basis = np.sqrt(2.0 / 11.0) * np.sin(np.pi * (index[:, None] + 1.0) * (index[None, :] + 1.0) / 11.0)
    values = 2.0 - 2.0 * np.cos(np.pi * (index + 1.0) / 11.0)
    to_z = np.zeros((BZ, 10 * EZ))
    from_z = np.zeros((10 * EZ, BZ))
    for e in range(EZ):
        for k in range(10):
            z = 8 * e + k - 1
            if 0 <= z < BZ:
                to_z[z, e::EZ] = basis[k]
            if 1 <= k <= 8:
                from_z[e::EZ, z] = basis[k]
    to_xy = np.zeros((10, EY, 10, 10, YR))
    from_xy = np.zeros((BX, BY, 10, EY, 10))
    for e in range(EY):
        for j in range(10):
            y = 8 * e + j - 1
            to_xy[:, e, :, :, y % YR] += basis.T[:, None, :] * basis[j][None, :, None]
            if 1 <= j <= 8:
                from_xy[:, y, :, e, :] = basis[1:9, :, None] * basis[j][None, None, :]
    to_xy = np.pad(to_xy.reshape(200, YW), ((0, AB - 200), (0, 0)))
    from_xy = np.pad(from_xy.reshape(BX * BY, 200), ((0, 0), (0, AB - 200)))
    column = np.zeros((AB, 128), np.float32)
    grid = np.zeros((10, EY, 10, 2))
    grid[..., 0] = values[:, None, None] + values[None, None, :]
    grid[..., 1] = np.arange(EY)[None, :, None]
    column[:200, :2] = grid.reshape(200, 2)
    column[200:, 0] = 1.0
    line = np.repeat(values, EZ)[None, :].astype(np.float32)
    return split_const(to_xy) + split_const(to_z) + split_const(from_xy) + split_const(from_z) + (column, line)


def dot(a, b):
    return jnp.dot(a, b, preferred_element_type=F32)


def split2(x):
    high = x.astype(BF16)
    return high, (x - high.astype(F32)).astype(BF16)


def split3(x):
    high = x.astype(BF16)
    rest = x - high.astype(F32)
    middle = rest.astype(BF16)
    return high, middle, (rest - middle.astype(F32)).astype(BF16)


def dot3(a, b):
    return dot(a[0], b[0]) + dot(a[0], b[1]) + dot(a[1], b[0])


def iota(shape, axis):
    return lax.broadcasted_iota(jnp.int32, shape, axis)


def total(x):
    while x.ndim > 2:
        x = jnp.sum(x, axis=0)
    return jnp.sum(jnp.sum(x, axis=0, keepdims=True), axis=1, keepdims=True)


def gather_table():
    shape = (BZ, EY * ELEMS)
    node, at = iota(shape, 0), iota(shape, 1)
    return jnp.where(at == node // 8 + (at // ELEMS) * (ELEMS + EZ), 1.0, 0.0).astype(BF16)


def spread_table():
    shape = (ELEMS, EY * BZ)
    element, at = iota(shape, 0), iota(shape, 1)
    return jnp.where(at // 8 == element, 1.0, 0.0).astype(BF16)


def element_row(field):
    parts = jnp.concatenate(split3(jnp.sum(field, axis=0)), axis=0)
    sums = dot(parts, gather_table())
    sums = sums[0:16] + sums[16:32] + sums[32:48]
    return jnp.sum(sums[0:8, 0:ELEMS], axis=0, keepdims=True) + jnp.sum(sums[8:16, ELEMS:], axis=0, keepdims=True)


def expand_rows(rows):
    count = rows.shape[0]
    tall = jnp.broadcast_to(rows, (16, ELEMS)) if count == 1 else jnp.concatenate([rows, jnp.zeros((16 - count, ELEMS), F32)], axis=0)
    wide = dot(jnp.concatenate(split3(tall), axis=0), spread_table())
    return (wide[0:16] + wide[16:32] + wide[32:48])[0:count]


def expand_block(row):
    wide = expand_rows(row)
    low = jnp.broadcast_to(wide[:, 0:BZ], (8, BZ))
    high = jnp.broadcast_to(wide[:, BZ:], (8, BZ))
    return jnp.concatenate([low, high], axis=0)


def slot_mask(slots, offset):
    slot_of_row = lax.rem(iota((ELEMS, ELEMS), 0) + offset, ELEMS)
    return slot_of_row == slots


def to_rows(element_values, slots, offset):
    return jnp.sum(jnp.where(slot_mask(slots, offset), element_values, 0.0), axis=1, keepdims=True)


def to_elements(row_values, slots, offset):
    return jnp.sum(jnp.where(slot_mask(slots, offset), row_values, 0.0), axis=0, keepdims=True)


def project(column, parts):
    out = 0.0
    at = 0
    for part in parts:
        size = part.shape[0]
        out = out + jnp.sum(column[at : at + size] * part[...], axis=0, keepdims=True)
        at += size
    return out


def correct(row, parts):
    out = []
    for part in parts:
        products = part[...] * row
        folded = products[:, 0:128]
        for at in range(128, KCOL, 128):
            folded = folded + products[:, at : at + 128]
        out.append(jnp.sum(folded, axis=1, keepdims=True))
    return jnp.concatenate(out, axis=0)


def store_sum(out_ref, first, second):
    count, _, width = out_ref.shape
    cut = width - 128
    out_ref[:, :, 0:cut] = jnp.broadcast_to(first[None], (count, 1, cut))
    out_ref[:, :, cut:width] = jnp.broadcast_to(second[None], (count, 1, 128))


def lanes(values):
    at = iota((1, 128), 1)
    row = jnp.zeros((1, 128), F32)
    for i, value in enumerate(values):
        row = jnp.where(at == i, value, row)
    return row


def lane(row, i):
    return jnp.sum(jnp.where(iota(row.shape, 1) == i, row, 0.0), axis=1, keepdims=True)


def odd(index):
    return lax.rem(index, 2) == 1


def pair_out(index, low, high):
    return jnp.where(odd(index), low, high), jnp.where(odd(index), high, low)


def pair_in(index, first, second):
    return jnp.where(odd(index), first, second), jnp.where(odd(index), second, first)


def extend_y(block, low, high, depth):
    at = iota((8, BZ), 0)
    tails = []
    for x in range(block.shape[0]):
        tail = jnp.zeros((8, BZ), F32)
        for i in range(depth):
            tail = jnp.where(at == i, high[i][x : x + 1], tail)
            tail = jnp.where(at == 8 - depth + i, low[i][x : x + 1], tail)
        tails.append(tail)
    return jnp.concatenate([block, jnp.stack(tails)], axis=1)


def roll_sum(x):
    count, rows, _ = x.shape
    beside = pltpu.roll(x, 1, 1) + pltpu.roll(x, rows - 1, 1)
    flat = x.reshape(count * rows, BZ)
    at = iota(flat.shape, 1)
    beside_z = jnp.where(at == 0, 0.0, pltpu.roll(flat, 1, 1)) + jnp.where(at == BZ - 1, 0.0, pltpu.roll(flat, BZ - 1, 1))
    return beside + beside_z.reshape(x.shape)


def fine_solve(rows, sigma, consts):
    wh, wl, th, tl, vh, vl, uh, ul, column, line = consts
    spectra = split2(dot3((wh.here()[...], wl.here()[...]), split2(rows)))
    column = column.here()
    sig = jnp.where(column[:, 1:2] == 0.0, tile_lanes(sigma, 0), tile_lanes(sigma, 1))
    inverse = 1.0 / (column[:, 0:1] + line.here()[...] + sig)
    spectra = dot3(spectra, (th.here()[...], tl.here()[...])) * inverse
    nodal = dot3((vh.here()[...], vl.here()[...]), split2(spectra))
    return dot3(split2(nodal), (uh.here()[...], ul.here()[...])).reshape(BX, BY, BZ)


def tile_lanes(sigma, e):
    low = iota((1, ELEMS), 1) < EZ
    rolled = pltpu.roll(sigma, EZ, 1)
    both = jnp.where(low, sigma, rolled) if e == 0 else jnp.where(low, rolled, sigma)
    return jnp.concatenate([both] * 5, axis=1)


def eye_mask():
    return iota((ELEMS, ELEMS), 0) == iota((ELEMS, ELEMS), 1)


def row_to_column(row):
    return jnp.sum(jnp.where(eye_mask(), row, 0.0), axis=1, keepdims=True)


def column_to_row(column):
    return jnp.sum(jnp.where(eye_mask(), column, 0.0), axis=0, keepdims=True)


def pad_tile(rows):
    at = iota((8, ELEMS), 0)
    tile = jnp.zeros((8, ELEMS), F32)
    for i, row in enumerate(rows):
        tile = jnp.where(at == i, row, tile)
    return jnp.concatenate([tile, jnp.zeros((8, BZ - ELEMS), F32)], axis=1)


def start_kernel(swapped, late, factor, right, diagonal, slots, c, ya, yb, ends, factor_here, *sent):
    d = lax.axis_index("narrow")
    half = ELEMS // 2
    late.start(factor, factor_here)
    if swapped:
        late.start(factor.at[pl.ds(pl.multiple_of((1 - d) * half, half), half)], sent[0])
    row = column_to_row(to_rows(element_row(right.here()[...]) * (1.0 / 16.0), slots[...], 0))
    c[...] = row
    for i, source in enumerate((right, diagonal)):
        ref = source.here()
        ya[i], yb[i] = pair_out(d, ref[:, 0, :], ref[:, BY - 1, :])
        ends[i, 0], ends[i, 1] = ref[0], ref[BX - 1]
    ya[2] = pad_tile([row, slots[...].astype(F32)])
    yb[2] = jnp.zeros((8, BZ), F32)


def project_kernel(swapped, late, c, ra, rb, ends, factor, sums, xa, xb):
    w, d = lax.axis_index("wide"), lax.axis_index("narrow")
    row = c[...]
    if swapped:
        half = ELEMS // 2
        other = pltpu.roll(ra[2, 0:1, 0:ELEMS], half, 1)
        row = jnp.where(iota((1, ELEMS), 1) // half == d, row, other)
    store_sum(sums, project(row_to_column(row), (factor,)), jnp.zeros((1, 128), F32))
    for i in range(2):
        low, high = pair_in(d, ra[i], rb[i])
        layers = [
            extend_y(ends[i, end][None], [low[x : x + 1]], [high[x : x + 1]], 1)[0] for end, x in ((0, 0), (1, BX - 1))
        ]
        xa[i], xb[i] = pair_out(w, *layers)


def widened(block, ya, yb, xa, xb, i):
    w, d = lax.axis_index("wide"), lax.axis_index("narrow")
    low, high = pair_in(d, ya[i], yb[i])
    x_low, x_high = pair_in(w, xa[i], xb[i])
    return jnp.concatenate([x_low[None], extend_y(block, [low], [high], 1), x_high[None]], axis=0)


def first_fine_kernel(late, factor, right, diagonal, *rest):
    ya, yb, xa, xb = rest[10:14]
    solved, sigma_out, factor_here = rest[14:]
    late.start(factor, factor_here)
    rows = widened(right.here()[...], ya, yb, xa, xb, 0)
    sigma = element_row(diagonal.here()[...]) * (1.0 / 512.0)
    sigma_out[...] = sigma
    solved[...] = fine_solve(rows.reshape(YW, BZ), sigma, rest[:10])


def first_coarse_kernel(swapped, late, sums, solved, slots, factor, ya, yb):
    d = lax.axis_index("narrow")
    row = jnp.sum(sums[...], axis=0)[:, 0:KCOL]
    column = correct(row, (factor,))
    for i in range(2):
        ya[i], yb[i] = pair_out(d, solved[:, i, :], solved[:, BY - 2 + i, :])
    ya[2] = pad_tile([column_to_row(column) if swapped else to_elements(column, slots[...], 0)])
    yb[2] = ya[2]


def extend_kernel(swapped, late, solved, slots, ra_first, own_ref, ra, rb, search, xa, xb):
    w, d = lax.axis_index("wide"), lax.axis_index("narrow")
    groups = lax.axis_size("narrow")
    own = own_ref[2, 0:1, 0:ELEMS]
    theirs = ra[2, 0:1, 0:ELEMS]
    if swapped:
        half = ELEMS // 2
        at = iota((1, ELEMS), 1) // half
        other = jnp.where(at == d, pltpu.roll(own, half, 1), theirs)
        own = jnp.where(at == d, own, pltpu.roll(theirs, half, 1))
        own = to_elements(row_to_column(own), slots[...], 0)
        other = to_elements(row_to_column(other), ra_first[2, 1:2, 0:ELEMS].astype(jnp.int32), 0)
        values_low, values_high = other, other
    else:
        values_low, values_high = pair_in(d, theirs, rb[2, 0:1, 0:ELEMS])
    values_low = jnp.where(d > 0, values_low, 0.0)
    values_high = jnp.where(d < groups - 1, values_high, 0.0)
    wide = expand_rows(jnp.concatenate([own, values_low, values_high], axis=0)) * (1.0 / 16.0)
    coarse = jnp.concatenate(
        [jnp.broadcast_to(wide[0:1, 0:BZ], (8, BZ)), jnp.broadcast_to(wide[0:1, BZ:], (8, BZ))], axis=0
    )
    low, high = [], []
    for i in range(2):
        one, two = pair_in(d, ra[i], rb[i])
        low.append(one + wide[1:2, BZ:])
        high.append(two + wide[2:3, 0:BZ])
    block = extend_y(solved[...] + coarse[None], low, high, 2)
    search[...] = block
    xa[...], xb[...] = pair_out(w, block[0:2], block[BX - 2 : BX])


def operator_kernel(
    swapped, sizes, late, factor, right, diagonal, search, sa, sb, ya, yb, xa, xb, slots, received, sums, image_out, halo, kept
):
    w, d = lax.axis_index("wide"), lax.axis_index("narrow")
    half = ELEMS // 2
    offset = d * half if swapped else 0
    load = late.start(factor.at[pl.ds(pl.multiple_of(offset, half), half)] if swapped else factor.at[0:half], kept)
    s_low, s_high = pair_in(w, sa[...], sb[...])
    vector = jnp.concatenate([s_low, search[...], s_high], axis=0)
    coefficient = widened(diagonal.here()[...], ya, yb, xa, xb, 1)
    centre = vector[1 : BX + 3]
    image = (6.0 + coefficient) * centre - (vector[0 : BX + 2] + vector[2 : BX + 4] + roll_sum(centre))
    x = iota(image.shape, 0)
    y = iota(image.shape, 1)
    inside = (y < BY) | ((y == BY) & (d < sizes[1] - 1)) | ((y == YR - 1) & (d > 0))
    inside &= ((x > 0) | (w > 0)) & ((x < BX + 1) | (w < sizes[0] - 1))
    image = jnp.where(inside, image, 0.0)
    image_out[...] = image
    halo[0:BY] = s_low[1, 0:BY]
    halo[BY : 2 * BY] = s_high[0, 0:BY]
    halo[2 * BY : 2 * BY + 8] = search[:, YR - 1, :]
    halo[2 * BY + 8 : 3 * BY] = search[:, BY, :]
    own = image[1 : BX + 1, 0:BY]
    own_search = search[:, 0:BY, :]
    column = to_rows(element_row(own) * (1.0 / 16.0), slots[...], offset)
    extra = lanes([total(right.here()[...] * own_search), total(own_search * own)])
    load.wait()
    store_sum(sums, project(column, (kept, received)), extra)


def second_fine_kernel(swapped, late, factor, *rest):
    w, d = lax.axis_index("wide"), lax.axis_index("narrow")
    image, sigma, received = rest[10:13]
    solved, ya, yb, xa, xb, owned = rest[13:]
    half = ELEMS // 2
    at = pl.multiple_of(d * half, half) if swapped else 0
    late.start(factor.at[pl.ds(at, half)], owned.at[0:half])
    late.start(received, owned.at[half:ELEMS])
    out = fine_solve(image[...].reshape(YW, BZ), sigma[...], rest[:10])
    solved[...] = out
    ya[...], yb[...] = pair_out(d, solved[:, 0, :], solved[:, BY - 1, :])
    xa[...], xb[...] = pair_out(w, out[0], out[BX - 1])


def second_coarse_kernel(
    swapped, late, right, diagonal, sums, solved, fya, fyb, fxa, fxb, search, halo, image, slots, owned,
    search_out, image_out, last, products,
):
    w, d = lax.axis_index("wide"), lax.axis_index("narrow")
    offset = d * (ELEMS // 2) if swapped else 0
    row = jnp.sum(sums[...], axis=0)
    products[...] = row[:, KCOL:WIDTH]
    step = lane(row[:, KCOL:WIDTH], 0) / lane(row[:, KCOL:WIDTH], 1)
    values = to_elements(correct(row[:, 0:KCOL], (owned,)), slots[...], offset)
    coarse = expand_block(values * (1.0 / 16.0))
    own_search = search[:, 0:BY, :]
    own_image = image[1 : BX + 1, 0:BY, :]
    vector = own_search - step * (solved[...] + coarse[None])
    f_low, f_high = pair_in(w, fxa[...], fxb[...])
    x_low = halo[0:BY] - step * f_low
    x_high = halo[BY : 2 * BY] - step * f_high
    g_low, g_high = pair_in(d, fya[...], fyb[...])
    y_low = halo[2 * BY : 2 * BY + 8] - step * g_low
    y_high = halo[2 * BY + 8 : 3 * BY] - step * g_high
    beside = roll_sum(extend_y(vector, [y_low], [y_high], 1))[:, 0:BY]
    beside = beside + jnp.concatenate([x_low[None], vector[0 : BX - 1]], axis=0)
    beside = beside + jnp.concatenate([vector[1:BX], x_high[None]], axis=0)
    next_image = (6.0 + diagonal.here()[...]) * vector - beside
    search_out[...] = vector
    image_out[...] = next_image
    residual = right.here()[...] - step * own_image
    edges = total(coarse * (x_low + x_high)) + total(y_low * coarse[0:1]) + total(y_high * coarse[BY - 1 : BY])
    store_sum(
        last,
        values,
        lanes([total(residual * vector), total(vector * next_image) + step * edges, total(vector * own_image)]),
    )


def last_kernel(sizes, late, right, products, last, search, image, next_search, next_image, x_out, r_out):
    w, d = lax.axis_index("wide"), lax.axis_index("narrow")
    groups = sizes[1]
    count = sizes[0] * groups
    product, bottom = lane(products[...], 0), lane(products[...], 1)
    step = product / bottom
    z = last[:, 0, 0:ELEMS]
    rows = iota((count, ELEMS), 0)
    at = iota((count, ELEMS), 1)
    faces = jnp.where(rows < count - groups, z * pltpu.roll(z, count - groups, 0), 0.0)
    across = pltpu.roll(pltpu.roll(z, count - 1, 0), EZ, 1)
    faces = faces + jnp.where((lax.rem(rows, groups) < groups - 1) & (at >= EZ), z * across, 0.0)
    sums = jnp.sum(last[:, :, ELEMS:], axis=0)
    next_product = lane(sums, 0)
    quadratic = lane(sums, 1) - step * step * 0.5 * total(faces)
    cross = lane(sums, 2)
    me = w * groups + d
    picked = []
    for index, there in ((me - groups, w > 0), (me + groups, w < sizes[0] - 1), (me - 1, d > 0), (me + 1, d < groups - 1)):
        picked.append(jnp.sum(jnp.where((rows == index) & there, z, 0.0), axis=0, keepdims=True))
    wide = expand_rows(jnp.concatenate(picked, axis=0)) * (1.0 / 16.0)
    layers = []
    for i in range(2):
        low = jnp.broadcast_to(wide[i : i + 1, 0:BZ], (8, BZ))
        high = jnp.broadcast_to(wide[i : i + 1, BZ:], (8, BZ))
        layers.append(jnp.concatenate([low, high], axis=0)[None])
    shape = (BX, BY, BZ)
    x, y = iota(shape, 0), iota(shape, 1)
    missing = jnp.where(x == 0, layers[0], 0.0) + jnp.where(x == BX - 1, layers[1], 0.0)
    missing = missing + jnp.where(y == 0, wide[2:3, BZ:][None], 0.0) + jnp.where(y == BY - 1, wide[3:4, 0:BZ][None], 0.0)
    ratio = next_product / product
    curvature = quadratic + 2.0 * ratio * cross + ratio * ratio * bottom
    step_next = next_product / curvature
    own_search = search[:, 0:BY, :]
    own_image = image[1 : BX + 1, 0:BY, :]
    direction = next_search[...] + ratio * own_search
    total_image = next_image[...] + step * missing + ratio * own_image
    x_out[...] = step * own_search + step_next * direction
    r_out[...] = (right.here()[...] - step * own_image) - step_next * total_image


class Loaded:
    def __init__(self, copy, ref):
        self.copy, self.ref, self.ready = copy, ref, False

    def wait(self):
        if not self.ready:
            self.copy.wait()
            self.ready = True

    def here(self):
        self.wait()
        return self.ref


class Copies:
    def __init__(self, semaphores):
        self.semaphores, self.all = semaphores, []

    def start(self, source, target):
        copy = pltpu.make_async_copy(source, target, self.semaphores.at[len(self.all)])
        copy.start()
        self.all.append(Loaded(copy, target))
        return self.all[-1]

    def finish(self):
        for loaded in self.all:
            loaded.wait()


def call(kernel, outs, far=(), late=(), near=(), far_outs=(), scratch=(), final=False):
    counts = (len(far), len(late), len(near), len(outs) + len(far_outs), len(scratch), len(late))

    def run(*refs):
        parts, at = [], 0
        for size in counts:
            parts.append(refs[at : at + size])
            at += size
        copies = Copies(refs[at])
        loaded = [copies.start(source, target) for source, target in zip(parts[1], parts[5])]
        kernel(copies, *parts[0], *loaded, *parts[2], *parts[3], *parts[4])
        copies.finish()

    near_shape = jax.ShapeDtypeStruct if final else pltpu.VMEM
    spaces = [pltpu.HBM] * (len(far) + len(late)) + [pltpu.VMEM] * len(near)
    out_spaces = [pltpu.VMEM] * len(outs) + [pltpu.HBM] * len(far_outs)
    return pl.pallas_call(
        run,
        out_shape=[*(near_shape(shape, F32) for shape in outs), *(pltpu.HBM(shape, F32) for shape in far_outs)],
        in_specs=[pl.BlockSpec(memory_space=space) for space in spaces],
        out_specs=[pl.BlockSpec(memory_space=space) for space in out_spaces],
        scratch_shapes=[
            *(pltpu.VMEM(shape, F32) for shape in scratch),
            *(pltpu.VMEM(array.shape, array.dtype) for array in late),
            pltpu.SemaphoreType.DMA((len(late) + 3,)),
        ],
        compiler_params=pltpu.CompilerParams(vmem_limit_bytes=16 * 1024 * 1024),
    )(*(pltpu.with_memory_space_constraint(array, pltpu.HBM) for array in (*far, *late)), *near)


def pair_swap(first, second, axis):
    size = lax.axis_size(axis)
    received = []
    for value, begin in ((first, 0), (second, 1)):
        perm = []
        for i in range(begin, size - 1, 2):
            perm += [(i, i + 1), (i + 1, i)]
        received.append(lax.ppermute(value, axis, perm) if perm else jnp.zeros_like(value))
    return received


def everywhere(rows):
    return lax.all_to_all(rows, AXES, split_axis=0, concat_axis=0, tiled=True)


def body(right, diagonal, coarse_slot, factor):
    sizes = (lax.axis_size("wide"), lax.axis_size("narrow"))
    groups = sizes[1]
    count = sizes[0] * groups
    fine = [jnp.asarray(c) for c in tables()]
    slots = coarse_slot.reshape(1, ELEMS)
    swapped = groups == 2
    if not swapped:
        factor = factor.reshape(groups, ELEMS // groups, KCOL)
        factor = lax.all_to_all(factor, "narrow", split_axis=0, concat_axis=0, tiled=True).reshape(ELEMS, KCOL)
    part = functools.partial

    block, layer, extended = (BX, BY, BZ), (YR, BZ), (BX, YR, BZ)
    y_shape, x_shape, half, whole = (3, BX, BZ), (2, YR, BZ), (ELEMS // 2, KCOL), (ELEMS, KCOL)
    c, ya, yb, ends, near_factor, *sent = call(
        part(start_kernel, swapped),
        [(1, ELEMS), y_shape, y_shape, (2, 2, BY, BZ), whole],
        far=[factor],
        late=[right, diagonal],
        near=[slots],
        far_outs=[half] * swapped,
    )
    ya, yb = pair_swap(ya, yb, "narrow")
    received = lax.ppermute(sent[0], "narrow", [(0, 1), (1, 0)]) if swapped else factor[ELEMS // 2 :]
    sums, xa, xb = call(
        part(project_kernel, swapped), [(count, 1, WIDTH), x_shape, x_shape], near=[c, ya, yb, ends, near_factor]
    )
    sums = everywhere(sums)
    xa, xb = pair_swap(xa, xb, "wide")
    solved, sigma, near_factor = call(
        first_fine_kernel,
        [block, (1, ELEMS), whole],
        far=[factor],
        late=[right, diagonal, *fine],
        near=[ya, yb, xa, xb],
    )
    ta, tb = call(part(first_coarse_kernel, swapped), [y_shape, y_shape], near=[sums, solved, slots, near_factor])
    ra, rb = pair_swap(ta, tb, "narrow")
    search, sa, sb = call(
        part(extend_kernel, swapped), [extended, (2,) + layer, (2,) + layer], near=[solved, slots, ya, ta, ra, rb]
    )
    sa, sb = pair_swap(sa, sb, "wide")
    sums, image, halo = call(
        part(operator_kernel, swapped, sizes),
        [(count, 1, WIDTH), (BX + 2, YR, BZ), (3 * BY, BZ)],
        far=[factor],
        late=[right, diagonal],
        near=[search, sa, sb, ya, yb, xa, xb, slots, received],
        scratch=[half],
    )
    sums = everywhere(sums)
    solved, ya, yb, fa, fb, owned = call(
        part(second_fine_kernel, swapped),
        [block, (BX, BZ), (BX, BZ), (BY, BZ), (BY, BZ), whole],
        far=[factor],
        late=fine,
        near=[image, sigma, received],
    )
    ya, yb = pair_swap(ya, yb, "narrow")
    fa, fb = pair_swap(fa, fb, "wide")
    next_search, next_image, last, products = call(
        part(second_coarse_kernel, swapped),
        [block, block, (count, 1, 2 * ELEMS), (1, 128)],
        late=[right, diagonal],
        near=[sums, solved, ya, yb, fa, fb, search, halo, image, slots, owned],
    )
    last = everywhere(last)
    return tuple(
        call(
            part(last_kernel, sizes),
            [block, block],
            late=[right],
            near=[products, last, search, image, next_search, next_image],
            final=True,
        )
    )


def solution(mesh):
    in_specs = (
        P("wide", "narrow", None),
        P("wide", "narrow", None),
        P("wide", "narrow", None),
        P(("wide", "narrow"), None),
    )
    out_specs = (P("wide", "narrow", None), P("wide", "narrow", None))
    return jax.shard_map(body, mesh=mesh, in_specs=in_specs, out_specs=out_specs, check_vma=False)
```

time: 90.6 us -> 92.5 us (1.021)
  Pallas kernels: 8.72 us -> 34.8 us
  local copies, waits for them, and re-layouts: 25.6 us -> 0.77 us
  waiting for transfers between devices: 13 us -> 15.8 us
  blocking collectives: 14.6 us -> 12.9 us
    pallas_call x9, Pallas kernels: 8.72 us -> 34.8 us  [call(): pl.pallas_call(run, out_shape=[*(near_shape(shape, F32) for shape in outs...]
    unnamed x91 -> x0, local copies, waits for them, and re-layouts: 21.9 us -> none
    ppermute x1, waiting for transfers between devices: 5.35 us -> 0.01 us  [body(): lax.ppermute(sent[0], 'narrow', [(0, 1), (1, 0)])]
    all_to_all x2, waiting for transfers between devices: 0.03 us -> 5.22 us  [everywhere(): return lax.all_to_all(rows, AXES, split_axis=0, concat_axis=0, tiled=True)]
    ppermute x9, waiting for transfers between devices: 7.59 us -> 10.6 us  [pair_swap(): lax.ppermute(value, axis, perm)]
    all_to_all x3 -> x0, local copies, waits for them, and re-layouts: 2.04 us -> none  [everywhere(): return lax.all_to_all(rows, AXES, split_axis=0, concat_axis=0, tiled=True)]
    all_to_all x1, blocking collectives: 14.6 us -> 12.9 us  [everywhere(): return lax.all_to_all(rows, AXES, split_axis=0, concat_axis=0, tiled=True)]
  transfers between devices with their start and end apart: 12 -> 12, of which waited for: 6 -> 7; matrix products, arithmetic and copies ran while one was open for 3% -> 0% of each run, Pallas kernels for 4% -> 11%
where the time goes in v2:
time: 92.5 us; the launch traced here: 92 us
  Pallas kernels  34.8 us (38%)
  starting transfers between devices  27 us (29%)
  waiting for transfers between devices  15.8 us (17%)
  blocking collectives  12.9 us (14%)
    pallas_call x9, Pallas kernels, call(): pl.pallas_call(run, out_shape=[*(near_shape(shape, F32) for shape in outs...  34.8 us
    all_to_all x2, starting transfers between devices, everywhere(): return lax.all_to_all(rows, AXES, split_axis=0, concat_axis=0, tiled=True)  17 us
    all_to_all x1, blocking collectives, everywhere(): return lax.all_to_all(rows, AXES, split_axis=0, concat_axis=0, tiled=True)  12.9 us
    ppermute x9, waiting for transfers between devices, pair_swap(): lax.ppermute(value, axis, perm)  10.6 us
    ppermute x9, starting transfers between devices, pair_swap(): lax.ppermute(value, axis, perm)  8.14 us
    all_to_all x2, waiting for transfers between devices, everywhere(): return lax.all_to_all(rows, AXES, split_axis=0, concat_axis=0, tiled=True)  5.22 us
  transfers between devices with their start and end apart: 12, of which 7 were waited for; matrix products, arithmetic and copies ran while one was open for 0% of the time, Pallas kernels for 11%

profile of v2, /device:TPU:0, one launch (start us, length us, event | category | flops | bytes accessed | tf_op | source)
XLA Modules:
  0.0 92.0 jit_solution(17605252220092784901)
XLA Ops:
  0.6 0.8 reshape.7.refs_3_.refs_2_.refs_1_.refs_10_.refs_11_
  1.4 17.6 %shard_map.149 = (f32[1,128]{1,0:T(1,128)S(1)}, f32[3,8,512]{2,1,0:T(8,128)S(1)}, f32[3,8,512]{2,1,0:T(8,128)}, f32[2,2,16,512]{3,2,1,0:T(8,128)S(1)}, f32[128,2048]{1,0:T(8,128)S(1)}, /*index=5*/f32[64,2048]{1,0:T(8,128)}) custom-call(f32[128,2048]{1,0:T(8,128)} %refs_0_.9, f32[8,16,512]{2,1,0:T(8,128)} %refs_0_.11, f32[8,16,512]{2,1,0:T(8,128)} %refs_1_.8, ...), custom_call_target="tpu_custom_call" | custom-call | tf_op jit(solution)/shard_map/pallas_call | solution.py:506
  19.0 3.0 %collective-permute-start = (f32[3,8,512]{2,1,0:T(8,128)S(1)}, f32[3,8,512]{2,1,0:T(8,128)S(1)}, u32[]{:S(2)}, u32[]{:S(2)}) collective-permute-start(f32[3,8,512]{2,1,0:T(8,128)S(1)} %get-tuple-element.29), channel_id=1, source_target_pairs={{0,1},{1,0},{2,3},{3,2},{4,5},{5,4},{6,7},{7,6},{8,9},{9,8},{10,11... | collective-permute-start | bytes 147464 | tf_op jit(solution)/shard_map/ppermute | solution.py:527
  22.0 2.1 %collective-permute-done.refs_1_.refs_13_.refs_2_.refs_6_ = f32[3,8,512]{2,1,0:T(8,128)S(1)} collective-permute-done((f32[3,8,512]{2,1,0:T(8,128)S(1)}, f32[3,8,512]{2,1,0:T(8,128)S(1)}, u32[]{:S(2)}, u32[]{:S(2)}) %collective-permute-start) | collective-permute-done | bytes 49184 | tf_op jit(solution)/shard_map/ppermute | solution.py:527
  24.1 1.0 %shard_map.150 = (f32[32,1,2176]{2,1,0:T(1,128)}, f32[2,24,512]{2,1,0:T(8,128)S(1)}, f32[2,24,512]{2,1,0:T(8,128)S(1)}) custom-call(f32[1,128]{1,0:T(1,128)S(1)} %get-tuple-element.30.refs_0_, f32[3,8,512]{2,1,0:T(8,128)S(1)} %collective-permute-done.refs_1_.refs_13_.refs_2_.refs_6_, ...), custom_call_target="tpu_custom_call" | custom-call | tf_op jit(solution)/shard_map/pallas_call | solution.py:506
  25.1 6.4 %all-to-all-start = ((f32[32,1,2176]{2,1,0:T(1,128)}), f32[32,1,2176]{2,1,0:T(1,128)S(1)}, u32[]{:S(2)}, u32[]{:S(2)}) async-start(f32[32,1,2176]{2,1,0:T(1,128)} %get-tuple-element.36), calls=%async_computation | async-start | bytes 557056 | tf_op jit(solution)/shard_map/all_to_all | solution.py:532
  31.5 1.8 %collective-permute-start.6 = (f32[64,2048]{1,0:T(8,128)}, f32[64,2048]{1,0:T(8,128)S(1)}, u32[]{:S(2)}, u32[]{:S(2)}) collective-permute-start(f32[64,2048]{1,0:T(8,128)} %get-tuple-element.42), channel_id=1, source_target_pairs={{0,1},{1,0},{2,3},{3,2},{4,5},{5,4},{6,7},{7,6},{8,9},{9,8},{10,11... | collective-permute-start | bytes 1572872 | tf_op jit(solution)/shard_map/ppermute | solution.py:558
  33.3 0.0 collective-permute-start.1
  33.3 0.7 collective-permute-start.2
  34.0 0.6 collective-permute-done.1.refs_15_.refs_8_
  34.6 0.0 collective-permute-done.2.refs_16_.refs_9_
  34.6 4.3 %shard_map.151 = (f32[8,16,512]{2,1,0:T(8,128)S(1)}, f32[1,128]{1,0:T(1,128)S(1)}, f32[128,2048]{1,0:T(8,128)S(1)}) custom-call(f32[128,2048]{1,0:T(8,128)} %refs_0_.9, f32[8,16,512]{2,1,0:T(8,128)} %refs_0_.11, f32[8,16,512]{2,1,0:T(8,128)} %refs_1_.8, bf16[208,240]{1,0:T(8,128)(2,1)} %constant.10.clone.refs_3_.refs_1_, ...), custom_call_target="tpu_custom_call" | custom-call | tf_op jit(solution)/shard_map/pallas_call | solution.py:506
  38.9 3.5 %all-to-all-done.refs_0_ = f32[32,1,2176]{2,1,0:T(1,128)S(1)} async-done(((f32[32,1,2176]{2,1,0:T(1,128)}), f32[32,1,2176]{2,1,0:T(1,128)S(1)}, u32[]{:S(2)}, u32[]{:S(2)}) %all-to-all-start) | async-done | bytes 278560 | tf_op jit(solution)/shard_map/all_to_all | solution.py:532
  42.5 0.9 %shard_map.152 = (f32[3,8,512]{2,1,0:T(8,128)S(1)}, f32[3,8,512]{2,1,0:T(8,128)}) custom-call(f32[32,1,2176]{2,1,0:T(1,128)S(1)} %all-to-all-done.refs_0_, f32[8,16,512]{2,1,0:T(8,128)S(1)} %get-tuple-element.35.refs_1_.refs_0_, s32[1,128]{1,0:T(1,128)S(1)} %reshape.7.refs_3_.refs_2_.refs_1_.refs_10_.refs_11_, f32[128,2048]{1,0:T(8,128)S(1)} %get-tuple-element.37.refs_3_), custom_call_target="tpu_custom_call" | custom-call | tf_op jit(solution)/shard_map/pallas_call | solution.py:506
  43.4 1.0 %collective-permute-start.3 = (f32[3,8,512]{2,1,0:T(8,128)S(1)}, f32[3,8,512]{2,1,0:T(8,128)S(1)}, u32[]{:S(2)}, u32[]{:S(2)}) collective-permute-start(f32[3,8,512]{2,1,0:T(8,128)S(1)} %get-tuple-element.38.refs_3_), channel_id=1, source_target_pairs={{0,1},{1,0},{2,3},{3,2},{4,5},{5,4},{6,7},{7,6},{8,9},{9,8},{10,11... | collective-permute-start | bytes 147464 | tf_op jit(solution)/shard_map/ppermute | solution.py:527
  44.5 5.2 %collective-permute-done.3.refs_4_ = f32[3,8,512]{2,1,0:T(8,128)S(1)} collective-permute-done((f32[3,8,512]{2,1,0:T(8,128)S(1)}, f32[3,8,512]{2,1,0:T(8,128)S(1)}, u32[]{:S(2)}, u32[]{:S(2)}) %collective-permute-start.3) | collective-permute-done | bytes 49184 | tf_op jit(solution)/shard_map/ppermute | solution.py:527
  49.6 0.4 shard_map.153
  50.1 0.1 collective-permute-start.4
  50.2 0.7 collective-permute-start.5
  50.8 0.0 collective-permute-done.6.refs_11_.refs_13_
  50.9 0.6 collective-permute-done.4.refs_4_
  51.5 0.0 collective-permute-done.5.refs_5_
  51.5 2.6 %shard_map.154 = (f32[32,1,2176]{2,1,0:T(1,128)}, f32[10,24,512]{2,1,0:T(8,128)S(1)}, f32[48,512]{1,0:T(8,128)S(1)}) custom-call(f32[128,2048]{1,0:T(8,128)} %refs_0_.9, f32[8,16,512]{2,1,0:T(8,128)} %refs_0_.11, f32[8,16,512]{2,1,0:T(8,128)} %refs_1_.8, f32[8,24,512]{2,1,0:T(8,128)S(1)} %get-tuple-element.39.refs_3_.refs_8_, ...), custom_call_target="tpu_custom_call" | custom-call | tf_op jit(solution)/shard_map/pallas_call | solution.py:506
  54.1 10.6 %all-to-all-start.1 = ((f32[32,1,2176]{2,1,0:T(1,128)}), f32[32,1,2176]{2,1,0:T(1,128)S(1)}, u32[]{:S(2)}, u32[]{:S(2)}) async-start(f32[32,1,2176]{2,1,0:T(1,128)} %get-tuple-element.43), calls=%async_computation.1 | async-start | bytes 557056 | tf_op jit(solution)/shard_map/all_to_all | solution.py:532
  64.7 4.5 %shard_map.155 = (f32[8,16,512]{2,1,0:T(8,128)S(1)}, f32[8,512]{1,0:T(8,128)S(1)}, f32[8,512]{1,0:T(8,128)}, f32[16,512]{1,0:T(8,128)S(1)}, f32[16,512]{1,0:T(8,128)S(1)}, /*index=5*/f32[128,2048]{1,0:T(8,128)S(1)}) custom-call(f32[128,2048]{1,0:T(8,128)} %refs_0_.9, bf16[208,240]{1,0:T(8,128)(2,1)} %constant.10.clone.refs_3_.refs_1_, ...), custom_call_target="tpu_custom_call" | custom-call | tf_op jit(solution)/shard_map/pallas_call | solution.py:506
  69.2 0.3 collective-permute-start.8
  69.5 0.7 collective-permute-start.9
  70.1 1.7 %collective-permute-start.7 = (f32[8,512]{1,0:T(8,128)S(1)}, f32[8,512]{1,0:T(8,128)S(1)}, u32[]{:S(2)}, u32[]{:S(2)}) collective-permute-start(f32[8,512]{1,0:T(8,128)S(1)} %get-tuple-element.47), channel_id=1, source_target_pairs={{0,1},{1,0},{2,3},{3,2},{4,5},{5,4},{6,7},{7,6},{8,9},{9,8},{10,11... | collective-permute-start | bytes 49160 | tf_op jit(solution)/shard_map/ppermute | solution.py:527
  71.9 2.1 %collective-permute-done.7.refs_4_ = f32[8,512]{1,0:T(8,128)S(1)} collective-permute-done((f32[8,512]{1,0:T(8,128)S(1)}, f32[8,512]{1,0:T(8,128)S(1)}, u32[]{:S(2)}, u32[]{:S(2)}) %collective-permute-start.7) | collective-permute-done | bytes 16416 | tf_op jit(solution)/shard_map/ppermute | solution.py:527
  73.9 0.0 collective-permute-done.8.refs_6_
  74.0 0.0 collective-permute-done.9.refs_7_
  74.0 1.7 %all-to-all-done.1.refs_2_ = f32[32,1,2176]{2,1,0:T(1,128)S(1)} async-done(((f32[32,1,2176]{2,1,0:T(1,128)}), f32[32,1,2176]{2,1,0:T(1,128)S(1)}, u32[]{:S(2)}, u32[]{:S(2)}) %all-to-all-start.1) | async-done | bytes 278560 | tf_op jit(solution)/shard_map/all_to_all | solution.py:532
  75.7 1.6 %shard_map.156 = (f32[8,16,512]{2,1,0:T(8,128)S(1)}, f32[8,16,512]{2,1,0:T(8,128)S(1)}, f32[32,1,256]{2,1,0:T(1,128)S(1)}, f32[1,128]{1,0:T(1,128)S(1)}) custom-call(f32[8,16,512]{2,1,0:T(8,128)} %refs_0_.11, f32[8,16,512]{2,1,0:T(8,128)} %refs_1_.8, f32[32,1,2176]{2,1,0:T(1,128)S(1)} %all-to-all-done.1.refs_2_, ...), custom_call_target="tpu_custom_call" | custom-call | tf_op jit(solution)/shard_map/pallas_call | solution.py:506
  77.3 12.9 %all_to_all.15.refs_2_ = f32[32,1,256]{2,1,0:T(1,128)S(1)} all-to-all(f32[32,1,256]{2,1,0:T(1,128)S(1)} %get-tuple-element.53), channel_id=1, replica_groups=mesh['wide'=16,'narrow'=2] {'wide','narrow'}, dimensions={0} | all-to-all | bytes 65536 | tf_op jit(solution)/shard_map/all_to_all | solution.py:532
  90.2 1.8 %shard_map.157 = (f32[8,16,512]{2,1,0:T(8,128)}, f32[8,16,512]{2,1,0:T(8,128)}) custom-call(f32[8,16,512]{2,1,0:T(8,128)} %refs_0_.11, f32[1,128]{1,0:T(1,128)S(1)} %get-tuple-element.52.refs_1_, f32[32,1,256]{2,1,0:T(1,128)S(1)} %all_to_all.15.refs_2_, f32[8,24,512]{2,1,0:T(8,128)S(1)} %get-tuple-element.39.refs_3_.refs_8_, ...), custom_call_target="tpu_custom_call" | custom-call | tf_op jit(solution)/shard_map/pallas_call | solution.py:506
  (2 shorter events, 0.0 us)
Async XLA Ops:
  19.0 5.1 %collective-permute-start = (f32[3,8,512]{2,1,0:T(8,128)S(1)}, f32[3,8,512]{2,1,0:T(8,128)S(1)}, u32[]{:S(2)}, u32[]{:S(2)}) collective-permute-start(f32[3,8,512]{2,1,0:T(8,128)S(1)} %get-tuple-element.29), channel_id=1, source_target_pairs={{0,1},{1,0},{2,3},{3,2},{4,5},{5,4},{6,7},{7,6},{8,9},{9,8},{10,11... | collective-permute-start | bytes 147464 | tf_op jit(solution)/shard_map/ppermute | solution.py:527
  25.1 17.4 %all-to-all-start = ((f32[32,1,2176]{2,1,0:T(1,128)}), f32[32,1,2176]{2,1,0:T(1,128)S(1)}, u32[]{:S(2)}, u32[]{:S(2)}) async-start(f32[32,1,2176]{2,1,0:T(1,128)} %get-tuple-element.36), calls=%async_computation | async-start | bytes 557056 | tf_op jit(solution)/shard_map/all_to_all | solution.py:532
  31.5 19.3 %collective-permute-start.6 = (f32[64,2048]{1,0:T(8,128)}, f32[64,2048]{1,0:T(8,128)S(1)}, u32[]{:S(2)}, u32[]{:S(2)}) collective-permute-start(f32[64,2048]{1,0:T(8,128)} %get-tuple-element.42), channel_id=1, source_target_pairs={{0,1},{1,0},{2,3},{3,2},{4,5},{5,4},{6,7},{7,6},{8,9},{9,8},{10,11... | collective-permute-start | bytes 1572872 | tf_op jit(solution)/shard_map/ppermute | solution.py:558
  33.3 1.3 %collective-permute-start.1 = (f32[2,24,512]{2,1,0:T(8,128)S(1)}, f32[2,24,512]{2,1,0:T(8,128)S(1)}, u32[]{:S(2)}, u32[]{:S(2)}) collective-permute-start(f32[2,24,512]{2,1,0:T(8,128)S(1)} %get-tuple-element.33), channel_id=1, source_target_pairs={{0,2},{2,0},{4,6},{6,4},{8,10},{10,8},{12,14},{14,12},{16,18},{18,... | collective-permute-start | bytes 294920 | tf_op jit(solution)/shard_map/ppermute | solution.py:527
  33.3 1.3 %collective-permute-start.2 = (f32[2,24,512]{2,1,0:T(8,128)S(1)}, f32[2,24,512]{2,1,0:T(8,128)S(1)}, u32[]{:S(2)}, u32[]{:S(2)}) collective-permute-start(f32[2,24,512]{2,1,0:T(8,128)S(1)} %get-tuple-element.34), channel_id=1, source_target_pairs={{2,4},{4,2},{6,8},{8,6},{10,12},{12,10},{14,16},{16,14},{18,20},{2... | collective-permute-start | bytes 294920 | tf_op jit(solution)/shard_map/ppermute | solution.py:527
  43.4 6.2 %collective-permute-start.3 = (f32[3,8,512]{2,1,0:T(8,128)S(1)}, f32[3,8,512]{2,1,0:T(8,128)S(1)}, u32[]{:S(2)}, u32[]{:S(2)}) collective-permute-start(f32[3,8,512]{2,1,0:T(8,128)S(1)} %get-tuple-element.38.refs_3_), channel_id=1, source_target_pairs={{0,1},{1,0},{2,3},{3,2},{4,5},{5,4},{6,7},{7,6},{8,9},{9,8},{10,11... | collective-permute-start | bytes 147464 | tf_op jit(solution)/shard_map/ppermute | solution.py:527
  50.1 1.4 %collective-permute-start.4 = (f32[2,24,512]{2,1,0:T(8,128)S(1)}, f32[2,24,512]{2,1,0:T(8,128)S(1)}, u32[]{:S(2)}, u32[]{:S(2)}) collective-permute-start(f32[2,24,512]{2,1,0:T(8,128)S(1)} %get-tuple-element.40), channel_id=1, source_target_pairs={{0,2},{2,0},{4,6},{6,4},{8,10},{10,8},{12,14},{14,12},{16,18},{18,... | collective-permute-start | bytes 294920 | tf_op jit(solution)/shard_map/ppermute | solution.py:527
  50.2 1.3 %collective-permute-start.5 = (f32[2,24,512]{2,1,0:T(8,128)S(1)}, f32[2,24,512]{2,1,0:T(8,128)S(1)}, u32[]{:S(2)}, u32[]{:S(2)}) collective-permute-start(f32[2,24,512]{2,1,0:T(8,128)S(1)} %get-tuple-element.41), channel_id=1, source_target_pairs={{2,4},{4,2},{6,8},{8,6},{10,12},{12,10},{14,16},{16,14},{18,20},{2... | collective-permute-start | bytes 294920 | tf_op jit(solution)/shard_map/ppermute | solution.py:527
  54.1 21.6 %all-to-all-start.1 = ((f32[32,1,2176]{2,1,0:T(1,128)}), f32[32,1,2176]{2,1,0:T(1,128)S(1)}, u32[]{:S(2)}, u32[]{:S(2)}) async-start(f32[32,1,2176]{2,1,0:T(1,128)} %get-tuple-element.43), calls=%async_computation.1 | async-start | bytes 557056 | tf_op jit(solution)/shard_map/all_to_all | solution.py:532
  69.2 4.8 %collective-permute-start.8 = (f32[16,512]{1,0:T(8,128)S(1)}, f32[16,512]{1,0:T(8,128)S(1)}, u32[]{:S(2)}, u32[]{:S(2)}) collective-permute-start(f32[16,512]{1,0:T(8,128)S(1)} %get-tuple-element.48), channel_id=1, source_target_pairs={{0,2},{2,0},{4,6},{6,4},{8,10},{10,8},{12,14},{14,12},{16,18},{18,... | collective-permute-start | bytes 98312 | tf_op jit(solution)/shard_map/ppermute | solution.py:527
  69.5 4.5 %collective-permute-start.9 = (f32[16,512]{1,0:T(8,128)S(1)}, f32[16,512]{1,0:T(8,128)S(1)}, u32[]{:S(2)}, u32[]{:S(2)}) collective-permute-start(f32[16,512]{1,0:T(8,128)S(1)} %get-tuple-element.49), channel_id=1, source_target_pairs={{2,4},{4,2},{6,8},{8,6},{10,12},{12,10},{14,16},{16,14},{18,20},{2... | collective-permute-start | bytes 98312 | tf_op jit(solution)/shard_map/ppermute | solution.py:527
  70.1 3.8 %collective-permute-start.7 = (f32[8,512]{1,0:T(8,128)S(1)}, f32[8,512]{1,0:T(8,128)S(1)}, u32[]{:S(2)}, u32[]{:S(2)}) collective-permute-start(f32[8,512]{1,0:T(8,128)S(1)} %get-tuple-element.47), channel_id=1, source_target_pairs={{0,1},{1,0},{2,3},{3,2},{4,5},{5,4},{6,7},{7,6},{8,9},{9,8},{10,11... | collective-permute-start | bytes 49160 | tf_op jit(solution)/shard_map/ppermute | solution.py:527

commit v3 on v2

--- a/solution.py
+++ b/solution.py
@@ -16,6 +16,8 @@
 YR = 24
 YW = YR * (BX + 2)
 AB = 208
+HZ = 256
+HW = 384
 KCOL = 2048
 WIDTH = KCOL + 128
 AXES = ("wide", "narrow")
@@ -32,15 +34,22 @@
     index = np.arange(10, dtype=np.float64)
     basis = np.sqrt(2.0 / 11.0) * np.sin(np.pi * (index[:, None] + 1.0) * (index[None, :] + 1.0) / 11.0)
     values = 2.0 - 2.0 * np.cos(np.pi * (index + 1.0) / 11.0)
-    to_z = np.zeros((BZ, 10 * EZ))
-    from_z = np.zeros((10 * EZ, BZ))
-    for e in range(EZ):
+    to_z = np.zeros((HZ, HW))
+    from_z = np.zeros((HW, HZ))
+    beyond = np.zeros((8, HW), np.float32)
+    last = HZ // 8 - 1
+    for e in range(last + 1):
+        at = slice(e, 10 * (last + 1), last + 1)
         for k in range(10):
             z = 8 * e + k - 1
-            if 0 <= z < BZ:
-                to_z[z, e::EZ] = basis[k]
+            if 0 <= z < HZ:
+                to_z[z, at] = basis[k]
             if 1 <= k <= 8:
-                from_z[e::EZ, z] = basis[k]
+                from_z[at, z] = basis[k]
+    beyond[0, last : 10 * (last + 1) : last + 1] = basis[9]
+    beyond[1, 0 : 10 * (last + 1) : last + 1] = basis[0]
+    beyond[2] = 1.0
+    beyond[2, : 10 * (last + 1)] = np.repeat(values, last + 1)
     to_xy = np.zeros((10, EY, 10, 10, YR))
     from_xy = np.zeros((BX, BY, 10, EY, 10))
     for e in range(EY):
@@ -57,8 +66,7 @@
     grid[..., 1] = np.arange(EY)[None, :, None]
     column[:200, :2] = grid.reshape(200, 2)
     column[200:, 0] = 1.0
-    line = np.repeat(values, EZ)[None, :].astype(np.float32)
-    return split_const(to_xy) + split_const(to_z) + split_const(from_xy) + split_const(from_z) + (column, line)
+    return split_const(to_xy) + split_const(to_z) + split_const(from_xy) + split_const(from_z) + (column, beyond)
 
 
 def dot(a, b):
@@ -210,22 +218,27 @@
     return beside + beside_z.reshape(x.shape)
 
 
-def fine_solve(rows, sigma, consts):
-    wh, wl, th, tl, vh, vl, uh, ul, column, line = consts
-    spectra = split2(dot3((wh.here()[...], wl.here()[...]), split2(rows)))
-    column = column.here()
-    sig = jnp.where(column[:, 1:2] == 0.0, tile_lanes(sigma, 0), tile_lanes(sigma, 1))
-    inverse = 1.0 / (column[:, 0:1] + line.here()[...] + sig)
-    spectra = dot3(spectra, (th.here()[...], tl.here()[...])) * inverse
-    nodal = dot3((vh.here()[...], vl.here()[...]), split2(spectra))
-    return dot3(split2(nodal), (uh.here()[...], ul.here()[...])).reshape(BX, BY, BZ)
-
-
-def tile_lanes(sigma, e):
-    low = iota((1, ELEMS), 1) < EZ
-    rolled = pltpu.roll(sigma, EZ, 1)
-    both = jnp.where(low, sigma, rolled) if e == 0 else jnp.where(low, rolled, sigma)
-    return jnp.concatenate([both] * 5, axis=1)
+def fine_solve(rows, sigma, tables):
+    wh, wl, th, tl, vh, vl, uh, ul, column, beyond = tables
+    spectra = dot3((wh.here()[...], wl.here()[...]), split2(rows))
+    th, tl, column, beyond, vh, vl, uh, ul = [table.here()[...] for table in (th, tl, column, beyond, vh, vl, uh, ul)]
+    nodal = []
+    for half in range(2):
+        part = spectra[:, half * HZ : (half + 1) * HZ]
+        edge = spectra[:, HZ : HZ + 1] if half == 0 else spectra[:, HZ - 1 : HZ]
+        part = dot3(split2(part), (th, tl)) + edge * beyond[half : half + 1]
+        sig = jnp.where(column[:, 1:2] == 0.0, repeat_lanes(sigma, half), repeat_lanes(sigma, 2 + half))
+        part = part / (column[:, 0:1] + beyond[2:3] + sig)
+        part = dot3((vh, vl), split2(part))
+        nodal.append(dot3(split2(part), (uh, ul)).reshape(BX, BY, HZ))
+    return jnp.concatenate(nodal, axis=2)
+
+
+def repeat_lanes(row, group):
+    only = jnp.where(iota((1, ELEMS), 1) // 32 == group, row, 0.0)
+    only = only + pltpu.roll(only, 64, 1)
+    only = only + pltpu.roll(only, 32, 1)
+    return jnp.concatenate([only] * 3, axis=1)
 
 
 def eye_mask():
@@ -248,23 +261,24 @@
     return jnp.concatenate([tile, jnp.zeros((8, BZ - ELEMS), F32)], axis=1)
 
 
-def start_kernel(swapped, late, factor, right, diagonal, slots, c, ya, yb, ends, factor_here, *sent):
+def start_kernel(swapped, late, right_far, diagonal_far, factor, slots, c, ya, yb, right, diagonal, factor_here, sent):
     d = lax.axis_index("narrow")
     half = ELEMS // 2
+    right_load = late.start(right_far, right)
+    diagonal_load = late.start(diagonal_far, diagonal)
+    late.start(factor.at[pl.ds(pl.multiple_of((1 - d) * half, half), half)] if swapped else factor.at[half:ELEMS], sent)
     late.start(factor, factor_here)
-    if swapped:
-        late.start(factor.at[pl.ds(pl.multiple_of((1 - d) * half, half), half)], sent[0])
-    row = column_to_row(to_rows(element_row(right.here()[...]) * (1.0 / 16.0), slots[...], 0))
+    right_load.wait()
+    row = column_to_row(to_rows(element_row(right[...]) * (1.0 / 16.0), slots[...], 0))
     c[...] = row
-    for i, source in enumerate((right, diagonal)):
-        ref = source.here()
+    diagonal_load.wait()
+    for i, ref in enumerate((right, diagonal)):
         ya[i], yb[i] = pair_out(d, ref[:, 0, :], ref[:, BY - 1, :])
-        ends[i, 0], ends[i, 1] = ref[0], ref[BX - 1]
     ya[2] = pad_tile([row, slots[...].astype(F32)])
     yb[2] = jnp.zeros((8, BZ), F32)
 
 
-def project_kernel(swapped, late, c, ra, rb, ends, factor, sums, xa, xb):
+def project_kernel(swapped, late, c, ra, rb, right, diagonal, factor, sums, xa, xb):
     w, d = lax.axis_index("wide"), lax.axis_index("narrow")
     row = c[...]
     if swapped:
@@ -272,11 +286,9 @@
         other = pltpu.roll(ra[2, 0:1, 0:ELEMS], half, 1)
         row = jnp.where(iota((1, ELEMS), 1) // half == d, row, other)
     store_sum(sums, project(row_to_column(row), (factor,)), jnp.zeros((1, 128), F32))
-    for i in range(2):
+    for i, ref in enumerate((right, diagonal)):
         low, high = pair_in(d, ra[i], rb[i])
-        layers = [
-            extend_y(ends[i, end][None], [low[x : x + 1]], [high[x : x + 1]], 1)[0] for end, x in ((0, 0), (1, BX - 1))
-        ]
+        layers = [extend_y(ref[x : x + 1], [low[x : x + 1]], [high[x : x + 1]], 1)[0] for x in (0, BX - 1)]
         xa[i], xb[i] = pair_out(w, *layers)
 
 
@@ -287,12 +299,10 @@
     return jnp.concatenate([x_low[None], extend_y(block, [low], [high], 1), x_high[None]], axis=0)
 
 
-def first_fine_kernel(late, factor, right, diagonal, *rest):
-    ya, yb, xa, xb = rest[10:14]
-    solved, sigma_out, factor_here = rest[14:]
-    late.start(factor, factor_here)
-    rows = widened(right.here()[...], ya, yb, xa, xb, 0)
-    sigma = element_row(diagonal.here()[...]) * (1.0 / 512.0)
+def first_fine_kernel(late, *rest):
+    right, diagonal, ya, yb, xa, xb, solved, sigma_out = rest[10:]
+    rows = widened(right[...], ya, yb, xa, xb, 0)
+    sigma = element_row(diagonal[...]) * (1.0 / 512.0)
     sigma_out[...] = sigma
     solved[...] = fine_solve(rows.reshape(YW, BZ), sigma, rest[:10])
 
@@ -338,16 +348,22 @@
     xa[...], xb[...] = pair_out(w, block[0:2], block[BX - 2 : BX])
 
 
+def owned_rows(swapped, factor, received):
+    half = ELEMS // 2
+    if not swapped:
+        return (factor,), 0
+    at = lax.axis_index("narrow") * half
+    return (factor.at[pl.ds(pl.multiple_of(at, half), half)], received), at
+
+
 def operator_kernel(
-    swapped, sizes, late, factor, right, diagonal, search, sa, sb, ya, yb, xa, xb, slots, received, sums, image_out, halo, kept
+    swapped, sizes, late, right, diagonal, factor, received, search, sa, sb, ya, yb, xa, xb, slots, sums, image_out, halo
 ):
     w, d = lax.axis_index("wide"), lax.axis_index("narrow")
-    half = ELEMS // 2
-    offset = d * half if swapped else 0
-    load = late.start(factor.at[pl.ds(pl.multiple_of(offset, half), half)] if swapped else factor.at[0:half], kept)
+    owned, offset = owned_rows(swapped, factor, received)
     s_low, s_high = pair_in(w, sa[...], sb[...])
     vector = jnp.concatenate([s_low, search[...], s_high], axis=0)
-    coefficient = widened(diagonal.here()[...], ya, yb, xa, xb, 1)
+    coefficient = widened(diagonal[...], ya, yb, xa, xb, 1)
     centre = vector[1 : BX + 3]
     image = (6.0 + coefficient) * centre - (vector[0 : BX + 2] + vector[2 : BX + 4] + roll_sum(centre))
     x = iota(image.shape, 0)
@@ -363,19 +379,13 @@
     own = image[1 : BX + 1, 0:BY]
     own_search = search[:, 0:BY, :]
     column = to_rows(element_row(own) * (1.0 / 16.0), slots[...], offset)
-    extra = lanes([total(right.here()[...] * own_search), total(own_search * own)])
-    load.wait()
-    store_sum(sums, project(column, (kept, received)), extra)
-
-
-def second_fine_kernel(swapped, late, factor, *rest):
+    extra = lanes([total(right[...] * own_search), total(own_search * own)])
+    store_sum(sums, project(column, owned), extra)
+
+
+def second_fine_kernel(late, *rest):
     w, d = lax.axis_index("wide"), lax.axis_index("narrow")
-    image, sigma, received = rest[10:13]
-    solved, ya, yb, xa, xb, owned = rest[13:]
-    half = ELEMS // 2
-    at = pl.multiple_of(d * half, half) if swapped else 0
-    late.start(factor.at[pl.ds(at, half)], owned.at[0:half])
-    late.start(received, owned.at[half:ELEMS])
+    image, sigma, solved, ya, yb, xa, xb = rest[10:]
     out = fine_solve(image[...].reshape(YW, BZ), sigma[...], rest[:10])
     solved[...] = out
     ya[...], yb[...] = pair_out(d, solved[:, 0, :], solved[:, BY - 1, :])
@@ -383,15 +393,15 @@
 
 
 def second_coarse_kernel(
-    swapped, late, right, diagonal, sums, solved, fya, fyb, fxa, fxb, search, halo, image, slots, owned,
+    swapped, late, right, diagonal, factor, received, sums, solved, fya, fyb, fxa, fxb, search, halo, image, slots,
     search_out, image_out, last, products,
 ):
     w, d = lax.axis_index("wide"), lax.axis_index("narrow")
-    offset = d * (ELEMS // 2) if swapped else 0
+    owned, offset = owned_rows(swapped, factor, received)
     row = jnp.sum(sums[...], axis=0)
     products[...] = row[:, KCOL:WIDTH]
     step = lane(row[:, KCOL:WIDTH], 0) / lane(row[:, KCOL:WIDTH], 1)
-    values = to_elements(correct(row[:, 0:KCOL], (owned,)), slots[...], offset)
+    values = to_elements(correct(row[:, 0:KCOL], owned), slots[...], offset)
     coarse = expand_block(values * (1.0 / 16.0))
     own_search = search[:, 0:BY, :]
     own_image = image[1 : BX + 1, 0:BY, :]
@@ -405,10 +415,10 @@
     beside = roll_sum(extend_y(vector, [y_low], [y_high], 1))[:, 0:BY]
     beside = beside + jnp.concatenate([x_low[None], vector[0 : BX - 1]], axis=0)
     beside = beside + jnp.concatenate([vector[1:BX], x_high[None]], axis=0)
-    next_image = (6.0 + diagonal.here()[...]) * vector - beside
+    next_image = (6.0 + diagonal[...]) * vector - beside
     search_out[...] = vector
     image_out[...] = next_image
-    residual = right.here()[...] - step * own_image
+    residual = right[...] - step * own_image
     edges = total(coarse * (x_low + x_high)) + total(y_low * coarse[0:1]) + total(y_high * coarse[BY - 1 : BY])
     store_sum(
         last,
@@ -455,7 +465,7 @@
     direction = next_search[...] + ratio * own_search
     total_image = next_image[...] + step * missing + ratio * own_image
     x_out[...] = step * own_search + step_next * direction
-    r_out[...] = (right.here()[...] - step * own_image) - step_next * total_image
+    r_out[...] = (right[...] - step * own_image) - step_next * total_image
 
 
 class Loaded:
@@ -487,32 +497,24 @@
             loaded.wait()
 
 
-def call(kernel, outs, far=(), late=(), near=(), far_outs=(), scratch=(), final=False):
-    counts = (len(far), len(late), len(near), len(outs) + len(far_outs), len(scratch), len(late))
+def call(kernel, outs, far=(), late=(), near=(), final=False):
+    first, second = len(far), len(far) + len(late)
 
     def run(*refs):
-        parts, at = [], 0
-        for size in counts:
-            parts.append(refs[at : at + size])
-            at += size
-        copies = Copies(refs[at])
-        loaded = [copies.start(source, target) for source, target in zip(parts[1], parts[5])]
-        kernel(copies, *parts[0], *loaded, *parts[2], *parts[3], *parts[4])
+        end = len(refs) - 1 - len(late)
+        copies = Copies(refs[-1])
+        loaded = [copies.start(source, target) for source, target in zip(refs[first:second], refs[end:-1])]
+        kernel(copies, *refs[:first], *loaded, *refs[second:end])
         copies.finish()
 
-    near_shape = jax.ShapeDtypeStruct if final else pltpu.VMEM
-    spaces = [pltpu.HBM] * (len(far) + len(late)) + [pltpu.VMEM] * len(near)
-    out_spaces = [pltpu.VMEM] * len(outs) + [pltpu.HBM] * len(far_outs)
+    shape_of = jax.ShapeDtypeStruct if final else pltpu.VMEM
+    spaces = [pltpu.HBM] * second + [pltpu.VMEM] * len(near)
     return pl.pallas_call(
         run,
-        out_shape=[*(near_shape(shape, F32) for shape in outs), *(pltpu.HBM(shape, F32) for shape in far_outs)],
+        out_shape=[shape_of(out, F32) for out in outs],
         in_specs=[pl.BlockSpec(memory_space=space) for space in spaces],
-        out_specs=[pl.BlockSpec(memory_space=space) for space in out_spaces],
-        scratch_shapes=[
-            *(pltpu.VMEM(shape, F32) for shape in scratch),
-            *(pltpu.VMEM(array.shape, array.dtype) for array in late),
-            pltpu.SemaphoreType.DMA((len(late) + 3,)),
-        ],
+        out_specs=[pl.BlockSpec(memory_space=pltpu.VMEM)] * len(outs),
+        scratch_shapes=[*(pltpu.VMEM(array.shape, array.dtype) for array in late), pltpu.SemaphoreType.DMA((second + 2,))],
         compiler_params=pltpu.CompilerParams(vmem_limit_bytes=16 * 1024 * 1024),
     )(*(pltpu.with_memory_space_constraint(array, pltpu.HBM) for array in (*far, *late)), *near)
 
@@ -546,29 +548,21 @@
 
     block, layer, extended = (BX, BY, BZ), (YR, BZ), (BX, YR, BZ)
     y_shape, x_shape, half, whole = (3, BX, BZ), (2, YR, BZ), (ELEMS // 2, KCOL), (ELEMS, KCOL)
-    c, ya, yb, ends, near_factor, *sent = call(
+    c, ya, yb, right, diagonal, factor, sent = call(
         part(start_kernel, swapped),
-        [(1, ELEMS), y_shape, y_shape, (2, 2, BY, BZ), whole],
-        far=[factor],
-        late=[right, diagonal],
+        [(1, ELEMS), y_shape, y_shape, block, block, whole, half],
+        far=[right, diagonal, factor],
         near=[slots],
-        far_outs=[half] * swapped,
     )
     ya, yb = pair_swap(ya, yb, "narrow")
-    received = lax.ppermute(sent[0], "narrow", [(0, 1), (1, 0)]) if swapped else factor[ELEMS // 2 :]
+    received = lax.ppermute(sent, "narrow", [(0, 1), (1, 0)]) if swapped else sent
     sums, xa, xb = call(
-        part(project_kernel, swapped), [(count, 1, WIDTH), x_shape, x_shape], near=[c, ya, yb, ends, near_factor]
+        part(project_kernel, swapped), [(count, 1, WIDTH), x_shape, x_shape], near=[c, ya, yb, right, diagonal, factor]
     )
     sums = everywhere(sums)
     xa, xb = pair_swap(xa, xb, "wide")
-    solved, sigma, near_factor = call(
-        first_fine_kernel,
-        [block, (1, ELEMS), whole],
-        far=[factor],
-        late=[right, diagonal, *fine],
-        near=[ya, yb, xa, xb],
-    )
-    ta, tb = call(part(first_coarse_kernel, swapped), [y_shape, y_shape], near=[sums, solved, slots, near_factor])
+    solved, sigma = call(first_fine_kernel, [block, (1, ELEMS)], late=fine, near=[right, diagonal, ya, yb, xa, xb])
+    ta, tb = call(part(first_coarse_kernel, swapped), [y_shape, y_shape], near=[sums, solved, slots, factor])
     ra, rb = pair_swap(ta, tb, "narrow")
     search, sa, sb = call(
         part(extend_kernel, swapped), [extended, (2,) + layer, (2,) + layer], near=[solved, slots, ya, ta, ra, rb]
@@ -577,34 +571,25 @@
     sums, image, halo = call(
         part(operator_kernel, swapped, sizes),
         [(count, 1, WIDTH), (BX + 2, YR, BZ), (3 * BY, BZ)],
-        far=[factor],
-        late=[right, diagonal],
-        near=[search, sa, sb, ya, yb, xa, xb, slots, received],
-        scratch=[half],
+        near=[right, diagonal, factor, received, search, sa, sb, ya, yb, xa, xb, slots],
     )
     sums = everywhere(sums)
-    solved, ya, yb, fa, fb, owned = call(
-        part(second_fine_kernel, swapped),
-        [block, (BX, BZ), (BX, BZ), (BY, BZ), (BY, BZ), whole],
-        far=[factor],
-        late=fine,
-        near=[image, sigma, received],
+    solved, ya, yb, fa, fb = call(
+        second_fine_kernel, [block, (BX, BZ), (BX, BZ), (BY, BZ), (BY, BZ)], late=fine, near=[image, sigma]
     )
     ya, yb = pair_swap(ya, yb, "narrow")
     fa, fb = pair_swap(fa, fb, "wide")
     next_search, next_image, last, products = call(
         part(second_coarse_kernel, swapped),
         [block, block, (count, 1, 2 * ELEMS), (1, 128)],
-        late=[right, diagonal],
-        near=[sums, solved, ya, yb, fa, fb, search, halo, image, slots, owned],
+        near=[right, diagonal, factor, received, sums, solved, ya, yb, fa, fb, search, halo, image, slots],
     )
     last = everywhere(last)
     return tuple(
         call(
             part(last_kernel, sizes),
             [block, block],
-            late=[right],
-            near=[products, last, search, image, next_search, next_image],
+            near=[right, products, last, search, image, next_search, next_image],
             final=True,
         )
     )

time: 92.5 us -> 77.2 us (0.83)
  Pallas kernels: 34.8 us -> 15.2 us
  local copies, waits for them, and re-layouts: 0.77 us -> 4.99 us
    pallas_call x9, Pallas kernels: 34.8 us -> 15.2 us  [call(): pl.pallas_call(run, out_shape=[shape_of(out, F32) for out in outs], in_sp...]
    unnamed x0 -> x18, local copies, waits for them, and re-layouts: none -> 4.22 us
where the time goes in v3:
time: 77.2 us; the launch traced here: 76.7 us
  starting transfers between devices  26.1 us (34%)
  waiting for transfers between devices  16.4 us (21%)
  Pallas kernels  15.2 us (20%)
  blocking collectives  13.2 us (17%)
  local copies, waits for them, and re-layouts  4.99 us (6%)
  between operations  0.79 us (1%)
    all_to_all x2, starting transfers between devices, everywhere(): return lax.all_to_all(rows, AXES, split_axis=0, concat_axis=0, tiled=True)  16.1 us
    pallas_call x9, Pallas kernels, call(): pl.pallas_call(run, out_shape=[shape_of(out, F32) for out in outs], in_sp...  15.2 us
    all_to_all x1, blocking collectives, everywhere(): return lax.all_to_all(rows, AXES, split_axis=0, concat_axis=0, tiled=True)  13.2 us
    ppermute x9, waiting for transfers between devices, pair_swap(): lax.ppermute(value, axis, perm)  10.6 us
    ppermute x9, starting transfers between devices, pair_swap(): lax.ppermute(value, axis, perm)  8.2 us
    all_to_all x2, waiting for transfers between devices, everywhere(): return lax.all_to_all(rows, AXES, split_axis=0, concat_axis=0, tiled=True)  5.78 us
    unnamed x18, local copies, waits for them, and re-layouts  4.22 us
    ppermute x1, starting transfers between devices, body(): lax.ppermute(sent, 'narrow', [(0, 1), (1, 0)])  1.83 us
  transfers between devices with their start and end apart: 12, of which 7 were waited for; matrix products, arithmetic and copies ran while one was open for 0% of the time, Pallas kernels for 11%

profile of v3, /device:TPU:0, one launch (start us, length us, event | category | flops | bytes accessed | tf_op | source)
XLA Modules:
  0.0 76.7 jit_solution(2714006748022679529)
XLA Ops:
  0.6 0.8 reshape.7.refs_3_.refs_2_.refs_1_.refs_11_.refs_13_
  1.4 0.0 copy-start.6
  1.4 2.2 %shard_map.149 = (f32[1,128]{1,0:T(1,128)S(1)}, f32[3,8,512]{2,1,0:T(8,128)S(1)}, f32[3,8,512]{2,1,0:T(8,128)}, f32[8,16,512]{2,1,0:T(8,128)S(1)}, f32[8,16,512]...) custom-call(f32[8,16,512]{2,1,0:T(8,128)} %refs_0_.3, f32[8,16,512]{2,1,0:T(8,128)} %refs_1_.3, ...), custom_call_target="tpu_custom_call" | custom-call | tf_op jit(solution)/shard_map/pallas_call | solution.py:512
  3.6 0.0 copy-start.8
  3.6 3.1 %collective-permute-start.1 = (f32[3,8,512]{2,1,0:T(8,128)S(1)}, f32[3,8,512]{2,1,0:T(8,128)S(1)}, u32[]{:S(2)}, u32[]{:S(2)}) collective-permute-start(f32[3,8,512]{2,1,0:T(8,128)S(1)} %get-tuple-element.32), channel_id=1, source_target_pairs={{0,1},{1,0},{2,3},{3,2},{4,5},{5,4},{6,7},{7,6},{8,9},{9,8},{10,11... | collective-permute-start | bytes 147464 | tf_op jit(solution)/shard_map/ppermute | solution.py:529
  6.7 2.1 %collective-permute-done.1.refs_1_.refs_12_.refs_2_.refs_7_ = f32[3,8,512]{2,1,0:T(8,128)S(1)} collective-permute-done((f32[3,8,512]{2,1,0:T(8,128)S(1)}, f32[3,8,512]{2,1,0:T(8,128)S(1)}, u32[]{:S(2)}, u32[]{:S(2)}) %collective-permute-start.1) | collective-permute-done | bytes 49184 | tf_op jit(solution)/shard_map/ppermute | solution.py:529
  8.8 1.0 %shard_map.150 = (f32[32,1,2176]{2,1,0:T(1,128)}, f32[2,24,512]{2,1,0:T(8,128)S(1)}, f32[2,24,512]{2,1,0:T(8,128)S(1)}) custom-call(f32[1,128]{1,0:T(1,128)S(1)} %get-tuple-element.33.refs_0_, f32[3,8,512]{2,1,0:T(8,128)S(1)} %collective-permute-done.1.refs_1_.refs_12_.refs_2_.refs_7_, ...), custom_call_target="tpu_custom_call" | custom-call | tf_op jit(solution)/shard_map/pallas_call | solution.py:512
  9.8 0.0 copy-done.8
  9.8 6.4 %all-to-all-start = ((f32[32,1,2176]{2,1,0:T(1,128)}), f32[32,1,2176]{2,1,0:T(1,128)S(1)}, u32[]{:S(2)}, u32[]{:S(2)}) async-start(f32[32,1,2176]{2,1,0:T(1,128)} %get-tuple-element.37), calls=%async_computation | async-start | bytes 557056 | tf_op jit(solution)/shard_map/all_to_all | solution.py:534
  16.2 1.8 %collective-permute-start = (f32[64,2048]{1,0:T(8,128)}, f32[64,2048]{1,0:T(8,128)S(1)}, u32[]{:S(2)}, u32[]{:S(2)}) collective-permute-start(f32[64,2048]{1,0:T(8,128)} %copy-done.8), channel_id=1, source_target_pairs={{0,1},{1,0},{2,3},{3,2},{4,5},{5,4},{6,7},{7,6},{8,9},{9,8},{10,11... | collective-permute-start | bytes 1572872 | tf_op jit(solution)/shard_map/ppermute | solution.py:558
  18.0 0.0 collective-permute-start.2
  18.0 0.7 collective-permute-start.3
  18.7 0.6 collective-permute-done.2.refs_14_.refs_9_
  19.3 0.0 collective-permute-done.3.refs_15_.refs_10_
  19.3 3.4 %shard_map.151 = (f32[8,16,512]{2,1,0:T(8,128)S(1)}, f32[1,128]{1,0:T(1,128)S(1)}) custom-call(bf16[208,240]{1,0:T(8,128)(2,1)} %constant.10.clone.refs_0_, bf16[208,240]{1,0:T(8,128)(2,1)} %constant.24.clone.refs_1_, bf16[256,384]{1,0:T(8,128)(2,1)} %constant.25.clone.refs_2_, bf16[256,384]{1,0:T(8,128)(2,1)} %constant.26.clone.refs_3_, ...), custom_call_target="tpu_custom_call" | custom-call | tf_op jit(solution)/shard_map/pallas_call | solution.py:512
  22.7 4.4 %all-to-all-done.refs_0_ = f32[32,1,2176]{2,1,0:T(1,128)S(1)} async-done(((f32[32,1,2176]{2,1,0:T(1,128)}), f32[32,1,2176]{2,1,0:T(1,128)S(1)}, u32[]{:S(2)}, u32[]{:S(2)}) %all-to-all-start) | async-done | bytes 278560 | tf_op jit(solution)/shard_map/all_to_all | solution.py:534
  27.1 0.9 %shard_map.152 = (f32[3,8,512]{2,1,0:T(8,128)S(1)}, f32[3,8,512]{2,1,0:T(8,128)}) custom-call(f32[32,1,2176]{2,1,0:T(1,128)S(1)} %all-to-all-done.refs_0_, f32[8,16,512]{2,1,0:T(8,128)S(1)} %get-tuple-element.36.refs_1_.refs_0_, s32[1,128]{1,0:T(1,128)S(1)} %reshape.7.refs_3_.refs_2_.refs_1_.refs_11_.refs_13_, ...), custom_call_target="tpu_custom_call" | custom-call | tf_op jit(solution)/shard_map/pallas_call | solution.py:512
  28.1 1.0 %collective-permute-start.4 = (f32[3,8,512]{2,1,0:T(8,128)S(1)}, f32[3,8,512]{2,1,0:T(8,128)S(1)}, u32[]{:S(2)}, u32[]{:S(2)}) collective-permute-start(f32[3,8,512]{2,1,0:T(8,128)S(1)} %get-tuple-element.38.refs_3_), channel_id=1, source_target_pairs={{0,1},{1,0},{2,3},{3,2},{4,5},{5,4},{6,7},{7,6},{8,9},{9,8},{10,11... | collective-permute-start | bytes 147464 | tf_op jit(solution)/shard_map/ppermute | solution.py:529
  29.1 5.2 %collective-permute-done.4.refs_4_ = f32[3,8,512]{2,1,0:T(8,128)S(1)} collective-permute-done((f32[3,8,512]{2,1,0:T(8,128)S(1)}, f32[3,8,512]{2,1,0:T(8,128)S(1)}, u32[]{:S(2)}, u32[]{:S(2)}) %collective-permute-start.4) | collective-permute-done | bytes 49184 | tf_op jit(solution)/shard_map/ppermute | solution.py:529
  34.3 0.4 shard_map.153
  34.7 0.1 collective-permute-start.5
  34.8 0.7 collective-permute-start.6
  35.5 0.0 collective-permute-done.refs_3_
  35.5 0.6 collective-permute-done.5.refs_5_
  36.1 0.0 collective-permute-done.6.refs_6_
  36.1 0.0 copy-done.6
  36.1 1.5 %shard_map.154 = (f32[32,1,2176]{2,1,0:T(1,128)}, f32[10,24,512]{2,1,0:T(8,128)S(1)}, f32[48,512]{1,0:T(8,128)S(1)}) custom-call(f32[8,16,512]{2,1,0:T(8,128)S(1)} %get-tuple-element.28.refs_3_.refs_10_.refs_0_, f32[8,16,512]{2,1,0:T(8,128)S(1)} %get-tuple-element.29.refs_4_.refs_11_.refs_1_, f32[128,2048]{1,0:T(8,128)S(1)} %get-tuple-element.30.refs_5_.refs_3_.refs_2_, ...), custom_call_target="tpu_custom_call" | custom-call | tf_op jit(solution)/shard_map/pallas_call | solution.py:512
  37.6 0.0 copy-start
  37.6 0.6 copy-done
  38.3 9.7 %all-to-all-start.1 = ((f32[32,1,2176]{2,1,0:T(1,128)}), f32[32,1,2176]{2,1,0:T(1,128)S(1)}, u32[]{:S(2)}, u32[]{:S(2)}) async-start(f32[32,1,2176]{2,1,0:T(1,128)} %get-tuple-element.42), calls=%async_computation.1 | async-start | bytes 557056 | tf_op jit(solution)/shard_map/all_to_all | solution.py:534
  48.0 3.6 %shard_map.155 = (f32[8,16,512]{2,1,0:T(8,128)S(1)}, f32[8,512]{1,0:T(8,128)S(1)}, f32[8,512]{1,0:T(8,128)}, f32[16,512]{1,0:T(8,128)S(1)}, f32[16,512]{1,0:T(8,128)S(1)}) custom-call(bf16[208,240]{1,0:T(8,128)(2,1)} %constant.10.clone.refs_0_, bf16[208,240]{1,0:T(8,128)(2,1)} %constant.24.clone.refs_1_, bf16[256,384]{1,0:T(8,128)(2,1)} %constant.25.clone.refs_2_, ...), custom_call_target="tpu_custom_call" | custom-call | tf_op jit(solution)/shard_map/pallas_call | solution.py:512
  51.6 0.3 collective-permute-start.8
  51.9 0.7 collective-permute-start.9
  52.5 1.7 %collective-permute-start.7 = (f32[8,512]{1,0:T(8,128)S(1)}, f32[8,512]{1,0:T(8,128)S(1)}, u32[]{:S(2)}, u32[]{:S(2)}) collective-permute-start(f32[8,512]{1,0:T(8,128)S(1)} %get-tuple-element.46), channel_id=1, source_target_pairs={{0,1},{1,0},{2,3},{3,2},{4,5},{5,4},{6,7},{7,6},{8,9},{9,8},{10,11... | collective-permute-start | bytes 49160 | tf_op jit(solution)/shard_map/ppermute | solution.py:529
  54.3 2.1 %collective-permute-done.7.refs_6_ = f32[8,512]{1,0:T(8,128)S(1)} collective-permute-done((f32[8,512]{1,0:T(8,128)S(1)}, f32[8,512]{1,0:T(8,128)S(1)}, u32[]{:S(2)}, u32[]{:S(2)}) %collective-permute-start.7) | collective-permute-done | bytes 16416 | tf_op jit(solution)/shard_map/ppermute | solution.py:529
  56.4 0.0 copy-start.4
  56.4 0.6 copy-done.4
  57.0 0.0 collective-permute-done.8.refs_8_
  57.0 0.0 collective-permute-done.9.refs_9_
  57.0 0.0 copy-start.2
  57.0 0.6 copy-done.2
  57.6 1.4 %all-to-all-done.1.refs_4_ = f32[32,1,2176]{2,1,0:T(1,128)S(1)} async-done(((f32[32,1,2176]{2,1,0:T(1,128)}), f32[32,1,2176]{2,1,0:T(1,128)S(1)}, u32[]{:S(2)}, u32[]{:S(2)}) %all-to-all-start.1) | async-done | bytes 278560 | tf_op jit(solution)/shard_map/all_to_all | solution.py:534
  59.0 0.0 copy-start.5
  59.0 0.0 copy-start.7
  59.0 0.7 copy-done.5
  59.7 0.0 copy-done.7
  59.7 0.0 copy-start.1
  59.7 0.9 %copy-done.1 = f32[48,512]{1,0:T(8,128)S(1)} copy-done((f32[48,512]{1,0:T(8,128)S(1)}, f32[48,512]{1,0:T(8,128)}, u32[]{:S(2)}) %copy-start.1) | copy-done | bytes 98328
  60.6 0.0 copy-start.3
  60.6 0.8 copy-done.3
  61.4 1.0 %shard_map.156 = (f32[8,16,512]{2,1,0:T(8,128)S(1)}, f32[8,16,512]{2,1,0:T(8,128)S(1)}, f32[32,1,256]{2,1,0:T(1,128)S(1)}, f32[1,128]{1,0:T(1,128)S(1)}) custom-call(f32[8,16,512]{2,1,0:T(8,128)S(1)} %get-tuple-element.28.refs_3_.refs_10_.refs_0_, f32[8,16,512]{2,1,0:T(8,128)S(1)} %get-tuple-element.29.refs_4_.refs_11_.refs_1_, ...), custom_call_target="tpu_custom_call" | custom-call | tf_op jit(solution)/shard_map/pallas_call | solution.py:512
  62.4 13.2 %all_to_all.15.refs_2_ = f32[32,1,256]{2,1,0:T(1,128)S(1)} all-to-all(f32[32,1,256]{2,1,0:T(1,128)S(1)} %get-tuple-element.51), channel_id=1, replica_groups=mesh['wide'=16,'narrow'=2] {'wide','narrow'}, dimensions={0} | all-to-all | bytes 65536 | tf_op jit(solution)/shard_map/all_to_all | solution.py:534
  75.6 1.1 %shard_map.157 = (f32[8,16,512]{2,1,0:T(8,128)}, f32[8,16,512]{2,1,0:T(8,128)}) custom-call(f32[8,16,512]{2,1,0:T(8,128)S(1)} %get-tuple-element.28.refs_3_.refs_10_.refs_0_, f32[1,128]{1,0:T(1,128)S(1)} %get-tuple-element.50.refs_1_, f32[32,1,256]{2,1,0:T(1,128)S(1)} %all_to_all.15.refs_2_, f32[8,24,512]{2,1,0:T(8,128)S(1)} %get-tuple-element.39.refs_4_.refs_10_.refs_3_, ...), custom_call_target="tpu_custom_call" | custom-call | tf_op jit(solution)/shard_map/pallas_call | solution.py:512
  (2 shorter events, 0.0 us)
Async XLA Ops:
  1.4 34.7 %copy-start.6 = (s32[1,128]{1,0:T(1,128)}, s32[1,128]{1,0:T(1,128)S(1)}, u32[]{:S(2)}) copy-start(s32[1,128]{1,0:T(1,128)S(1)} %reshape.7.refs_3_.refs_2_.refs_1_.refs_11_.refs_13_) | copy-start | bytes 1540
  3.6 6.1 %copy-start.8 = (f32[64,2048]{1,0:T(8,128)}, f32[64,2048]{1,0:T(8,128)S(1)}, u32[]{:S(2)}) copy-start(f32[64,2048]{1,0:T(8,128)S(1)} %get-tuple-element.31) | copy-start | bytes 1572868
  3.6 5.1 %collective-permute-start.1 = (f32[3,8,512]{2,1,0:T(8,128)S(1)}, f32[3,8,512]{2,1,0:T(8,128)S(1)}, u32[]{:S(2)}, u32[]{:S(2)}) collective-permute-start(f32[3,8,512]{2,1,0:T(8,128)S(1)} %get-tuple-element.32), channel_id=1, source_target_pairs={{0,1},{1,0},{2,3},{3,2},{4,5},{5,4},{6,7},{7,6},{8,9},{9,8},{10,11... | collective-permute-start | bytes 147464 | tf_op jit(solution)/shard_map/ppermute | solution.py:529
  9.8 17.4 %all-to-all-start = ((f32[32,1,2176]{2,1,0:T(1,128)}), f32[32,1,2176]{2,1,0:T(1,128)S(1)}, u32[]{:S(2)}, u32[]{:S(2)}) async-start(f32[32,1,2176]{2,1,0:T(1,128)} %get-tuple-element.37), calls=%async_computation | async-start | bytes 557056 | tf_op jit(solution)/shard_map/all_to_all | solution.py:534
  16.2 19.3 %collective-permute-start = (f32[64,2048]{1,0:T(8,128)}, f32[64,2048]{1,0:T(8,128)S(1)}, u32[]{:S(2)}, u32[]{:S(2)}) collective-permute-start(f32[64,2048]{1,0:T(8,128)} %copy-done.8), channel_id=1, source_target_pairs={{0,1},{1,0},{2,3},{3,2},{4,5},{5,4},{6,7},{7,6},{8,9},{9,8},{10,11... | collective-permute-start | bytes 1572872 | tf_op jit(solution)/shard_map/ppermute | solution.py:558
  18.0 1.3 %collective-permute-start.2 = (f32[2,24,512]{2,1,0:T(8,128)S(1)}, f32[2,24,512]{2,1,0:T(8,128)S(1)}, u32[]{:S(2)}, u32[]{:S(2)}) collective-permute-start(f32[2,24,512]{2,1,0:T(8,128)S(1)} %get-tuple-element.34), channel_id=1, source_target_pairs={{0,2},{2,0},{4,6},{6,4},{8,10},{10,8},{12,14},{14,12},{16,18},{18,... | collective-permute-start | bytes 294920 | tf_op jit(solution)/shard_map/ppermute | solution.py:529
  18.0 1.3 %collective-permute-start.3 = (f32[2,24,512]{2,1,0:T(8,128)S(1)}, f32[2,24,512]{2,1,0:T(8,128)S(1)}, u32[]{:S(2)}, u32[]{:S(2)}) collective-permute-start(f32[2,24,512]{2,1,0:T(8,128)S(1)} %get-tuple-element.35), channel_id=1, source_target_pairs={{2,4},{4,2},{6,8},{8,6},{10,12},{12,10},{14,16},{16,14},{18,20},{2... | collective-permute-start | bytes 294920 | tf_op jit(solution)/shard_map/ppermute | solution.py:529
  28.1 6.2 %collective-permute-start.4 = (f32[3,8,512]{2,1,0:T(8,128)S(1)}, f32[3,8,512]{2,1,0:T(8,128)S(1)}, u32[]{:S(2)}, u32[]{:S(2)}) collective-permute-start(f32[3,8,512]{2,1,0:T(8,128)S(1)} %get-tuple-element.38.refs_3_), channel_id=1, source_target_pairs={{0,1},{1,0},{2,3},{3,2},{4,5},{5,4},{6,7},{7,6},{8,9},{9,8},{10,11... | collective-permute-start | bytes 147464 | tf_op jit(solution)/shard_map/ppermute | solution.py:529
  34.7 1.4 %collective-permute-start.5 = (f32[2,24,512]{2,1,0:T(8,128)S(1)}, f32[2,24,512]{2,1,0:T(8,128)S(1)}, u32[]{:S(2)}, u32[]{:S(2)}) collective-permute-start(f32[2,24,512]{2,1,0:T(8,128)S(1)} %get-tuple-element.40), channel_id=1, source_target_pairs={{0,2},{2,0},{4,6},{6,4},{8,10},{10,8},{12,14},{14,12},{16,18},{18,... | collective-permute-start | bytes 294920 | tf_op jit(solution)/shard_map/ppermute | solution.py:529
  34.8 1.3 %collective-permute-start.6 = (f32[2,24,512]{2,1,0:T(8,128)S(1)}, f32[2,24,512]{2,1,0:T(8,128)S(1)}, u32[]{:S(2)}, u32[]{:S(2)}) collective-permute-start(f32[2,24,512]{2,1,0:T(8,128)S(1)} %get-tuple-element.41), channel_id=1, source_target_pairs={{2,4},{4,2},{6,8},{8,6},{10,12},{12,10},{14,16},{16,14},{18,20},{2... | collective-permute-start | bytes 294920 | tf_op jit(solution)/shard_map/ppermute | solution.py:529
  37.6 0.6 copy-start
  38.3 20.7 %all-to-all-start.1 = ((f32[32,1,2176]{2,1,0:T(1,128)}), f32[32,1,2176]{2,1,0:T(1,128)S(1)}, u32[]{:S(2)}, u32[]{:S(2)}) async-start(f32[32,1,2176]{2,1,0:T(1,128)} %get-tuple-element.42), calls=%async_computation.1 | async-start | bytes 557056 | tf_op jit(solution)/shard_map/all_to_all | solution.py:534
  51.6 5.5 %collective-permute-start.8 = (f32[16,512]{1,0:T(8,128)S(1)}, f32[16,512]{1,0:T(8,128)S(1)}, u32[]{:S(2)}, u32[]{:S(2)}) collective-permute-start(f32[16,512]{1,0:T(8,128)S(1)} %get-tuple-element.47), channel_id=1, source_target_pairs={{0,2},{2,0},{4,6},{6,4},{8,10},{10,8},{12,14},{14,12},{16,18},{18,... | collective-permute-start | bytes 98312 | tf_op jit(solution)/shard_map/ppermute | solution.py:529
  51.9 5.1 %collective-permute-start.9 = (f32[16,512]{1,0:T(8,128)S(1)}, f32[16,512]{1,0:T(8,128)S(1)}, u32[]{:S(2)}, u32[]{:S(2)}) collective-permute-start(f32[16,512]{1,0:T(8,128)S(1)} %get-tuple-element.48), channel_id=1, source_target_pairs={{2,4},{4,2},{6,8},{8,6},{10,12},{12,10},{14,16},{16,14},{18,20},{2... | collective-permute-start | bytes 98312 | tf_op jit(solution)/shard_map/ppermute | solution.py:529
  52.5 3.9 %collective-permute-start.7 = (f32[8,512]{1,0:T(8,128)S(1)}, f32[8,512]{1,0:T(8,128)S(1)}, u32[]{:S(2)}, u32[]{:S(2)}) collective-permute-start(f32[8,512]{1,0:T(8,128)S(1)} %get-tuple-element.46), channel_id=1, source_target_pairs={{0,1},{1,0},{2,3},{3,2},{4,5},{5,4},{6,7},{7,6},{8,9},{9,8},{10,11... | collective-permute-start | bytes 49160 | tf_op jit(solution)/shard_map/ppermute | solution.py:529
  56.4 0.6 copy-start.4
  57.0 0.6 copy-start.2
  59.0 0.7 copy-start.5
  59.0 0.7 copy-start.7
  59.7 0.9 %copy-start.1 = (f32[48,512]{1,0:T(8,128)S(1)}, f32[48,512]{1,0:T(8,128)}, u32[]{:S(2)}) copy-start(f32[48,512]{1,0:T(8,128)} %copy-done) | copy-start | bytes 294916
  60.6 0.8 copy-start.3

commit v4 on v3

--- a/solution.py
+++ b/solution.py
@@ -134,7 +134,7 @@
 
 def slot_mask(slots, offset):
     slot_of_row = lax.rem(iota((ELEMS, ELEMS), 0) + offset, ELEMS)
-    return slot_of_row == slots
+    return slot_of_row.astype(F32) == slots
 
 
 def to_rows(element_values, slots, offset):
@@ -261,31 +261,40 @@
     return jnp.concatenate([tile, jnp.zeros((8, BZ - ELEMS), F32)], axis=1)
 
 
-def start_kernel(swapped, late, right_far, diagonal_far, factor, slots, c, ya, yb, right, diagonal, factor_here, sent):
+def start_kernel(
+    swapped, late, right_far, diagonal_far, factor, slots_far, c, ya, yb, right, diagonal, kept, sent, slots_out
+):
     d = lax.axis_index("narrow")
     half = ELEMS // 2
+    at = pl.multiple_of(d * half, half) if swapped else 0
+    there = pl.multiple_of((1 - d) * half, half) if swapped else half
     right_load = late.start(right_far, right)
     diagonal_load = late.start(diagonal_far, diagonal)
-    late.start(factor.at[pl.ds(pl.multiple_of((1 - d) * half, half), half)] if swapped else factor.at[half:ELEMS], sent)
-    late.start(factor, factor_here)
+    late.start(factor.at[pl.ds(there, half)], sent)
+    late.start(factor.at[pl.ds(at, half)], kept)
+    slots_in = slots_far.here()
+    slots = jnp.concatenate([slots_in[0:1], slots_in[1:2]], axis=1).astype(F32)
+    slots_out[...] = slots
     right_load.wait()
-    row = column_to_row(to_rows(element_row(right[...]) * (1.0 / 16.0), slots[...], 0))
+    row = column_to_row(to_rows(element_row(right[...]) * (1.0 / 16.0), slots, 0))
     c[...] = row
     diagonal_load.wait()
     for i, ref in enumerate((right, diagonal)):
         ya[i], yb[i] = pair_out(d, ref[:, 0, :], ref[:, BY - 1, :])
-    ya[2] = pad_tile([row, slots[...].astype(F32)])
+    ya[2] = pad_tile([row, slots])
     yb[2] = jnp.zeros((8, BZ), F32)
 
 
-def project_kernel(swapped, late, c, ra, rb, right, diagonal, factor, sums, xa, xb):
+def project_kernel(swapped, late, c, ra, rb, right, diagonal, kept, sent, sums, xa, xb):
     w, d = lax.axis_index("wide"), lax.axis_index("narrow")
     row = c[...]
     if swapped:
         half = ELEMS // 2
-        other = pltpu.roll(ra[2, 0:1, 0:ELEMS], half, 1)
-        row = jnp.where(iota((1, ELEMS), 1) // half == d, row, other)
-    store_sum(sums, project(row_to_column(row), (factor,)), jnp.zeros((1, 128), F32))
+        other = ra[2, 0:1, 0:ELEMS]
+        row = jnp.where(d == 0, row, pltpu.roll(row, half, 1))
+        other = jnp.where(d == 0, pltpu.roll(other, half, 1), other)
+        row = jnp.where(iota((1, ELEMS), 1) < half, row, other)
+    store_sum(sums, project(row_to_column(row), (kept, sent)), jnp.zeros((1, 128), F32))
     for i, ref in enumerate((right, diagonal)):
         low, high = pair_in(d, ra[i], rb[i])
         layers = [extend_y(ref[x : x + 1], [low[x : x + 1]], [high[x : x + 1]], 1)[0] for x in (0, BX - 1)]
@@ -307,13 +316,18 @@
     solved[...] = fine_solve(rows.reshape(YW, BZ), sigma, rest[:10])
 
 
-def first_coarse_kernel(swapped, late, sums, solved, slots, factor, ya, yb):
+def first_coarse_kernel(swapped, late, sums, solved, slots, kept, sent, ya, yb):
     d = lax.axis_index("narrow")
     row = jnp.sum(sums[...], axis=0)[:, 0:KCOL]
-    column = correct(row, (factor,))
+    column = correct(row, (kept, sent))
     for i in range(2):
         ya[i], yb[i] = pair_out(d, solved[:, i, :], solved[:, BY - 2 + i, :])
-    ya[2] = pad_tile([column_to_row(column) if swapped else to_elements(column, slots[...], 0)])
+    if swapped:
+        values = column_to_row(column)
+        values = jnp.where(d == 0, values, pltpu.roll(values, ELEMS // 2, 1))
+    else:
+        values = to_elements(column, slots[...], 0)
+    ya[2] = pad_tile([values])
     yb[2] = ya[2]
 
 
@@ -328,7 +342,7 @@
         other = jnp.where(at == d, pltpu.roll(own, half, 1), theirs)
         own = jnp.where(at == d, own, pltpu.roll(theirs, half, 1))
         own = to_elements(row_to_column(own), slots[...], 0)
-        other = to_elements(row_to_column(other), ra_first[2, 1:2, 0:ELEMS].astype(jnp.int32), 0)
+        other = to_elements(row_to_column(other), ra_first[2, 1:2, 0:ELEMS], 0)
         values_low, values_high = other, other
     else:
         values_low, values_high = pair_in(d, theirs, rb[2, 0:1, 0:ELEMS])
@@ -348,19 +362,11 @@
     xa[...], xb[...] = pair_out(w, block[0:2], block[BX - 2 : BX])
 
 
-def owned_rows(swapped, factor, received):
-    half = ELEMS // 2
-    if not swapped:
-        return (factor,), 0
-    at = lax.axis_index("narrow") * half
-    return (factor.at[pl.ds(pl.multiple_of(at, half), half)], received), at
-
-
 def operator_kernel(
-    swapped, sizes, late, right, diagonal, factor, received, search, sa, sb, ya, yb, xa, xb, slots, sums, image_out, halo
+    swapped, sizes, late, right, diagonal, kept, received, search, sa, sb, ya, yb, xa, xb, slots, sums, image_out, halo
 ):
     w, d = lax.axis_index("wide"), lax.axis_index("narrow")
-    owned, offset = owned_rows(swapped, factor, received)
+    owned, offset = (kept, received), d * (ELEMS // 2) if swapped else 0
     s_low, s_high = pair_in(w, sa[...], sb[...])
     vector = jnp.concatenate([s_low, search[...], s_high], axis=0)
     coefficient = widened(diagonal[...], ya, yb, xa, xb, 1)
@@ -393,11 +399,11 @@
 
 
 def second_coarse_kernel(
-    swapped, late, right, diagonal, factor, received, sums, solved, fya, fyb, fxa, fxb, search, halo, image, slots,
+    swapped, late, right, diagonal, kept, received, sums, solved, fya, fyb, fxa, fxb, search, halo, image, slots,
     search_out, image_out, last, products,
 ):
     w, d = lax.axis_index("wide"), lax.axis_index("narrow")
-    owned, offset = owned_rows(swapped, factor, received)
+    owned, offset = (kept, received), d * (ELEMS // 2) if swapped else 0
     row = jnp.sum(sums[...], axis=0)
     products[...] = row[:, KCOL:WIDTH]
     step = lane(row[:, KCOL:WIDTH], 0) / lane(row[:, KCOL:WIDTH], 1)
@@ -514,7 +520,7 @@
         out_shape=[shape_of(out, F32) for out in outs],
         in_specs=[pl.BlockSpec(memory_space=space) for space in spaces],
         out_specs=[pl.BlockSpec(memory_space=pltpu.VMEM)] * len(outs),
-        scratch_shapes=[*(pltpu.VMEM(array.shape, array.dtype) for array in late), pltpu.SemaphoreType.DMA((second + 2,))],
+        scratch_shapes=[*(pltpu.VMEM(array.shape, array.dtype) for array in late), pltpu.SemaphoreType.DMA((second + 4,))],
         compiler_params=pltpu.CompilerParams(vmem_limit_bytes=16 * 1024 * 1024),
     )(*(pltpu.with_memory_space_constraint(array, pltpu.HBM) for array in (*far, *late)), *near)
 
@@ -539,7 +545,7 @@
     groups = sizes[1]
     count = sizes[0] * groups
     fine = [jnp.asarray(c) for c in tables()]
-    slots = coarse_slot.reshape(1, ELEMS)
+    slots = coarse_slot.reshape(EY, EZ)
     swapped = groups == 2
     if not swapped:
         factor = factor.reshape(groups, ELEMS // groups, KCOL)
@@ -547,23 +553,25 @@
     part = functools.partial
 
     block, layer, extended = (BX, BY, BZ), (YR, BZ), (BX, YR, BZ)
-    y_shape, x_shape, half, whole = (3, BX, BZ), (2, YR, BZ), (ELEMS // 2, KCOL), (ELEMS, KCOL)
-    c, ya, yb, right, diagonal, factor, sent = call(
+    y_shape, x_shape, half = (3, BX, BZ), (2, YR, BZ), (ELEMS // 2, KCOL)
+    c, ya, yb, right, diagonal, kept, sent, slots = call(
         part(start_kernel, swapped),
-        [(1, ELEMS), y_shape, y_shape, block, block, whole, half],
+        [(1, ELEMS), y_shape, y_shape, block, block, half, half, (1, ELEMS)],
         far=[right, diagonal, factor],
-        near=[slots],
+        late=[slots],
     )
     ya, yb = pair_swap(ya, yb, "narrow")
-    received = lax.ppermute(sent, "narrow", [(0, 1), (1, 0)]) if swapped else sent
     sums, xa, xb = call(
-        part(project_kernel, swapped), [(count, 1, WIDTH), x_shape, x_shape], near=[c, ya, yb, right, diagonal, factor]
+        part(project_kernel, swapped), [(count, 1, WIDTH), x_shape, x_shape], near=[c, ya, yb, right, diagonal, kept, sent]
     )
     sums = everywhere(sums)
     xa, xb = pair_swap(xa, xb, "wide")
     solved, sigma = call(first_fine_kernel, [block, (1, ELEMS)], late=fine, near=[right, diagonal, ya, yb, xa, xb])
-    ta, tb = call(part(first_coarse_kernel, swapped), [y_shape, y_shape], near=[sums, solved, slots, factor])
+    ta, tb = call(part(first_coarse_kernel, swapped), [y_shape, y_shape], near=[sums, solved, slots, kept, sent])
     ra, rb = pair_swap(ta, tb, "narrow")
+    if swapped:
+        ra, sent = lax.optimization_barrier((ra, sent))
+    received = lax.ppermute(sent, "narrow", [(0, 1), (1, 0)]) if swapped else sent
     search, sa, sb = call(
         part(extend_kernel, swapped), [extended, (2,) + layer, (2,) + layer], near=[solved, slots, ya, ta, ra, rb]
     )
@@ -571,7 +579,7 @@
     sums, image, halo = call(
         part(operator_kernel, swapped, sizes),
         [(count, 1, WIDTH), (BX + 2, YR, BZ), (3 * BY, BZ)],
-        near=[right, diagonal, factor, received, search, sa, sb, ya, yb, xa, xb, slots],
+        near=[right, diagonal, kept, received, search, sa, sb, ya, yb, xa, xb, slots],
     )
     sums = everywhere(sums)
     solved, ya, yb, fa, fb = call(
@@ -582,7 +590,7 @@
     next_search, next_image, last, products = call(
         part(second_coarse_kernel, swapped),
         [block, block, (count, 1, 2 * ELEMS), (1, 128)],
-        near=[right, diagonal, factor, received, sums, solved, ya, yb, fa, fb, search, halo, image, slots],
+        near=[right, diagonal, kept, received, sums, solved, ya, yb, fa, fb, search, halo, image, slots],
     )
     last = everywhere(last)
     return tuple(

time: 77.2 us -> 77.3 us (level)
  waiting for transfers between devices: 16.4 us -> 27.2 us
  local copies, waits for them, and re-layouts: 4.99 us -> 0.01 us
  starting transfers between devices: 26.1 us -> 21.7 us
  blocking collectives: 13.2 us -> 12 us
    ppermute x1, waiting for transfers between devices: 0.01 us -> 10 us  [body(): lax.ppermute(sent, 'narrow', [(0, 1), (1, 0)])]
    unnamed x18 -> x0, local copies, waits for them, and re-layouts: 4.22 us -> none
    all_to_all x2, starting transfers between devices: 16.1 us -> 12.3 us  [everywhere(): return lax.all_to_all(rows, AXES, split_axis=0, concat_axis=0, tiled=True)]
    all_to_all x2, waiting for transfers between devices: 5.78 us -> 8.74 us  [everywhere(): return lax.all_to_all(rows, AXES, split_axis=0, concat_axis=0, tiled=True)]
    ppermute x9, waiting for transfers between devices: 10.6 us -> 8.41 us  [pair_swap(): lax.ppermute(value, axis, perm)]
    all_to_all x1, blocking collectives: 13.2 us -> 12 us  [everywhere(): return lax.all_to_all(rows, AXES, split_axis=0, concat_axis=0, tiled=True)]
    ppermute x1, starting transfers between devices: 1.83 us -> 0.97 us  [body(): lax.ppermute(sent, 'narrow', [(0, 1), (1, 0)])]
  transfers between devices with their start and end apart: 12 -> 12, of which waited for: 7 -> 8; matrix products, arithmetic and copies ran while one was open for 0% -> 0% of each run, Pallas kernels for 11% -> 10%
where the time goes in v4:
time: 77.3 us; the launch traced here: 76.9 us
  waiting for transfers between devices  27.2 us (35%)
  starting transfers between devices  21.7 us (28%)
  Pallas kernels  15.3 us (20%)
  blocking collectives  12 us (16%)
    pallas_call x9, Pallas kernels, call(): pl.pallas_call(run, out_shape=[shape_of(out, F32) for out in outs], in_sp...  15.3 us
    all_to_all x2, starting transfers between devices, everywhere(): return lax.all_to_all(rows, AXES, split_axis=0, concat_axis=0, tiled=True)  12.3 us
    all_to_all x1, blocking collectives, everywhere(): return lax.all_to_all(rows, AXES, split_axis=0, concat_axis=0, tiled=True)  12 us
    ppermute x1, waiting for transfers between devices, body(): lax.ppermute(sent, 'narrow', [(0, 1), (1, 0)])  10 us
    all_to_all x2, waiting for transfers between devices, everywhere(): return lax.all_to_all(rows, AXES, split_axis=0, concat_axis=0, tiled=True)  8.74 us
    ppermute x9, waiting for transfers between devices, pair_swap(): lax.ppermute(value, axis, perm)  8.41 us
    ppermute x9, starting transfers between devices, pair_swap(): lax.ppermute(value, axis, perm)  8.36 us
  transfers between devices with their start and end apart: 12, of which 8 were waited for; matrix products, arithmetic and copies ran while one was open for 0% of the time, Pallas kernels for 10%

profile of v4, /device:TPU:0, one launch (start us, length us, event | category | flops | bytes accessed | tf_op | source)
XLA Modules:
  0.0 76.9 jit_solution(3276156271033550965)
XLA Ops:
  0.6 2.1 %shard_map.149 = (f32[1,128]{1,0:T(1,128)S(1)}, f32[3,8,512]{2,1,0:T(8,128)S(1)}, f32[3,8,512]{2,1,0:T(8,128)}, f32[8,16,512]{2,1,0:T(8,128)S(1)}, f32[8,16,512]...) custom-call(f32[8,16,512]{2,1,0:T(8,128)} %refs_0_.3, ...), custom_call_target="tpu_custom_call" | custom-call | tf_op jit(solution)/shard_map/pallas_call | solution.py:518
  2.7 3.0 %collective-permute-start = (f32[3,8,512]{2,1,0:T(8,128)S(1)}, f32[3,8,512]{2,1,0:T(8,128)S(1)}, u32[]{:S(2)}, u32[]{:S(2)}) collective-permute-start(f32[3,8,512]{2,1,0:T(8,128)S(1)} %get-tuple-element.35), channel_id=1, source_target_pairs={{0,1},{1,0},{2,3},{3,2},{4,5},{5,4},{6,7},{7,6},{8,9},{9,8},{10,11... | collective-permute-start | bytes 147464 | tf_op jit(solution)/shard_map/ppermute | solution.py:535
  5.7 2.1 %collective-permute-done.refs_1_.refs_12_.refs_2_.refs_7_ = f32[3,8,512]{2,1,0:T(8,128)S(1)} collective-permute-done((f32[3,8,512]{2,1,0:T(8,128)S(1)}, f32[3,8,512]{2,1,0:T(8,128)S(1)}, u32[]{:S(2)}, u32[]{:S(2)}) %collective-permute-start) | collective-permute-done | bytes 49184 | tf_op jit(solution)/shard_map/ppermute | solution.py:535
  7.8 1.0 %shard_map.150 = (f32[32,1,2176]{2,1,0:T(1,128)}, f32[2,24,512]{2,1,0:T(8,128)S(1)}, f32[2,24,512]{2,1,0:T(8,128)S(1)}) custom-call(f32[1,128]{1,0:T(1,128)S(1)} %get-tuple-element.34.refs_0_, f32[3,8,512]{2,1,0:T(8,128)S(1)} %collective-permute-done.refs_1_.refs_12_.refs_2_.refs_7_, ...), custom_call_target="tpu_custom_call" | custom-call | tf_op jit(solution)/shard_map/pallas_call | solution.py:518
  8.8 6.4 %all-to-all-start = ((f32[32,1,2176]{2,1,0:T(1,128)}), f32[32,1,2176]{2,1,0:T(1,128)S(1)}, u32[]{:S(2)}, u32[]{:S(2)}) async-start(f32[32,1,2176]{2,1,0:T(1,128)} %get-tuple-element.37), calls=%async_computation | async-start | bytes 557056 | tf_op jit(solution)/shard_map/all_to_all | solution.py:540
  15.2 0.3 collective-permute-start.1
  15.5 0.7 collective-permute-start.2
  16.2 0.4 collective-permute-done.1.refs_14_.refs_9_
  16.6 0.0 collective-permute-done.2.refs_15_.refs_10_
  16.6 3.4 %shard_map.151 = (f32[8,16,512]{2,1,0:T(8,128)S(1)}, f32[1,128]{1,0:T(1,128)S(1)}) custom-call(bf16[208,240]{1,0:T(8,128)(2,1)} %constant.10.clone.refs_0_, bf16[208,240]{1,0:T(8,128)(2,1)} %constant.24.clone.refs_1_, bf16[256,384]{1,0:T(8,128)(2,1)} %constant.25.clone.refs_2_, bf16[256,384]{1,0:T(8,128)(2,1)} %constant.26.clone.refs_3_, ...), custom_call_target="tpu_custom_call" | custom-call | tf_op jit(solution)/shard_map/pallas_call | solution.py:518
  20.0 6.1 %all-to-all-done.refs_0_ = f32[32,1,2176]{2,1,0:T(1,128)S(1)} async-done(((f32[32,1,2176]{2,1,0:T(1,128)}), f32[32,1,2176]{2,1,0:T(1,128)S(1)}, u32[]{:S(2)}, u32[]{:S(2)}) %all-to-all-start) | async-done | bytes 278560 | tf_op jit(solution)/shard_map/all_to_all | solution.py:540
  26.1 1.1 %shard_map.152 = (f32[3,8,512]{2,1,0:T(8,128)S(1)}, f32[3,8,512]{2,1,0:T(8,128)}) custom-call(f32[32,1,2176]{2,1,0:T(1,128)S(1)} %all-to-all-done.refs_0_, f32[8,16,512]{2,1,0:T(8,128)S(1)} %get-tuple-element.40.refs_1_.refs_0_, f32[1,128]{1,0:T(1,128)S(1)} %get-tuple-element.41.refs_2_.refs_1_.refs_11_.refs_13_, ...), custom_call_target="tpu_custom_call" | custom-call | tf_op jit(solution)/shard_map/pallas_call | solution.py:518
  27.3 0.9 %collective-permute-start.3 = (f32[3,8,512]{2,1,0:T(8,128)S(1)}, f32[3,8,512]{2,1,0:T(8,128)S(1)}, u32[]{:S(2)}, u32[]{:S(2)}) collective-permute-start(f32[3,8,512]{2,1,0:T(8,128)S(1)} %get-tuple-element.42.refs_3_), channel_id=1, source_target_pairs={{0,1},{1,0},{2,3},{3,2},{4,5},{5,4},{6,7},{7,6},{8,9},{9,8},{10,11... | collective-permute-start | bytes 147464 | tf_op jit(solution)/shard_map/ppermute | solution.py:535
  28.2 3.2 %collective-permute-done.3.refs_4_ = f32[3,8,512]{2,1,0:T(8,128)S(1)} collective-permute-done((f32[3,8,512]{2,1,0:T(8,128)S(1)}, f32[3,8,512]{2,1,0:T(8,128)S(1)}, u32[]{:S(2)}, u32[]{:S(2)}) %collective-permute-start.3) | collective-permute-done | bytes 49184 | tf_op jit(solution)/shard_map/ppermute | solution.py:535
  31.4 1.0 %collective-permute-start.4 = (f32[64,2048]{1,0:T(8,128)S(1)}, f32[64,2048]{1,0:T(8,128)S(1)}, u32[]{:S(2)}, u32[]{:S(2)}) collective-permute-start(f32[64,2048]{1,0:T(8,128)S(1)} %get-tuple-element.43.refs_6_.refs_4_), channel_id=1, source_target_pairs={{0,1},{1,0},{2,3},{3,2},{4,5},{5,4},{6,7},{7,6},{8,9},{9,8},{10,11... | collective-permute-start | bytes 1572872 | tf_op jit(solution)/shard_map/ppermute | solution.py:574
  32.4 0.5 shard_map.153
  32.9 0.1 collective-permute-start.5
  32.9 0.7 collective-permute-start.6
  33.6 0.6 collective-permute-done.5.refs_5_
  34.2 0.0 collective-permute-done.6.refs_6_
  34.2 10.0 %collective-permute-done.4.refs_3_ = f32[64,2048]{1,0:T(8,128)S(1)} collective-permute-done((f32[64,2048]{1,0:T(8,128)S(1)}, f32[64,2048]{1,0:T(8,128)S(1)}, u32[]{:S(2)}, u32[]{:S(2)}) %collective-permute-start.4) | collective-permute-done | bytes 524320 | tf_op jit(solution)/shard_map/ppermute | solution.py:574
  44.3 1.5 %shard_map.154 = (f32[32,1,2176]{2,1,0:T(1,128)}, f32[10,24,512]{2,1,0:T(8,128)S(1)}, f32[48,512]{1,0:T(8,128)S(1)}) custom-call(f32[8,16,512]{2,1,0:T(8,128)S(1)} %get-tuple-element.31.refs_3_.refs_10_.refs_0_, f32[8,16,512]{2,1,0:T(8,128)S(1)} %get-tuple-element.32.refs_4_.refs_11_.refs_1_, f32[64,2048]{1,0:T(8,128)S(1)} %get-tuple-element.33.refs_5_.refs_3_.refs_2_, ...), custom_call_target="tpu_custom_call" | custom-call | tf_op jit(solution)/shard_map/pallas_call | solution.py:518
  45.8 5.9 %all-to-all-start.1 = ((f32[32,1,2176]{2,1,0:T(1,128)}), f32[32,1,2176]{2,1,0:T(1,128)S(1)}, u32[]{:S(2)}, u32[]{:S(2)}) async-start(f32[32,1,2176]{2,1,0:T(1,128)} %get-tuple-element.48), calls=%async_computation.1 | async-start | bytes 557056 | tf_op jit(solution)/shard_map/all_to_all | solution.py:540
  51.7 3.6 %shard_map.155 = (f32[8,16,512]{2,1,0:T(8,128)S(1)}, f32[8,512]{1,0:T(8,128)S(1)}, f32[8,512]{1,0:T(8,128)}, f32[16,512]{1,0:T(8,128)S(1)}, f32[16,512]{1,0:T(8,128)S(1)}) custom-call(bf16[208,240]{1,0:T(8,128)(2,1)} %constant.10.clone.refs_0_, bf16[208,240]{1,0:T(8,128)(2,1)} %constant.24.clone.refs_1_, bf16[256,384]{1,0:T(8,128)(2,1)} %constant.25.clone.refs_2_, ...), custom_call_target="tpu_custom_call" | custom-call | tf_op jit(solution)/shard_map/pallas_call | solution.py:518
  55.4 0.3 collective-permute-start.8
  55.7 0.7 collective-permute-start.9
  56.3 1.7 %collective-permute-start.7 = (f32[8,512]{1,0:T(8,128)S(1)}, f32[8,512]{1,0:T(8,128)S(1)}, u32[]{:S(2)}, u32[]{:S(2)}) collective-permute-start(f32[8,512]{1,0:T(8,128)S(1)} %get-tuple-element.52), channel_id=1, source_target_pairs={{0,1},{1,0},{2,3},{3,2},{4,5},{5,4},{6,7},{7,6},{8,9},{9,8},{10,11... | collective-permute-start | bytes 49160 | tf_op jit(solution)/shard_map/ppermute | solution.py:535
  58.1 2.1 %collective-permute-done.7.refs_6_ = f32[8,512]{1,0:T(8,128)S(1)} collective-permute-done((f32[8,512]{1,0:T(8,128)S(1)}, f32[8,512]{1,0:T(8,128)S(1)}, u32[]{:S(2)}, u32[]{:S(2)}) %collective-permute-start.7) | collective-permute-done | bytes 16416 | tf_op jit(solution)/shard_map/ppermute | solution.py:535
  60.2 0.0 collective-permute-done.8.refs_8_
  60.2 0.0 collective-permute-done.9.refs_9_
  60.2 2.6 %all-to-all-done.1.refs_4_ = f32[32,1,2176]{2,1,0:T(1,128)S(1)} async-done(((f32[32,1,2176]{2,1,0:T(1,128)}), f32[32,1,2176]{2,1,0:T(1,128)S(1)}, u32[]{:S(2)}, u32[]{:S(2)}) %all-to-all-start.1) | async-done | bytes 278560 | tf_op jit(solution)/shard_map/all_to_all | solution.py:540
  62.8 1.0 %shard_map.156 = (f32[8,16,512]{2,1,0:T(8,128)S(1)}, f32[8,16,512]{2,1,0:T(8,128)S(1)}, f32[32,1,256]{2,1,0:T(1,128)S(1)}, f32[1,128]{1,0:T(1,128)S(1)}) custom-call(f32[8,16,512]{2,1,0:T(8,128)S(1)} %get-tuple-element.31.refs_3_.refs_10_.refs_0_, f32[8,16,512]{2,1,0:T(8,128)S(1)} %get-tuple-element.32.refs_4_.refs_11_.refs_1_, ...), custom_call_target="tpu_custom_call" | custom-call | tf_op jit(solution)/shard_map/pallas_call | solution.py:518
  63.8 12.0 %all_to_all.15.refs_2_ = f32[32,1,256]{2,1,0:T(1,128)S(1)} all-to-all(f32[32,1,256]{2,1,0:T(1,128)S(1)} %get-tuple-element.57), channel_id=1, replica_groups=mesh['wide'=16,'narrow'=2] {'wide','narrow'}, dimensions={0} | all-to-all | bytes 65536 | tf_op jit(solution)/shard_map/all_to_all | solution.py:540
  75.8 1.1 %shard_map.157 = (f32[8,16,512]{2,1,0:T(8,128)}, f32[8,16,512]{2,1,0:T(8,128)}) custom-call(f32[8,16,512]{2,1,0:T(8,128)S(1)} %get-tuple-element.31.refs_3_.refs_10_.refs_0_, f32[1,128]{1,0:T(1,128)S(1)} %get-tuple-element.56.refs_1_, f32[32,1,256]{2,1,0:T(1,128)S(1)} %all_to_all.15.refs_2_, f32[8,24,512]{2,1,0:T(8,128)S(1)} %get-tuple-element.45.refs_4_.refs_10_.refs_3_, ...), custom_call_target="tpu_custom_call" | custom-call | tf_op jit(solution)/shard_map/pallas_call | solution.py:518
  (2 shorter events, 0.0 us)
Async XLA Ops:
  2.7 5.1 %collective-permute-start = (f32[3,8,512]{2,1,0:T(8,128)S(1)}, f32[3,8,512]{2,1,0:T(8,128)S(1)}, u32[]{:S(2)}, u32[]{:S(2)}) collective-permute-start(f32[3,8,512]{2,1,0:T(8,128)S(1)} %get-tuple-element.35), channel_id=1, source_target_pairs={{0,1},{1,0},{2,3},{3,2},{4,5},{5,4},{6,7},{7,6},{8,9},{9,8},{10,11... | collective-permute-start | bytes 147464 | tf_op jit(solution)/shard_map/ppermute | solution.py:535
  8.8 17.3 %all-to-all-start = ((f32[32,1,2176]{2,1,0:T(1,128)}), f32[32,1,2176]{2,1,0:T(1,128)S(1)}, u32[]{:S(2)}, u32[]{:S(2)}) async-start(f32[32,1,2176]{2,1,0:T(1,128)} %get-tuple-element.37), calls=%async_computation | async-start | bytes 557056 | tf_op jit(solution)/shard_map/all_to_all | solution.py:540
  15.2 1.4 %collective-permute-start.1 = (f32[2,24,512]{2,1,0:T(8,128)S(1)}, f32[2,24,512]{2,1,0:T(8,128)S(1)}, u32[]{:S(2)}, u32[]{:S(2)}) collective-permute-start(f32[2,24,512]{2,1,0:T(8,128)S(1)} %get-tuple-element.38), channel_id=1, source_target_pairs={{0,2},{2,0},{4,6},{6,4},{8,10},{10,8},{12,14},{14,12},{16,18},{18,... | collective-permute-start | bytes 294920 | tf_op jit(solution)/shard_map/ppermute | solution.py:535
  15.5 1.1 %collective-permute-start.2 = (f32[2,24,512]{2,1,0:T(8,128)S(1)}, f32[2,24,512]{2,1,0:T(8,128)S(1)}, u32[]{:S(2)}, u32[]{:S(2)}) collective-permute-start(f32[2,24,512]{2,1,0:T(8,128)S(1)} %get-tuple-element.39), channel_id=1, source_target_pairs={{2,4},{4,2},{6,8},{8,6},{10,12},{12,10},{14,16},{16,14},{18,20},{2... | collective-permute-start | bytes 294920 | tf_op jit(solution)/shard_map/ppermute | solution.py:535
  27.3 4.2 %collective-permute-start.3 = (f32[3,8,512]{2,1,0:T(8,128)S(1)}, f32[3,8,512]{2,1,0:T(8,128)S(1)}, u32[]{:S(2)}, u32[]{:S(2)}) collective-permute-start(f32[3,8,512]{2,1,0:T(8,128)S(1)} %get-tuple-element.42.refs_3_), channel_id=1, source_target_pairs={{0,1},{1,0},{2,3},{3,2},{4,5},{5,4},{6,7},{7,6},{8,9},{9,8},{10,11... | collective-permute-start | bytes 147464 | tf_op jit(solution)/shard_map/ppermute | solution.py:535
  31.4 12.8 %collective-permute-start.4 = (f32[64,2048]{1,0:T(8,128)S(1)}, f32[64,2048]{1,0:T(8,128)S(1)}, u32[]{:S(2)}, u32[]{:S(2)}) collective-permute-start(f32[64,2048]{1,0:T(8,128)S(1)} %get-tuple-element.43.refs_6_.refs_4_), channel_id=1, source_target_pairs={{0,1},{1,0},{2,3},{3,2},{4,5},{5,4},{6,7},{7,6},{8,9},{9,8},{10,11... | collective-permute-start | bytes 1572872 | tf_op jit(solution)/shard_map/ppermute | solution.py:574
  32.9 1.4 %collective-permute-start.5 = (f32[2,24,512]{2,1,0:T(8,128)S(1)}, f32[2,24,512]{2,1,0:T(8,128)S(1)}, u32[]{:S(2)}, u32[]{:S(2)}) collective-permute-start(f32[2,24,512]{2,1,0:T(8,128)S(1)} %get-tuple-element.46), channel_id=1, source_target_pairs={{0,2},{2,0},{4,6},{6,4},{8,10},{10,8},{12,14},{14,12},{16,18},{18,... | collective-permute-start | bytes 294920 | tf_op jit(solution)/shard_map/ppermute | solution.py:535
  32.9 1.3 %collective-permute-start.6 = (f32[2,24,512]{2,1,0:T(8,128)S(1)}, f32[2,24,512]{2,1,0:T(8,128)S(1)}, u32[]{:S(2)}, u32[]{:S(2)}) collective-permute-start(f32[2,24,512]{2,1,0:T(8,128)S(1)} %get-tuple-element.47), channel_id=1, source_target_pairs={{2,4},{4,2},{6,8},{8,6},{10,12},{12,10},{14,16},{16,14},{18,20},{2... | collective-permute-start | bytes 294920 | tf_op jit(solution)/shard_map/ppermute | solution.py:535
  45.8 17.0 %all-to-all-start.1 = ((f32[32,1,2176]{2,1,0:T(1,128)}), f32[32,1,2176]{2,1,0:T(1,128)S(1)}, u32[]{:S(2)}, u32[]{:S(2)}) async-start(f32[32,1,2176]{2,1,0:T(1,128)} %get-tuple-element.48), calls=%async_computation.1 | async-start | bytes 557056 | tf_op jit(solution)/shard_map/all_to_all | solution.py:540
  55.4 4.8 %collective-permute-start.8 = (f32[16,512]{1,0:T(8,128)S(1)}, f32[16,512]{1,0:T(8,128)S(1)}, u32[]{:S(2)}, u32[]{:S(2)}) collective-permute-start(f32[16,512]{1,0:T(8,128)S(1)} %get-tuple-element.53), channel_id=1, source_target_pairs={{0,2},{2,0},{4,6},{6,4},{8,10},{10,8},{12,14},{14,12},{16,18},{18,... | collective-permute-start | bytes 98312 | tf_op jit(solution)/shard_map/ppermute | solution.py:535
  55.7 4.5 %collective-permute-start.9 = (f32[16,512]{1,0:T(8,128)S(1)}, f32[16,512]{1,0:T(8,128)S(1)}, u32[]{:S(2)}, u32[]{:S(2)}) collective-permute-start(f32[16,512]{1,0:T(8,128)S(1)} %get-tuple-element.54), channel_id=1, source_target_pairs={{2,4},{4,2},{6,8},{8,6},{10,12},{12,10},{14,16},{16,14},{18,20},{2... | collective-permute-start | bytes 98312 | tf_op jit(solution)/shard_map/ppermute | solution.py:535
  56.3 3.9 %collective-permute-start.7 = (f32[8,512]{1,0:T(8,128)S(1)}, f32[8,512]{1,0:T(8,128)S(1)}, u32[]{:S(2)}, u32[]{:S(2)}) collective-permute-start(f32[8,512]{1,0:T(8,128)S(1)} %get-tuple-element.52), channel_id=1, source_target_pairs={{0,1},{1,0},{2,3},{3,2},{4,5},{5,4},{6,7},{7,6},{8,9},{9,8},{10,11... | collective-permute-start | bytes 49160 | tf_op jit(solution)/shard_map/ppermute | solution.py:535

commit v5 on v4

--- a/solution.py
+++ b/solution.py
@@ -18,6 +18,8 @@
 AB = 208
 HZ = 256
 HW = 384
+STAGED = 4
+TABLES = 10
 KCOL = 2048
 WIDTH = KCOL + 128
 AXES = ("wide", "narrow")
@@ -220,8 +222,8 @@
 
 def fine_solve(rows, sigma, tables):
     wh, wl, th, tl, vh, vl, uh, ul, column, beyond = tables
-    spectra = dot3((wh.here()[...], wl.here()[...]), split2(rows))
-    th, tl, column, beyond, vh, vl, uh, ul = [table.here()[...] for table in (th, tl, column, beyond, vh, vl, uh, ul)]
+    spectra = dot3((value(wh), value(wl)), split2(rows))
+    th, tl, vh, vl, uh, ul, column, beyond = [value(table) for table in (th, tl, vh, vl, uh, ul, column, beyond)]
     nodal = []
     for half in range(2):
         part = spectra[:, half * HZ : (half + 1) * HZ]
@@ -234,6 +236,10 @@
     return jnp.concatenate(nodal, axis=2)
 
 
+def value(table):
+    return (table.here() if isinstance(table, Loaded) else table)[...]
+
+
 def repeat_lanes(row, group):
     only = jnp.where(iota((1, ELEMS), 1) // 32 == group, row, 0.0)
     only = only + pltpu.roll(only, 64, 1)
@@ -262,16 +268,11 @@
 
 
 def start_kernel(
-    swapped, late, right_far, diagonal_far, factor, slots_far, c, ya, yb, right, diagonal, kept, sent, slots_out
+    late, right_far, diagonal_far, slots_far, c, ya, yb, right, diagonal, slots_out
 ):
     d = lax.axis_index("narrow")
-    half = ELEMS // 2
-    at = pl.multiple_of(d * half, half) if swapped else 0
-    there = pl.multiple_of((1 - d) * half, half) if swapped else half
     right_load = late.start(right_far, right)
     diagonal_load = late.start(diagonal_far, diagonal)
-    late.start(factor.at[pl.ds(there, half)], sent)
-    late.start(factor.at[pl.ds(at, half)], kept)
     slots_in = slots_far.here()
     slots = jnp.concatenate([slots_in[0:1], slots_in[1:2]], axis=1).astype(F32)
     slots_out[...] = slots
@@ -283,6 +284,19 @@
         ya[i], yb[i] = pair_out(d, ref[:, 0, :], ref[:, BY - 1, :])
     ya[2] = pad_tile([row, slots])
     yb[2] = jnp.zeros((8, BZ), F32)
+
+
+def stage_kernel(swapped, late, factor, *refs):
+    d = lax.axis_index("narrow")
+    half = ELEMS // 2
+    at = pl.multiple_of(d * half, half) if swapped else 0
+    there = pl.multiple_of((1 - d) * half, half) if swapped else half
+    after, sent, kept, done = refs[STAGED : STAGED + 4]
+    late.start(factor.at[pl.ds(at, half)], kept)
+    late.start(factor.at[pl.ds(there, half)], sent)
+    for source, target in zip(refs[:STAGED], refs[STAGED + 4 :]):
+        late.start(source, target)
+    done[...] = after[...]
 
 
 def project_kernel(swapped, late, c, ra, rb, right, diagonal, kept, sent, sums, xa, xb):
@@ -309,11 +323,12 @@
 
 
 def first_fine_kernel(late, *rest):
-    right, diagonal, ya, yb, xa, xb, solved, sigma_out = rest[10:]
+    right, diagonal, ya, yb, xa, xb, solved, sigma_out = rest[TABLES:]
     rows = widened(right[...], ya, yb, xa, xb, 0)
     sigma = element_row(diagonal[...]) * (1.0 / 512.0)
     sigma_out[...] = sigma
-    solved[...] = fine_solve(rows.reshape(YW, BZ), sigma, rest[:10])
+    tables = rest[TABLES - STAGED : TABLES] + rest[: TABLES - STAGED]
+    solved[...] = fine_solve(rows.reshape(YW, BZ), sigma, tables)
 
 
 def first_coarse_kernel(swapped, late, sums, solved, slots, kept, sent, ya, yb):
@@ -391,8 +406,8 @@
 
 def second_fine_kernel(late, *rest):
     w, d = lax.axis_index("wide"), lax.axis_index("narrow")
-    image, sigma, solved, ya, yb, xa, xb = rest[10:]
-    out = fine_solve(image[...].reshape(YW, BZ), sigma[...], rest[:10])
+    image, sigma, solved, ya, yb, xa, xb = rest[TABLES:]
+    out = fine_solve(image[...].reshape(YW, BZ), sigma[...], rest[:TABLES])
     solved[...] = out
     ya[...], yb[...] = pair_out(d, solved[:, 0, :], solved[:, BY - 1, :])
     xa[...], xb[...] = pair_out(w, out[0], out[BX - 1])
@@ -421,10 +436,10 @@
     beside = roll_sum(extend_y(vector, [y_low], [y_high], 1))[:, 0:BY]
     beside = beside + jnp.concatenate([x_low[None], vector[0 : BX - 1]], axis=0)
     beside = beside + jnp.concatenate([vector[1:BX], x_high[None]], axis=0)
-    next_image = (6.0 + diagonal[...]) * vector - beside
+    next_image = (6.0 + diagonal.here()[...]) * vector - beside
     search_out[...] = vector
     image_out[...] = next_image
-    residual = right[...] - step * own_image
+    residual = right.here()[...] - step * own_image
     edges = total(coarse * (x_low + x_high)) + total(y_low * coarse[0:1]) + total(y_high * coarse[BY - 1 : BY])
     store_sum(
         last,
@@ -471,7 +486,7 @@
     direction = next_search[...] + ratio * own_search
     total_image = next_image[...] + step * missing + ratio * own_image
     x_out[...] = step * own_search + step_next * direction
-    r_out[...] = (right[...] - step * own_image) - step_next * total_image
+    r_out[...] = (right.here()[...] - step * own_image) - step_next * total_image
 
 
 class Loaded:
@@ -517,10 +532,10 @@
     spaces = [pltpu.HBM] * second + [pltpu.VMEM] * len(near)
     return pl.pallas_call(
         run,
-        out_shape=[shape_of(out, F32) for out in outs],
+        out_shape=[shape_of(getattr(out, "shape", out), getattr(out, "dtype", F32)) for out in outs],
         in_specs=[pl.BlockSpec(memory_space=space) for space in spaces],
         out_specs=[pl.BlockSpec(memory_space=pltpu.VMEM)] * len(outs),
-        scratch_shapes=[*(pltpu.VMEM(array.shape, array.dtype) for array in late), pltpu.SemaphoreType.DMA((second + 4,))],
+        scratch_shapes=[*(pltpu.VMEM(array.shape, array.dtype) for array in late), pltpu.SemaphoreType.DMA((second + 2,))],
         compiler_params=pltpu.CompilerParams(vmem_limit_bytes=16 * 1024 * 1024),
     )(*(pltpu.with_memory_space_constraint(array, pltpu.HBM) for array in (*far, *late)), *near)
 
@@ -554,26 +569,27 @@
 
     block, layer, extended = (BX, BY, BZ), (YR, BZ), (BX, YR, BZ)
     y_shape, x_shape, half = (3, BX, BZ), (2, YR, BZ), (ELEMS // 2, KCOL)
-    c, ya, yb, right, diagonal, kept, sent, slots = call(
-        part(start_kernel, swapped),
-        [(1, ELEMS), y_shape, y_shape, block, block, half, half, (1, ELEMS)],
-        far=[right, diagonal, factor],
-        late=[slots],
+    right_far, diagonal_far = right, diagonal
+    c, ya, yb, right, diagonal, slots = call(
+        start_kernel, [(1, ELEMS), y_shape, y_shape, block, block, (1, ELEMS)], far=[right, diagonal], late=[slots]
     )
     ya, yb = pair_swap(ya, yb, "narrow")
+    sent, kept, c, *near = call(
+        part(stage_kernel, swapped), [half, half, (1, ELEMS), *fine[:STAGED]], far=[factor, *fine[:STAGED]], near=[c]
+    )
     sums, xa, xb = call(
         part(project_kernel, swapped), [(count, 1, WIDTH), x_shape, x_shape], near=[c, ya, yb, right, diagonal, kept, sent]
     )
     sums = everywhere(sums)
     xa, xb = pair_swap(xa, xb, "wide")
-    solved, sigma = call(first_fine_kernel, [block, (1, ELEMS)], late=fine, near=[right, diagonal, ya, yb, xa, xb])
+    solved, sigma = call(first_fine_kernel, [block, (1, ELEMS)], late=fine[STAGED:], near=[*near, right, diagonal, ya, yb, xa, xb])
     ta, tb = call(part(first_coarse_kernel, swapped), [y_shape, y_shape], near=[sums, solved, slots, kept, sent])
     ra, rb = pair_swap(ta, tb, "narrow")
-    if swapped:
-        ra, sent = lax.optimization_barrier((ra, sent))
     received = lax.ppermute(sent, "narrow", [(0, 1), (1, 0)]) if swapped else sent
     search, sa, sb = call(
-        part(extend_kernel, swapped), [extended, (2,) + layer, (2,) + layer], near=[solved, slots, ya, ta, ra, rb]
+        part(extend_kernel, swapped),
+        [extended, (2,) + layer, (2,) + layer],
+        near=[solved, slots, ya, ta, ra, rb],
     )
     sa, sb = pair_swap(sa, sb, "wide")
     sums, image, halo = call(
@@ -590,14 +606,16 @@
     next_search, next_image, last, products = call(
         part(second_coarse_kernel, swapped),
         [block, block, (count, 1, 2 * ELEMS), (1, 128)],
-        near=[right, diagonal, kept, received, sums, solved, ya, yb, fa, fb, search, halo, image, slots],
+        late=[right_far, diagonal_far],
+        near=[kept, received, sums, solved, ya, yb, fa, fb, search, halo, image, slots],
     )
     last = everywhere(last)
     return tuple(
         call(
             part(last_kernel, sizes),
             [block, block],
-            near=[right, products, last, search, image, next_search, next_image],
+            late=[right_far],
+            near=[products, last, search, image, next_search, next_image],
             final=True,
         )
     )

time: 77.3 us -> 73.3 us (0.948)
  waiting for transfers between devices: 27.2 us -> 16 us
  starting transfers between devices: 21.7 us -> 26.2 us
  Pallas kernels: 15.3 us -> 17.8 us
    ppermute x1, waiting for transfers between devices: 10 us -> 0.01 us  [body(): lax.ppermute(sent, 'narrow', [(0, 1), (1, 0)])]
    all_to_all x2, starting transfers between devices: 12.3 us -> 16.2 us  [everywhere(): return lax.all_to_all(rows, AXES, split_axis=0, concat_axis=0, tiled=True)]
    pallas_call x9 -> x10, Pallas kernels: 15.3 us -> 17.8 us  [call(): pl.pallas_call(run, out_shape=[shape_of(getattr(out, 'shape', out), getat...]
    all_to_all x2, waiting for transfers between devices: 8.74 us -> 7.04 us  [everywhere(): return lax.all_to_all(rows, AXES, split_axis=0, concat_axis=0, tiled=True)]
    ppermute x1, starting transfers between devices: 0.97 us -> 1.83 us  [body(): lax.ppermute(sent, 'narrow', [(0, 1), (1, 0)])]
  transfers between devices with their start and end apart: 12 -> 12, of which waited for: 8 -> 7; matrix products, arithmetic and copies ran while one was open for 0% -> 0% of each run, Pallas kernels for 10% -> 14%
where the time goes in v5:
time: 73.3 us; the launch traced here: 72.8 us
  starting transfers between devices  26.2 us (36%)
  Pallas kernels  17.8 us (24%)
  waiting for transfers between devices  16 us (22%)
  blocking collectives  12 us (16%)
  between operations  0.77 us (1%)
    pallas_call x10, Pallas kernels, call(): pl.pallas_call(run, out_shape=[shape_of(getattr(out, 'shape', out), getat...  17.8 us
    all_to_all x2, starting transfers between devices, everywhere(): return lax.all_to_all(rows, AXES, split_axis=0, concat_axis=0, tiled=True)  16.2 us
    all_to_all x1, blocking collectives, everywhere(): return lax.all_to_all(rows, AXES, split_axis=0, concat_axis=0, tiled=True)  12 us
    ppermute x9, waiting for transfers between devices, pair_swap(): lax.ppermute(value, axis, perm)  9 us
    ppermute x9, starting transfers between devices, pair_swap(): lax.ppermute(value, axis, perm)  8.14 us
    all_to_all x2, waiting for transfers between devices, everywhere(): return lax.all_to_all(rows, AXES, split_axis=0, concat_axis=0, tiled=True)  7.04 us
    ppermute x1, starting transfers between devices, body(): lax.ppermute(sent, 'narrow', [(0, 1), (1, 0)])  1.83 us
  transfers between devices with their start and end apart: 12, of which 7 were waited for; matrix products, arithmetic and copies ran while one was open for 0% of the time, Pallas kernels for 14%

profile of v5, /device:TPU:0, one launch (start us, length us, event | category | flops | bytes accessed | tf_op | source)
XLA Modules:
  0.0 72.8 jit_solution(18121353430305028935)
XLA Ops:
  0.6 2.0 %shard_map.149 = (f32[1,128]{1,0:T(1,128)S(1)}, f32[3,8,512]{2,1,0:T(8,128)S(1)}, f32[3,8,512]{2,1,0:T(8,128)}, f32[8,16,512]{2,1,0:T(8,128)S(1)}, f32[8,16,512]{2,1,0:T(8,128)S(1)}, /*index=5*/f32[1,128]{1,0:T(1,128)S(1)}) custom-call(f32[8,16,512]{2,1,0:T(8,128)} %refs_0_.9, f32[8,16,512]{2,1,0:T(8,128)} %refs_1_.6, s32[2,64]{1,0:T(2,128)} %bitcast.1), custom_call_target="tpu_custom_call" | custom-call | tf_op jit(solution)/shard_map/pallas_call | solution.py:533
  2.6 3.0 %collective-permute-start.1 = (f32[3,8,512]{2,1,0:T(8,128)S(1)}, f32[3,8,512]{2,1,0:T(8,128)S(1)}, u32[]{:S(2)}, u32[]{:S(2)}) collective-permute-start(f32[3,8,512]{2,1,0:T(8,128)S(1)} %get-tuple-element.43), channel_id=1, source_target_pairs={{0,1},{1,0},{2,3},{3,2},{4,5},{5,4},{6,7},{7,6},{8,9},{9,8},{10,11... | collective-permute-start | bytes 147464 | tf_op jit(solution)/shard_map/ppermute | solution.py:550
  5.6 1.5 %shard_map.150 = (f32[64,2048]{1,0:T(8,128)S(1)}, f32[64,2048]{1,0:T(8,128)S(1)}, f32[1,128]{1,0:T(1,128)S(1)}, bf16[208,240]{1,0:T(8,128)(2,1)S(1)}, bf16[208,2...) custom-call(f32[128,2048]{1,0:T(8,128)} %refs_0_.7, ...), custom_call_target="tpu_custom_call" | custom-call | tf_op jit(solution)/shard_map/pallas_call | solution.py:533
  7.1 0.6 collective-permute-done.1.refs_1_.refs_12_.refs_2_.refs_7_
  7.7 1.0 %shard_map.151 = (f32[32,1,2176]{2,1,0:T(1,128)}, f32[2,24,512]{2,1,0:T(8,128)S(1)}, f32[2,24,512]{2,1,0:T(8,128)S(1)}) custom-call(f32[1,128]{1,0:T(1,128)S(1)} %get-tuple-element.44.refs_0_, f32[3,8,512]{2,1,0:T(8,128)S(1)} %collective-permute-done.1.refs_1_.refs_12_.refs_2_.refs_7_, ...), custom_call_target="tpu_custom_call" | custom-call | tf_op jit(solution)/shard_map/pallas_call | solution.py:533
  8.7 6.4 %all-to-all-start = ((f32[32,1,2176]{2,1,0:T(1,128)}), f32[32,1,2176]{2,1,0:T(1,128)S(1)}, u32[]{:S(2)}, u32[]{:S(2)}) async-start(f32[32,1,2176]{2,1,0:T(1,128)} %get-tuple-element.49), calls=%async_computation | async-start | bytes 557056 | tf_op jit(solution)/shard_map/all_to_all | solution.py:555
  15.1 1.8 %collective-permute-start = (f32[64,2048]{1,0:T(8,128)S(1)}, f32[64,2048]{1,0:T(8,128)S(1)}, u32[]{:S(2)}, u32[]{:S(2)}) collective-permute-start(f32[64,2048]{1,0:T(8,128)S(1)} %get-tuple-element.36.refs_6_.refs_4_), channel_id=1, source_target_pairs={{0,1},{1,0},{2,3},{3,2},{4,5},{5,4},{6,7},{7,6},{8,9},{9,8},{10,11... | collective-permute-start | bytes 1572872 | tf_op jit(solution)/shard_map/ppermute | solution.py:588
  16.9 0.0 collective-permute-start.2
  16.9 0.7 collective-permute-start.3
  17.6 0.6 collective-permute-done.2.refs_14_.refs_9_
  18.2 0.0 collective-permute-done.3.refs_15_.refs_10_
  18.2 3.4 %shard_map.152 = (f32[8,16,512]{2,1,0:T(8,128)S(1)}, f32[1,128]{1,0:T(1,128)S(1)}) custom-call(bf16[128,208]{1,0:T(8,128)(2,1)} %constant.27.clone.refs_0_.refs_4_, bf16[128,208]{1,0:T(8,128)(2,1)} %constant.28.clone.refs_1_.refs_5_, bf16[384,256]{1,0:T(8,128)(2,1)} %constant.29.clone.refs_2_.refs_6_, bf16[384,256]{1,0:T(8,128)(2,1)} %constant.30.clone.refs_3_.refs_7_, ...), custom_call_target="tpu_custom_call" | custom-call | tf_op jit(solution)/shard_map/pallas_call | solution.py:533
  21.6 4.4 %all-to-all-done.refs_0_ = f32[32,1,2176]{2,1,0:T(1,128)S(1)} async-done(((f32[32,1,2176]{2,1,0:T(1,128)}), f32[32,1,2176]{2,1,0:T(1,128)S(1)}, u32[]{:S(2)}, u32[]{:S(2)}) %all-to-all-start) | async-done | bytes 278560 | tf_op jit(solution)/shard_map/all_to_all | solution.py:555
  26.0 1.1 %shard_map.153 = (f32[3,8,512]{2,1,0:T(8,128)S(1)}, f32[3,8,512]{2,1,0:T(8,128)}) custom-call(f32[32,1,2176]{2,1,0:T(1,128)S(1)} %all-to-all-done.refs_0_, f32[8,16,512]{2,1,0:T(8,128)S(1)} %get-tuple-element.47.refs_1_.refs_0_, f32[1,128]{1,0:T(1,128)S(1)} %get-tuple-element.48.refs_2_.refs_1_.refs_11_.refs_13_, ...), custom_call_target="tpu_custom_call" | custom-call | tf_op jit(solution)/shard_map/pallas_call | solution.py:533
  27.1 1.0 %collective-permute-start.4 = (f32[3,8,512]{2,1,0:T(8,128)S(1)}, f32[3,8,512]{2,1,0:T(8,128)S(1)}, u32[]{:S(2)}, u32[]{:S(2)}) collective-permute-start(f32[3,8,512]{2,1,0:T(8,128)S(1)} %get-tuple-element.50.refs_3_), channel_id=1, source_target_pairs={{0,1},{1,0},{2,3},{3,2},{4,5},{5,4},{6,7},{7,6},{8,9},{9,8},{10,11... | collective-permute-start | bytes 147464 | tf_op jit(solution)/shard_map/ppermute | solution.py:550
  28.2 5.0 %collective-permute-done.4.refs_4_ = f32[3,8,512]{2,1,0:T(8,128)S(1)} collective-permute-done((f32[3,8,512]{2,1,0:T(8,128)S(1)}, f32[3,8,512]{2,1,0:T(8,128)S(1)}, u32[]{:S(2)}, u32[]{:S(2)}) %collective-permute-start.4) | collective-permute-done | bytes 49184 | tf_op jit(solution)/shard_map/ppermute | solution.py:550
  33.2 0.4 shard_map.154
  33.6 0.1 collective-permute-start.5
  33.7 0.7 collective-permute-start.6
  34.4 0.0 collective-permute-done.refs_3_
  34.4 0.6 collective-permute-done.5.refs_5_
  35.0 0.0 collective-permute-done.6.refs_6_
  35.0 1.5 %shard_map.155 = (f32[32,1,2176]{2,1,0:T(1,128)}, f32[10,24,512]{2,1,0:T(8,128)S(1)}, f32[48,512]{1,0:T(8,128)S(1)}) custom-call(f32[8,16,512]{2,1,0:T(8,128)S(1)} %get-tuple-element.37.refs_3_.refs_10_.refs_0_, f32[8,16,512]{2,1,0:T(8,128)S(1)} %get-tuple-element.38.refs_4_.refs_11_.refs_1_, f32[64,2048]{1,0:T(8,128)S(1)} %get-tuple-element.35.refs_5_.refs_3_.refs_2_, ...), custom_call_target="tpu_custom_call" | custom-call | tf_op jit(solution)/shard_map/pallas_call | solution.py:533
  36.5 9.8 %all-to-all-start.1 = ((f32[32,1,2176]{2,1,0:T(1,128)}), f32[32,1,2176]{2,1,0:T(1,128)S(1)}, u32[]{:S(2)}, u32[]{:S(2)}) async-start(f32[32,1,2176]{2,1,0:T(1,128)} %get-tuple-element.54), calls=%async_computation.1 | async-start | bytes 557056 | tf_op jit(solution)/shard_map/all_to_all | solution.py:555
  46.4 3.6 %shard_map.156 = (f32[8,16,512]{2,1,0:T(8,128)S(1)}, f32[8,512]{1,0:T(8,128)S(1)}, f32[8,512]{1,0:T(8,128)}, f32[16,512]{1,0:T(8,128)S(1)}, f32[16,512]{1,0:T(8,128)S(1)}) custom-call(bf16[208,240]{1,0:T(8,128)(2,1)} %constant.10.clone.refs_1_.refs_0_, bf16[208,240]{1,0:T(8,128)(2,1)} %constant.24.clone.refs_2_.refs_1_, ...), custom_call_target="tpu_custom_call" | custom-call | tf_op jit(solution)/shard_map/pallas_call | solution.py:533
  49.9 0.3 collective-permute-start.8
  50.3 0.7 collective-permute-start.9
  50.9 1.7 %collective-permute-start.7 = (f32[8,512]{1,0:T(8,128)S(1)}, f32[8,512]{1,0:T(8,128)S(1)}, u32[]{:S(2)}, u32[]{:S(2)}) collective-permute-start(f32[8,512]{1,0:T(8,128)S(1)} %get-tuple-element.58), channel_id=1, source_target_pairs={{0,1},{1,0},{2,3},{3,2},{4,5},{5,4},{6,7},{7,6},{8,9},{9,8},{10,11... | collective-permute-start | bytes 49160 | tf_op jit(solution)/shard_map/ppermute | solution.py:550
  52.7 2.1 %collective-permute-done.7.refs_6_ = f32[8,512]{1,0:T(8,128)S(1)} collective-permute-done((f32[8,512]{1,0:T(8,128)S(1)}, f32[8,512]{1,0:T(8,128)S(1)}, u32[]{:S(2)}, u32[]{:S(2)}) %collective-permute-start.7) | collective-permute-done | bytes 16416 | tf_op jit(solution)/shard_map/ppermute | solution.py:550
  54.8 0.0 collective-permute-done.8.refs_8_
  54.8 0.0 collective-permute-done.9.refs_9_
  54.8 2.6 %all-to-all-done.1.refs_4_ = f32[32,1,2176]{2,1,0:T(1,128)S(1)} async-done(((f32[32,1,2176]{2,1,0:T(1,128)}), f32[32,1,2176]{2,1,0:T(1,128)S(1)}, u32[]{:S(2)}, u32[]{:S(2)}) %all-to-all-start.1) | async-done | bytes 278560 | tf_op jit(solution)/shard_map/all_to_all | solution.py:555
  57.4 1.6 %shard_map.157 = (f32[8,16,512]{2,1,0:T(8,128)S(1)}, f32[8,16,512]{2,1,0:T(8,128)S(1)}, f32[32,1,256]{2,1,0:T(1,128)S(1)}, f32[1,128]{1,0:T(1,128)S(1)}) custom-call(f32[8,16,512]{2,1,0:T(8,128)} %refs_0_.9, f32[8,16,512]{2,1,0:T(8,128)} %refs_1_.6, f32[64,2048]{1,0:T(8,128)S(1)} %get-tuple-element.35.refs_5_.refs_3_.refs_2_, ...), custom_call_target="tpu_custom_call" | custom-call | tf_op jit(solution)/shard_map/pallas_call | solution.py:533
  59.0 12.0 %all_to_all.15.refs_2_ = f32[32,1,256]{2,1,0:T(1,128)S(1)} all-to-all(f32[32,1,256]{2,1,0:T(1,128)S(1)} %get-tuple-element.63), channel_id=1, replica_groups=mesh['wide'=16,'narrow'=2] {'wide','narrow'}, dimensions={0} | all-to-all | bytes 65536 | tf_op jit(solution)/shard_map/all_to_all | solution.py:555
  71.0 1.8 %shard_map.158 = (f32[8,16,512]{2,1,0:T(8,128)}, f32[8,16,512]{2,1,0:T(8,128)}) custom-call(f32[8,16,512]{2,1,0:T(8,128)} %refs_0_.9, f32[1,128]{1,0:T(1,128)S(1)} %get-tuple-element.62.refs_1_, f32[32,1,256]{2,1,0:T(1,128)S(1)} %all_to_all.15.refs_2_, f32[8,24,512]{2,1,0:T(8,128)S(1)} %get-tuple-element.51.refs_4_.refs_10_.refs_3_, ...), custom_call_target="tpu_custom_call" | custom-call | tf_op jit(solution)/shard_map/pallas_call | solution.py:533
  (2 shorter events, 0.0 us)
Async XLA Ops:
  2.6 5.1 %collective-permute-start.1 = (f32[3,8,512]{2,1,0:T(8,128)S(1)}, f32[3,8,512]{2,1,0:T(8,128)S(1)}, u32[]{:S(2)}, u32[]{:S(2)}) collective-permute-start(f32[3,8,512]{2,1,0:T(8,128)S(1)} %get-tuple-element.43), channel_id=1, source_target_pairs={{0,1},{1,0},{2,3},{3,2},{4,5},{5,4},{6,7},{7,6},{8,9},{9,8},{10,11... | collective-permute-start | bytes 147464 | tf_op jit(solution)/shard_map/ppermute | solution.py:550
  8.7 17.4 %all-to-all-start = ((f32[32,1,2176]{2,1,0:T(1,128)}), f32[32,1,2176]{2,1,0:T(1,128)S(1)}, u32[]{:S(2)}, u32[]{:S(2)}) async-start(f32[32,1,2176]{2,1,0:T(1,128)} %get-tuple-element.49), calls=%async_computation | async-start | bytes 557056 | tf_op jit(solution)/shard_map/all_to_all | solution.py:555
  15.1 19.3 %collective-permute-start = (f32[64,2048]{1,0:T(8,128)S(1)}, f32[64,2048]{1,0:T(8,128)S(1)}, u32[]{:S(2)}, u32[]{:S(2)}) collective-permute-start(f32[64,2048]{1,0:T(8,128)S(1)} %get-tuple-element.36.refs_6_.refs_4_), channel_id=1, source_target_pairs={{0,1},{1,0},{2,3},{3,2},{4,5},{5,4},{6,7},{7,6},{8,9},{9,8},{10,11... | collective-permute-start | bytes 1572872 | tf_op jit(solution)/shard_map/ppermute | solution.py:588
  16.9 1.3 %collective-permute-start.2 = (f32[2,24,512]{2,1,0:T(8,128)S(1)}, f32[2,24,512]{2,1,0:T(8,128)S(1)}, u32[]{:S(2)}, u32[]{:S(2)}) collective-permute-start(f32[2,24,512]{2,1,0:T(8,128)S(1)} %get-tuple-element.45), channel_id=1, source_target_pairs={{0,2},{2,0},{4,6},{6,4},{8,10},{10,8},{12,14},{14,12},{16,18},{18,... | collective-permute-start | bytes 294920 | tf_op jit(solution)/shard_map/ppermute | solution.py:550
  16.9 1.3 %collective-permute-start.3 = (f32[2,24,512]{2,1,0:T(8,128)S(1)}, f32[2,24,512]{2,1,0:T(8,128)S(1)}, u32[]{:S(2)}, u32[]{:S(2)}) collective-permute-start(f32[2,24,512]{2,1,0:T(8,128)S(1)} %get-tuple-element.46), channel_id=1, source_target_pairs={{2,4},{4,2},{6,8},{8,6},{10,12},{12,10},{14,16},{16,14},{18,20},{2... | collective-permute-start | bytes 294920 | tf_op jit(solution)/shard_map/ppermute | solution.py:550
  27.1 6.1 %collective-permute-start.4 = (f32[3,8,512]{2,1,0:T(8,128)S(1)}, f32[3,8,512]{2,1,0:T(8,128)S(1)}, u32[]{:S(2)}, u32[]{:S(2)}) collective-permute-start(f32[3,8,512]{2,1,0:T(8,128)S(1)} %get-tuple-element.50.refs_3_), channel_id=1, source_target_pairs={{0,1},{1,0},{2,3},{3,2},{4,5},{5,4},{6,7},{7,6},{8,9},{9,8},{10,11... | collective-permute-start | bytes 147464 | tf_op jit(solution)/shard_map/ppermute | solution.py:550
  33.6 1.4 %collective-permute-start.5 = (f32[2,24,512]{2,1,0:T(8,128)S(1)}, f32[2,24,512]{2,1,0:T(8,128)S(1)}, u32[]{:S(2)}, u32[]{:S(2)}) collective-permute-start(f32[2,24,512]{2,1,0:T(8,128)S(1)} %get-tuple-element.52), channel_id=1, source_target_pairs={{0,2},{2,0},{4,6},{6,4},{8,10},{10,8},{12,14},{14,12},{16,18},{18,... | collective-permute-start | bytes 294920 | tf_op jit(solution)/shard_map/ppermute | solution.py:550
  33.7 1.3 %collective-permute-start.6 = (f32[2,24,512]{2,1,0:T(8,128)S(1)}, f32[2,24,512]{2,1,0:T(8,128)S(1)}, u32[]{:S(2)}, u32[]{:S(2)}) collective-permute-start(f32[2,24,512]{2,1,0:T(8,128)S(1)} %get-tuple-element.53), channel_id=1, source_target_pairs={{2,4},{4,2},{6,8},{8,6},{10,12},{12,10},{14,16},{16,14},{18,20},{2... | collective-permute-start | bytes 294920 | tf_op jit(solution)/shard_map/ppermute | solution.py:550
  36.5 20.9 %all-to-all-start.1 = ((f32[32,1,2176]{2,1,0:T(1,128)}), f32[32,1,2176]{2,1,0:T(1,128)S(1)}, u32[]{:S(2)}, u32[]{:S(2)}) async-start(f32[32,1,2176]{2,1,0:T(1,128)} %get-tuple-element.54), calls=%async_computation.1 | async-start | bytes 557056 | tf_op jit(solution)/shard_map/all_to_all | solution.py:555
  49.9 4.8 %collective-permute-start.8 = (f32[16,512]{1,0:T(8,128)S(1)}, f32[16,512]{1,0:T(8,128)S(1)}, u32[]{:S(2)}, u32[]{:S(2)}) collective-permute-start(f32[16,512]{1,0:T(8,128)S(1)} %get-tuple-element.59), channel_id=1, source_target_pairs={{0,2},{2,0},{4,6},{6,4},{8,10},{10,8},{12,14},{14,12},{16,18},{18,... | collective-permute-start | bytes 98312 | tf_op jit(solution)/shard_map/ppermute | solution.py:550
  50.3 4.5 %collective-permute-start.9 = (f32[16,512]{1,0:T(8,128)S(1)}, f32[16,512]{1,0:T(8,128)S(1)}, u32[]{:S(2)}, u32[]{:S(2)}) collective-permute-start(f32[16,512]{1,0:T(8,128)S(1)} %get-tuple-element.60), channel_id=1, source_target_pairs={{2,4},{4,2},{6,8},{8,6},{10,12},{12,10},{14,16},{16,14},{18,20},{2... | collective-permute-start | bytes 98312 | tf_op jit(solution)/shard_map/ppermute | solution.py:550
  50.9 3.9 %collective-permute-start.7 = (f32[8,512]{1,0:T(8,128)S(1)}, f32[8,512]{1,0:T(8,128)S(1)}, u32[]{:S(2)}, u32[]{:S(2)}) collective-permute-start(f32[8,512]{1,0:T(8,128)S(1)} %get-tuple-element.58), channel_id=1, source_target_pairs={{0,1},{1,0},{2,3},{3,2},{4,5},{5,4},{6,7},{7,6},{8,9},{9,8},{10,11... | collective-permute-start | bytes 49160 | tf_op jit(solution)/shard_map/ppermute | solution.py:550

commit v6 on v5

--- a/solution.py
+++ b/solution.py
@@ -18,7 +18,7 @@
 AB = 208
 HZ = 256
 HW = 384
-STAGED = 4
+STAGED = 3
 TABLES = 10
 KCOL = 2048
 WIDTH = KCOL + 128
@@ -113,9 +113,9 @@
     return jnp.where(at // 8 == element, 1.0, 0.0).astype(BF16)
 
 
-def element_row(field):
+def element_row(field, table):
     parts = jnp.concatenate(split3(jnp.sum(field, axis=0)), axis=0)
-    sums = dot(parts, gather_table())
+    sums = dot(parts, table)
     sums = sums[0:16] + sums[16:32] + sums[32:48]
     return jnp.sum(sums[0:8, 0:ELEMS], axis=0, keepdims=True) + jnp.sum(sums[8:16, ELEMS:], axis=0, keepdims=True)
 
@@ -268,7 +268,7 @@
 
 
 def start_kernel(
-    late, right_far, diagonal_far, slots_far, c, ya, yb, right, diagonal, slots_out
+    late, right_far, diagonal_far, slots_far, c, ya, yb, right, diagonal, slots_out, table_out
 ):
     d = lax.axis_index("narrow")
     right_load = late.start(right_far, right)
@@ -276,8 +276,10 @@
     slots_in = slots_far.here()
     slots = jnp.concatenate([slots_in[0:1], slots_in[1:2]], axis=1).astype(F32)
     slots_out[...] = slots
+    table = gather_table()
+    table_out[...] = table
     right_load.wait()
-    row = column_to_row(to_rows(element_row(right[...]) * (1.0 / 16.0), slots, 0))
+    row = column_to_row(to_rows(element_row(right[...], table) * (1.0 / 16.0), slots, 0))
     c[...] = row
     diagonal_load.wait()
     for i, ref in enumerate((right, diagonal)):
@@ -291,12 +293,13 @@
     half = ELEMS // 2
     at = pl.multiple_of(d * half, half) if swapped else 0
     there = pl.multiple_of((1 - d) * half, half) if swapped else half
-    after, sent, kept, done = refs[STAGED : STAGED + 4]
+    after, diagonal, table, sent, kept, done, sigma = refs[STAGED : STAGED + 7]
     late.start(factor.at[pl.ds(at, half)], kept)
     late.start(factor.at[pl.ds(there, half)], sent)
-    for source, target in zip(refs[:STAGED], refs[STAGED + 4 :]):
+    for source, target in zip(refs[:STAGED], refs[STAGED + 7 :]):
         late.start(source, target)
     done[...] = after[...]
+    sigma[...] = element_row(diagonal[...], table[...]) * (1.0 / 512.0)
 
 
 def project_kernel(swapped, late, c, ra, rb, right, diagonal, kept, sent, sums, xa, xb):
@@ -323,12 +326,10 @@
 
 
 def first_fine_kernel(late, *rest):
-    right, diagonal, ya, yb, xa, xb, solved, sigma_out = rest[TABLES:]
+    right, ya, yb, xa, xb, sigma, solved = rest[TABLES:]
     rows = widened(right[...], ya, yb, xa, xb, 0)
-    sigma = element_row(diagonal[...]) * (1.0 / 512.0)
-    sigma_out[...] = sigma
     tables = rest[TABLES - STAGED : TABLES] + rest[: TABLES - STAGED]
-    solved[...] = fine_solve(rows.reshape(YW, BZ), sigma, tables)
+    solved[...] = fine_solve(rows.reshape(YW, BZ), sigma[...], tables)
 
 
 def first_coarse_kernel(swapped, late, sums, solved, slots, kept, sent, ya, yb):
@@ -377,30 +378,41 @@
     xa[...], xb[...] = pair_out(w, block[0:2], block[BX - 2 : BX])
 
 
+def interior_kernel(late, right, diagonal, search, ya, yb, image, product, table):
+    d = lax.axis_index("narrow")
+    low, high = pair_in(d, ya[1], yb[1])
+    centre = search[...]
+    part = (6.0 + extend_y(diagonal[...], [low], [high], 1)) * centre - roll_sum(centre)
+    zero = jnp.zeros((1, YR, BZ), F32)
+    part = part - jnp.concatenate([zero, centre[0 : BX - 1]], axis=0) - jnp.concatenate([centre[1:BX], zero], axis=0)
+    image[...] = part
+    product[...] = lanes([total(right[...] * centre[:, 0:BY])])
+    table[...] = gather_table()
+
+
 def operator_kernel(
-    swapped, sizes, late, right, diagonal, kept, received, search, sa, sb, ya, yb, xa, xb, slots, sums, image_out, halo
+    swapped, sizes, late, kept, received, search, inner, product, table, sa, sb, xa, xb, slots, sums, image_out, halo
 ):
     w, d = lax.axis_index("wide"), lax.axis_index("narrow")
     owned, offset = (kept, received), d * (ELEMS // 2) if swapped else 0
     s_low, s_high = pair_in(w, sa[...], sb[...])
-    vector = jnp.concatenate([s_low, search[...], s_high], axis=0)
-    coefficient = widened(diagonal[...], ya, yb, xa, xb, 1)
-    centre = vector[1 : BX + 3]
-    image = (6.0 + coefficient) * centre - (vector[0 : BX + 2] + vector[2 : BX + 4] + roll_sum(centre))
-    x = iota(image.shape, 0)
-    y = iota(image.shape, 1)
+    d_low, d_high = pair_in(w, xa[1], xb[1])
+    low = (6.0 + d_low) * s_low[1] - s_low[0] - search[0] - roll_sum(s_low[1:2])[0]
+    high = (6.0 + d_high) * s_high[0] - s_high[1] - search[BX - 1] - roll_sum(s_high[0:1])[0]
+    y = iota((YR, BZ), 0)
     inside = (y < BY) | ((y == BY) & (d < sizes[1] - 1)) | ((y == YR - 1) & (d > 0))
-    inside &= ((x > 0) | (w > 0)) & ((x < BX + 1) | (w < sizes[0] - 1))
-    image = jnp.where(inside, image, 0.0)
-    image_out[...] = image
+    image_out[0] = jnp.where(inside & (w > 0), low, 0.0)
+    image_out[1] = jnp.where(inside, inner[0] - s_low[1], 0.0)
+    image_out[2:BX] = jnp.where(inside[None], inner[1 : BX - 1], 0.0)
+    image_out[BX] = jnp.where(inside, inner[BX - 1] - s_high[0], 0.0)
+    image_out[BX + 1] = jnp.where(inside & (w < sizes[0] - 1), high, 0.0)
     halo[0:BY] = s_low[1, 0:BY]
     halo[BY : 2 * BY] = s_high[0, 0:BY]
     halo[2 * BY : 2 * BY + 8] = search[:, YR - 1, :]
     halo[2 * BY + 8 : 3 * BY] = search[:, BY, :]
-    own = image[1 : BX + 1, 0:BY]
-    own_search = search[:, 0:BY, :]
-    column = to_rows(element_row(own) * (1.0 / 16.0), slots[...], offset)
-    extra = lanes([total(right[...] * own_search), total(own_search * own)])
+    own = image_out[1 : BX + 1, 0:BY, :]
+    column = to_rows(element_row(own, table[...]) * (1.0 / 16.0), slots[...], offset)
+    extra = lanes([lane(product[...], 0), total(search[:, 0:BY, :] * own)])
     store_sum(sums, project(column, owned), extra)
 
 
@@ -436,10 +448,10 @@
     beside = roll_sum(extend_y(vector, [y_low], [y_high], 1))[:, 0:BY]
     beside = beside + jnp.concatenate([x_low[None], vector[0 : BX - 1]], axis=0)
     beside = beside + jnp.concatenate([vector[1:BX], x_high[None]], axis=0)
-    next_image = (6.0 + diagonal.here()[...]) * vector - beside
+    next_image = (6.0 + diagonal[...]) * vector - beside
     search_out[...] = vector
     image_out[...] = next_image
-    residual = right.here()[...] - step * own_image
+    residual = right[...] - step * own_image
     edges = total(coarse * (x_low + x_high)) + total(y_low * coarse[0:1]) + total(y_high * coarse[BY - 1 : BY])
     store_sum(
         last,
@@ -486,7 +498,7 @@
     direction = next_search[...] + ratio * own_search
     total_image = next_image[...] + step * missing + ratio * own_image
     x_out[...] = step * own_search + step_next * direction
-    r_out[...] = (right.here()[...] - step * own_image) - step_next * total_image
+    r_out[...] = (right[...] - step * own_image) - step_next * total_image
 
 
 class Loaded:
@@ -569,20 +581,26 @@
 
     block, layer, extended = (BX, BY, BZ), (YR, BZ), (BX, YR, BZ)
     y_shape, x_shape, half = (3, BX, BZ), (2, YR, BZ), (ELEMS // 2, KCOL)
-    right_far, diagonal_far = right, diagonal
-    c, ya, yb, right, diagonal, slots = call(
-        start_kernel, [(1, ELEMS), y_shape, y_shape, block, block, (1, ELEMS)], far=[right, diagonal], late=[slots]
+    gather = jax.ShapeDtypeStruct((BZ, EY * ELEMS), BF16)
+    c, ya, yb, right, diagonal, slots, table = call(
+        start_kernel,
+        [(1, ELEMS), y_shape, y_shape, block, block, (1, ELEMS), gather],
+        far=[right, diagonal],
+        late=[slots],
     )
     ya, yb = pair_swap(ya, yb, "narrow")
-    sent, kept, c, *near = call(
-        part(stage_kernel, swapped), [half, half, (1, ELEMS), *fine[:STAGED]], far=[factor, *fine[:STAGED]], near=[c]
+    sent, kept, c, sigma, *near = call(
+        part(stage_kernel, swapped),
+        [half, half, (1, ELEMS), (1, ELEMS), *fine[:STAGED]],
+        far=[factor, *fine[:STAGED]],
+        near=[c, diagonal, table],
     )
     sums, xa, xb = call(
         part(project_kernel, swapped), [(count, 1, WIDTH), x_shape, x_shape], near=[c, ya, yb, right, diagonal, kept, sent]
     )
     sums = everywhere(sums)
     xa, xb = pair_swap(xa, xb, "wide")
-    solved, sigma = call(first_fine_kernel, [block, (1, ELEMS)], late=fine[STAGED:], near=[*near, right, diagonal, ya, yb, xa, xb])
+    (solved,) = call(first_fine_kernel, [block], late=fine[STAGED:], near=[*near, right, ya, yb, xa, xb, sigma])
     ta, tb = call(part(first_coarse_kernel, swapped), [y_shape, y_shape], near=[sums, solved, slots, kept, sent])
     ra, rb = pair_swap(ta, tb, "narrow")
     received = lax.ppermute(sent, "narrow", [(0, 1), (1, 0)]) if swapped else sent
@@ -592,10 +610,13 @@
         near=[solved, slots, ya, ta, ra, rb],
     )
     sa, sb = pair_swap(sa, sb, "wide")
+    inner, product, table = call(
+        interior_kernel, [extended, (1, 128), gather], near=[right, diagonal, search, ya, yb]
+    )
     sums, image, halo = call(
         part(operator_kernel, swapped, sizes),
         [(count, 1, WIDTH), (BX + 2, YR, BZ), (3 * BY, BZ)],
-        near=[right, diagonal, kept, received, search, sa, sb, ya, yb, xa, xb, slots],
+        near=[kept, received, search, inner, product, table, sa, sb, xa, xb, slots],
     )
     sums = everywhere(sums)
     solved, ya, yb, fa, fb = call(
@@ -606,16 +627,14 @@
     next_search, next_image, last, products = call(
         part(second_coarse_kernel, swapped),
         [block, block, (count, 1, 2 * ELEMS), (1, 128)],
-        late=[right_far, diagonal_far],
-        near=[kept, received, sums, solved, ya, yb, fa, fb, search, halo, image, slots],
+        near=[right, diagonal, kept, received, sums, solved, ya, yb, fa, fb, search, halo, image, slots],
     )
     last = everywhere(last)
     return tuple(
         call(
             part(last_kernel, sizes),
             [block, block],
-            late=[right_far],
-            near=[products, last, search, image, next_search, next_image],
+            near=[right, products, last, search, image, next_search, next_image],
             final=True,
         )
     )

time: 73.3 us -> 71.1 us (0.970)
  Pallas kernels: 17.8 us -> 16.1 us
    pallas_call x10 -> x11, Pallas kernels: 17.8 us -> 16.1 us  [call(): pl.pallas_call(run, out_shape=[shape_of(getattr(out, 'shape', out), getat...]
where the time goes in v6:
time: 71.1 us; the launch traced here: 70.7 us
  starting transfers between devices  25.8 us (36%)
  Pallas kernels  16.1 us (23%)
  waiting for transfers between devices  16 us (23%)
  blocking collectives  12 us (17%)
  between operations  0.77 us (1%)
    pallas_call x11, Pallas kernels, call(): pl.pallas_call(run, out_shape=[shape_of(getattr(out, 'shape', out), getat...  16.1 us
    all_to_all x2, starting transfers between devices, everywhere(): return lax.all_to_all(rows, AXES, split_axis=0, concat_axis=0, tiled=True)  15.8 us
    all_to_all x1, blocking collectives, everywhere(): return lax.all_to_all(rows, AXES, split_axis=0, concat_axis=0, tiled=True)  12 us
    ppermute x9, waiting for transfers between devices, pair_swap(): lax.ppermute(value, axis, perm)  8.48 us
    ppermute x9, starting transfers between devices, pair_swap(): lax.ppermute(value, axis, perm)  8.15 us
    all_to_all x2, waiting for transfers between devices, everywhere(): return lax.all_to_all(rows, AXES, split_axis=0, concat_axis=0, tiled=True)  7.5 us
    ppermute x1, starting transfers between devices, body(): lax.ppermute(sent, 'narrow', [(0, 1), (1, 0)])  1.83 us
  transfers between devices with their start and end apart: 12, of which 7 were waited for; matrix products, arithmetic and copies ran while one was open for 0% of the time, Pallas kernels for 14%

profile of v6, /device:TPU:0, one launch (start us, length us, event | category | flops | bytes accessed | tf_op | source)
XLA Modules:
  0.0 70.7 jit_solution(9912553272944830512)
XLA Ops:
  0.6 1.9 %shard_map.149 = (f32[1,128]{1,0:T(1,128)S(1)}, f32[3,8,512]{2,1,0:T(8,128)S(1)}, f32[3,8,512]{2,1,0:T(8,128)}, f32[8,16,512]{2,1,0:T(8,128)S(1)}, f32[8,16,512]...) custom-call(f32[8,16,512]{2,1,0:T(8,128)} %refs_0_.4, f32[8,16,512]{2,1,0:T(8,128)} %refs_1_.4, ...), custom_call_target="tpu_custom_call" | custom-call | tf_op jit(solution)/shard_map/pallas_call | solution.py:545
  2.6 3.0 %collective-permute-start.1 = (f32[3,8,512]{2,1,0:T(8,128)S(1)}, f32[3,8,512]{2,1,0:T(8,128)S(1)}, u32[]{:S(2)}, u32[]{:S(2)}) collective-permute-start(f32[3,8,512]{2,1,0:T(8,128)S(1)} %get-tuple-element.45), channel_id=1, source_target_pairs={{0,1},{1,0},{2,3},{3,2},{4,5},{5,4},{6,7},{7,6},{8,9},{9,8},{10,11... | collective-permute-start | bytes 147464 | tf_op jit(solution)/shard_map/ppermute | solution.py:562
  5.6 1.4 %shard_map.150 = (f32[64,2048]{1,0:T(8,128)S(1)}, f32[64,2048]{1,0:T(8,128)S(1)}, f32[1,128]{1,0:T(1,128)S(1)}, f32[1,128]{1,0:T(1,128)S(1)}, bf16[208,240]{1,0:...) custom-call(f32[128,2048]{1,0:T(8,128)} %refs_0_.5, ...), custom_call_target="tpu_custom_call" | custom-call | tf_op jit(solution)/shard_map/pallas_call | solution.py:545
  7.0 0.6 collective-permute-done.1.refs_1_.refs_11_.refs_2_.refs_3_
  7.6 1.0 %shard_map.151 = (f32[32,1,2176]{2,1,0:T(1,128)}, f32[2,24,512]{2,1,0:T(8,128)S(1)}, f32[2,24,512]{2,1,0:T(8,128)S(1)}) custom-call(f32[1,128]{1,0:T(1,128)S(1)} %get-tuple-element.46.refs_0_, f32[3,8,512]{2,1,0:T(8,128)S(1)} %collective-permute-done.1.refs_1_.refs_11_.refs_2_.refs_3_, ...), custom_call_target="tpu_custom_call" | custom-call | tf_op jit(solution)/shard_map/pallas_call | solution.py:545
  8.6 6.4 %all-to-all-start = ((f32[32,1,2176]{2,1,0:T(1,128)}), f32[32,1,2176]{2,1,0:T(1,128)S(1)}, u32[]{:S(2)}, u32[]{:S(2)}) async-start(f32[32,1,2176]{2,1,0:T(1,128)} %get-tuple-element.51), calls=%async_computation | async-start | bytes 557056 | tf_op jit(solution)/shard_map/all_to_all | solution.py:567
  15.0 1.8 %collective-permute-start = (f32[64,2048]{1,0:T(8,128)S(1)}, f32[64,2048]{1,0:T(8,128)S(1)}, u32[]{:S(2)}, u32[]{:S(2)}) collective-permute-start(f32[64,2048]{1,0:T(8,128)S(1)} %get-tuple-element.41.refs_6_.refs_4_), channel_id=1, source_target_pairs={{0,1},{1,0},{2,3},{3,2},{4,5},{5,4},{6,7},{7,6},{8,9},{9,8},{10,11... | collective-permute-start | bytes 1572872 | tf_op jit(solution)/shard_map/ppermute | solution.py:606
  16.9 0.0 collective-permute-start.2
  16.9 0.7 collective-permute-start.3
  17.5 0.6 collective-permute-done.2.refs_13_.refs_8_
  18.2 0.0 collective-permute-done.3.refs_14_.refs_9_
  18.2 2.9 %shard_map.152.refs_1_.refs_0_ = f32[8,16,512]{2,1,0:T(8,128)S(1)} custom-call(bf16[256,384]{1,0:T(8,128)(2,1)} %constant.26.clone.refs_0_.refs_3_, bf16[128,208]{1,0:T(8,128)(2,1)} %constant.27.clone.refs_1_.refs_4_, bf16[128,208]{1,0:T(8,128)(2,1)} %constant.28.clone.refs_2_.refs_5_, bf16[384,256]{1,0:T(8,128)(2,1)} %constant.29.clone.refs_3_.refs_6_, ...), custom_call_target="tpu_custom_call" | custom-call | tf_op jit(solution)/shard_map/pallas_call | solution.py:545
  21.1 4.9 %all-to-all-done.refs_0_ = f32[32,1,2176]{2,1,0:T(1,128)S(1)} async-done(((f32[32,1,2176]{2,1,0:T(1,128)}), f32[32,1,2176]{2,1,0:T(1,128)S(1)}, u32[]{:S(2)}, u32[]{:S(2)}) %all-to-all-start) | async-done | bytes 278560 | tf_op jit(solution)/shard_map/all_to_all | solution.py:567
  26.0 1.1 %shard_map.153 = (f32[3,8,512]{2,1,0:T(8,128)S(1)}, f32[3,8,512]{2,1,0:T(8,128)}) custom-call(f32[32,1,2176]{2,1,0:T(1,128)S(1)} %all-to-all-done.refs_0_, f32[8,16,512]{2,1,0:T(8,128)S(1)} %shard_map.152.refs_1_.refs_0_, f32[1,128]{1,0:T(1,128)S(1)} %get-tuple-element.50.refs_2_.refs_1_.refs_10_.refs_13_, ...), custom_call_target="tpu_custom_call" | custom-call | tf_op jit(solution)/shard_map/pallas_call | solution.py:545
  27.1 1.0 %collective-permute-start.4 = (f32[3,8,512]{2,1,0:T(8,128)S(1)}, f32[3,8,512]{2,1,0:T(8,128)S(1)}, u32[]{:S(2)}, u32[]{:S(2)}) collective-permute-start(f32[3,8,512]{2,1,0:T(8,128)S(1)} %get-tuple-element.52.refs_3_), channel_id=1, source_target_pairs={{0,1},{1,0},{2,3},{3,2},{4,5},{5,4},{6,7},{7,6},{8,9},{9,8},{10,11... | collective-permute-start | bytes 147464 | tf_op jit(solution)/shard_map/ppermute | solution.py:562
  28.1 5.0 %collective-permute-done.4.refs_4_ = f32[3,8,512]{2,1,0:T(8,128)S(1)} collective-permute-done((f32[3,8,512]{2,1,0:T(8,128)S(1)}, f32[3,8,512]{2,1,0:T(8,128)S(1)}, u32[]{:S(2)}, u32[]{:S(2)}) %collective-permute-start.4) | collective-permute-done | bytes 49184 | tf_op jit(solution)/shard_map/ppermute | solution.py:562
  33.2 0.4 shard_map.154
  33.6 0.1 collective-permute-start.5
  33.7 0.7 collective-permute-start.6
  34.4 0.5 shard_map.155
  34.9 0.0 collective-permute-done.refs_1_.refs_3_
  34.9 0.1 collective-permute-done.5.refs_6_
  35.0 0.0 collective-permute-done.6.refs_7_
  35.0 1.1 %shard_map.156 = (f32[32,1,2176]{2,1,0:T(1,128)}, f32[10,24,512]{2,1,0:T(8,128)S(1)}, f32[48,512]{1,0:T(8,128)S(1)}) custom-call(f32[64,2048]{1,0:T(8,128)S(1)} %get-tuple-element.40.refs_5_.refs_3_.refs_0_.refs_2_, f32[64,2048]{1,0:T(8,128)S(1)} %collective-permute-done.refs_1_.refs_3_, f32[8,24,512]{2,1,0:T(8,128)S(1)} %get-tuple-element.53.refs_2_.refs_10_.refs_3_, ...), custom_call_target="tpu_custom_call" | custom-call | tf_op jit(solution)/shard_map/pallas_call | solution.py:545
  36.1 9.4 %all-to-all-start.1 = ((f32[32,1,2176]{2,1,0:T(1,128)}), f32[32,1,2176]{2,1,0:T(1,128)S(1)}, u32[]{:S(2)}, u32[]{:S(2)}) async-start(f32[32,1,2176]{2,1,0:T(1,128)} %get-tuple-element.59), calls=%async_computation.1 | async-start | bytes 557056 | tf_op jit(solution)/shard_map/all_to_all | solution.py:567
  45.6 3.6 %shard_map.157 = (f32[8,16,512]{2,1,0:T(8,128)S(1)}, f32[8,512]{1,0:T(8,128)S(1)}, f32[8,512]{1,0:T(8,128)}, f32[16,512]{1,0:T(8,128)S(1)}, f32[16,512]{1,0:T(8,128)S(1)}) custom-call(bf16[208,240]{1,0:T(8,128)(2,1)} %constant.10.clone.refs_1_.refs_0_, bf16[208,240]{1,0:T(8,128)(2,1)} %constant.24.clone.refs_2_.refs_1_, ...), custom_call_target="tpu_custom_call" | custom-call | tf_op jit(solution)/shard_map/pallas_call | solution.py:545
  49.1 0.3 collective-permute-start.8
  49.5 0.7 collective-permute-start.9
  50.1 1.7 %collective-permute-start.7 = (f32[8,512]{1,0:T(8,128)S(1)}, f32[8,512]{1,0:T(8,128)S(1)}, u32[]{:S(2)}, u32[]{:S(2)}) collective-permute-start(f32[8,512]{1,0:T(8,128)S(1)} %get-tuple-element.62), channel_id=1, source_target_pairs={{0,1},{1,0},{2,3},{3,2},{4,5},{5,4},{6,7},{7,6},{8,9},{9,8},{10,11... | collective-permute-start | bytes 49160 | tf_op jit(solution)/shard_map/ppermute | solution.py:562
  51.9 2.1 %collective-permute-done.7.refs_6_ = f32[8,512]{1,0:T(8,128)S(1)} collective-permute-done((f32[8,512]{1,0:T(8,128)S(1)}, f32[8,512]{1,0:T(8,128)S(1)}, u32[]{:S(2)}, u32[]{:S(2)}) %collective-permute-start.7) | collective-permute-done | bytes 16416 | tf_op jit(solution)/shard_map/ppermute | solution.py:562
  54.0 0.0 collective-permute-done.8.refs_8_
  54.0 0.0 collective-permute-done.9.refs_9_
  54.0 2.6 %all-to-all-done.1.refs_4_ = f32[32,1,2176]{2,1,0:T(1,128)S(1)} async-done(((f32[32,1,2176]{2,1,0:T(1,128)}), f32[32,1,2176]{2,1,0:T(1,128)S(1)}, u32[]{:S(2)}, u32[]{:S(2)}) %all-to-all-start.1) | async-done | bytes 278560 | tf_op jit(solution)/shard_map/all_to_all | solution.py:567
  56.6 1.0 %shard_map.158 = (f32[8,16,512]{2,1,0:T(8,128)S(1)}, f32[8,16,512]{2,1,0:T(8,128)S(1)}, f32[32,1,256]{2,1,0:T(1,128)S(1)}, f32[1,128]{1,0:T(1,128)S(1)}) custom-call(f32[8,16,512]{2,1,0:T(8,128)S(1)} %get-tuple-element.36.refs_3_.refs_10_.refs_0_, f32[8,16,512]{2,1,0:T(8,128)S(1)} %get-tuple-element.37.refs_5_.refs_4_.refs_1_, ...), custom_call_target="tpu_custom_call" | custom-call | tf_op jit(solution)/shard_map/pallas_call | solution.py:545
  57.6 12.0 %all_to_all.15.refs_2_ = f32[32,1,256]{2,1,0:T(1,128)S(1)} all-to-all(f32[32,1,256]{2,1,0:T(1,128)S(1)} %get-tuple-element.67), channel_id=1, replica_groups=mesh['wide'=16,'narrow'=2] {'wide','narrow'}, dimensions={0} | all-to-all | bytes 65536 | tf_op jit(solution)/shard_map/all_to_all | solution.py:567
  69.6 1.1 %shard_map.159 = (f32[8,16,512]{2,1,0:T(8,128)}, f32[8,16,512]{2,1,0:T(8,128)}) custom-call(f32[8,16,512]{2,1,0:T(8,128)S(1)} %get-tuple-element.36.refs_3_.refs_10_.refs_0_, f32[1,128]{1,0:T(1,128)S(1)} %get-tuple-element.66.refs_1_, f32[32,1,256]{2,1,0:T(1,128)S(1)} %all_to_all.15.refs_2_, f32[8,24,512]{2,1,0:T(8,128)S(1)} %get-tuple-element.53.refs_2_.refs_10_.refs_3_, ...), custom_call_target="tpu_custom_call" | custom-call | tf_op jit(solution)/shard_map/pallas_call | solution.py:545
  (2 shorter events, 0.0 us)
Async XLA Ops:
  2.6 5.1 %collective-permute-start.1 = (f32[3,8,512]{2,1,0:T(8,128)S(1)}, f32[3,8,512]{2,1,0:T(8,128)S(1)}, u32[]{:S(2)}, u32[]{:S(2)}) collective-permute-start(f32[3,8,512]{2,1,0:T(8,128)S(1)} %get-tuple-element.45), channel_id=1, source_target_pairs={{0,1},{1,0},{2,3},{3,2},{4,5},{5,4},{6,7},{7,6},{8,9},{9,8},{10,11... | collective-permute-start | bytes 147464 | tf_op jit(solution)/shard_map/ppermute | solution.py:562
  8.6 17.4 %all-to-all-start = ((f32[32,1,2176]{2,1,0:T(1,128)}), f32[32,1,2176]{2,1,0:T(1,128)S(1)}, u32[]{:S(2)}, u32[]{:S(2)}) async-start(f32[32,1,2176]{2,1,0:T(1,128)} %get-tuple-element.51), calls=%async_computation | async-start | bytes 557056 | tf_op jit(solution)/shard_map/all_to_all | solution.py:567
  15.0 19.9 %collective-permute-start = (f32[64,2048]{1,0:T(8,128)S(1)}, f32[64,2048]{1,0:T(8,128)S(1)}, u32[]{:S(2)}, u32[]{:S(2)}) collective-permute-start(f32[64,2048]{1,0:T(8,128)S(1)} %get-tuple-element.41.refs_6_.refs_4_), channel_id=1, source_target_pairs={{0,1},{1,0},{2,3},{3,2},{4,5},{5,4},{6,7},{7,6},{8,9},{9,8},{10,11... | collective-permute-start | bytes 1572872 | tf_op jit(solution)/shard_map/ppermute | solution.py:606
  16.9 1.3 %collective-permute-start.2 = (f32[2,24,512]{2,1,0:T(8,128)S(1)}, f32[2,24,512]{2,1,0:T(8,128)S(1)}, u32[]{:S(2)}, u32[]{:S(2)}) collective-permute-start(f32[2,24,512]{2,1,0:T(8,128)S(1)} %get-tuple-element.47), channel_id=1, source_target_pairs={{0,2},{2,0},{4,6},{6,4},{8,10},{10,8},{12,14},{14,12},{16,18},{18,... | collective-permute-start | bytes 294920 | tf_op jit(solution)/shard_map/ppermute | solution.py:562
  16.9 1.3 %collective-permute-start.3 = (f32[2,24,512]{2,1,0:T(8,128)S(1)}, f32[2,24,512]{2,1,0:T(8,128)S(1)}, u32[]{:S(2)}, u32[]{:S(2)}) collective-permute-start(f32[2,24,512]{2,1,0:T(8,128)S(1)} %get-tuple-element.48), channel_id=1, source_target_pairs={{2,4},{4,2},{6,8},{8,6},{10,12},{12,10},{14,16},{16,14},{18,20},{2... | collective-permute-start | bytes 294920 | tf_op jit(solution)/shard_map/ppermute | solution.py:562
  27.1 6.1 %collective-permute-start.4 = (f32[3,8,512]{2,1,0:T(8,128)S(1)}, f32[3,8,512]{2,1,0:T(8,128)S(1)}, u32[]{:S(2)}, u32[]{:S(2)}) collective-permute-start(f32[3,8,512]{2,1,0:T(8,128)S(1)} %get-tuple-element.52.refs_3_), channel_id=1, source_target_pairs={{0,1},{1,0},{2,3},{3,2},{4,5},{5,4},{6,7},{7,6},{8,9},{9,8},{10,11... | collective-permute-start | bytes 147464 | tf_op jit(solution)/shard_map/ppermute | solution.py:562
  33.6 1.4 %collective-permute-start.5 = (f32[2,24,512]{2,1,0:T(8,128)S(1)}, f32[2,24,512]{2,1,0:T(8,128)S(1)}, u32[]{:S(2)}, u32[]{:S(2)}) collective-permute-start(f32[2,24,512]{2,1,0:T(8,128)S(1)} %get-tuple-element.57), channel_id=1, source_target_pairs={{0,2},{2,0},{4,6},{6,4},{8,10},{10,8},{12,14},{14,12},{16,18},{18,... | collective-permute-start | bytes 294920 | tf_op jit(solution)/shard_map/ppermute | solution.py:562
  33.7 1.3 %collective-permute-start.6 = (f32[2,24,512]{2,1,0:T(8,128)S(1)}, f32[2,24,512]{2,1,0:T(8,128)S(1)}, u32[]{:S(2)}, u32[]{:S(2)}) collective-permute-start(f32[2,24,512]{2,1,0:T(8,128)S(1)} %get-tuple-element.58), channel_id=1, source_target_pairs={{2,4},{4,2},{6,8},{8,6},{10,12},{12,10},{14,16},{16,14},{18,20},{2... | collective-permute-start | bytes 294920 | tf_op jit(solution)/shard_map/ppermute | solution.py:562
  36.1 20.5 %all-to-all-start.1 = ((f32[32,1,2176]{2,1,0:T(1,128)}), f32[32,1,2176]{2,1,0:T(1,128)S(1)}, u32[]{:S(2)}, u32[]{:S(2)}) async-start(f32[32,1,2176]{2,1,0:T(1,128)} %get-tuple-element.59), calls=%async_computation.1 | async-start | bytes 557056 | tf_op jit(solution)/shard_map/all_to_all | solution.py:567
  49.1 4.9 %collective-permute-start.8 = (f32[16,512]{1,0:T(8,128)S(1)}, f32[16,512]{1,0:T(8,128)S(1)}, u32[]{:S(2)}, u32[]{:S(2)}) collective-permute-start(f32[16,512]{1,0:T(8,128)S(1)} %get-tuple-element.63), channel_id=1, source_target_pairs={{0,2},{2,0},{4,6},{6,4},{8,10},{10,8},{12,14},{14,12},{16,18},{18,... | collective-permute-start | bytes 98312 | tf_op jit(solution)/shard_map/ppermute | solution.py:562
  49.5 4.5 %collective-permute-start.9 = (f32[16,512]{1,0:T(8,128)S(1)}, f32[16,512]{1,0:T(8,128)S(1)}, u32[]{:S(2)}, u32[]{:S(2)}) collective-permute-start(f32[16,512]{1,0:T(8,128)S(1)} %get-tuple-element.64), channel_id=1, source_target_pairs={{2,4},{4,2},{6,8},{8,6},{10,12},{12,10},{14,16},{16,14},{18,20},{2... | collective-permute-start | bytes 98312 | tf_op jit(solution)/shard_map/ppermute | solution.py:562
  50.1 3.9 %collective-permute-start.7 = (f32[8,512]{1,0:T(8,128)S(1)}, f32[8,512]{1,0:T(8,128)S(1)}, u32[]{:S(2)}, u32[]{:S(2)}) collective-permute-start(f32[8,512]{1,0:T(8,128)S(1)} %get-tuple-element.62), channel_id=1, source_target_pairs={{0,1},{1,0},{2,3},{3,2},{4,5},{5,4},{6,7},{7,6},{8,9},{9,8},{10,11... | collective-permute-start | bytes 49160 | tf_op jit(solution)/shard_map/ppermute | solution.py:562

commit v7 on v6

--- a/solution.py
+++ b/solution.py
@@ -18,7 +18,7 @@
 AB = 208
 HZ = 256
 HW = 384
-STAGED = 3
+STAGED = 6
 TABLES = 10
 KCOL = 2048
 WIDTH = KCOL + 128
@@ -222,7 +222,11 @@
 
 def fine_solve(rows, sigma, tables):
     wh, wl, th, tl, vh, vl, uh, ul, column, beyond = tables
-    spectra = dot3((value(wh), value(wl)), split2(rows))
+    high, low = value(wh), value(wl)
+    for table in tables:
+        if isinstance(table, Loaded):
+            table.begin()
+    spectra = dot3((high, low), split2(rows))
     th, tl, vh, vl, uh, ul, column, beyond = [value(table) for table in (th, tl, vh, vl, uh, ul, column, beyond)]
     nodal = []
     for half in range(2):
@@ -378,10 +382,11 @@
     xa[...], xb[...] = pair_out(w, block[0:2], block[BX - 2 : BX])
 
 
-def interior_kernel(late, right, diagonal, search, ya, yb, image, product, table):
+def interior_kernel(late, diagonal_late, right, search, ya, yb, image, product, table, diagonal):
     d = lax.axis_index("narrow")
     low, high = pair_in(d, ya[1], yb[1])
     centre = search[...]
+    diagonal[...] = diagonal_late.here()[...]
     part = (6.0 + extend_y(diagonal[...], [low], [high], 1)) * centre - roll_sum(centre)
     zero = jnp.zeros((1, YR, BZ), F32)
     part = part - jnp.concatenate([zero, centre[0 : BX - 1]], axis=0) - jnp.concatenate([centre[1:BX], zero], axis=0)
@@ -503,9 +508,15 @@
 
 class Loaded:
     def __init__(self, copy, ref):
-        self.copy, self.ref, self.ready = copy, ref, False
+        self.copy, self.ref, self.begun, self.ready = copy, ref, False, False
+
+    def begin(self):
+        if not self.begun:
+            self.copy.start()
+            self.begun = True
 
     def wait(self):
+        self.begin()
         if not self.ready:
             self.copy.wait()
             self.ready = True
@@ -519,10 +530,10 @@
     def __init__(self, semaphores):
         self.semaphores, self.all = semaphores, []
 
-    def start(self, source, target):
-        copy = pltpu.make_async_copy(source, target, self.semaphores.at[len(self.all)])
-        copy.start()
-        self.all.append(Loaded(copy, target))
+    def start(self, source, target, begin=True):
+        self.all.append(Loaded(pltpu.make_async_copy(source, target, self.semaphores.at[len(self.all)]), target))
+        if begin:
+            self.all[-1].begin()
         return self.all[-1]
 
     def finish(self):
@@ -530,13 +541,16 @@
             loaded.wait()
 
 
-def call(kernel, outs, far=(), late=(), near=(), final=False):
+def call(kernel, outs, far=(), late=(), near=(), final=False, first_wave=99):
     first, second = len(far), len(far) + len(late)
 
     def run(*refs):
         end = len(refs) - 1 - len(late)
         copies = Copies(refs[-1])
-        loaded = [copies.start(source, target) for source, target in zip(refs[first:second], refs[end:-1])]
+        loaded = [
+            copies.start(source, target, i < first_wave)
+            for i, (source, target) in enumerate(zip(refs[first:second], refs[end:-1]))
+        ]
         kernel(copies, *refs[:first], *loaded, *refs[second:end])
         copies.finish()
 
@@ -582,6 +596,7 @@
     block, layer, extended = (BX, BY, BZ), (YR, BZ), (BX, YR, BZ)
     y_shape, x_shape, half = (3, BX, BZ), (2, YR, BZ), (ELEMS // 2, KCOL)
     gather = jax.ShapeDtypeStruct((BZ, EY * ELEMS), BF16)
+    diagonal_far = diagonal
     c, ya, yb, right, diagonal, slots, table = call(
         start_kernel,
         [(1, ELEMS), y_shape, y_shape, block, block, (1, ELEMS), gather],
@@ -610,8 +625,8 @@
         near=[solved, slots, ya, ta, ra, rb],
     )
     sa, sb = pair_swap(sa, sb, "wide")
-    inner, product, table = call(
-        interior_kernel, [extended, (1, 128), gather], near=[right, diagonal, search, ya, yb]
+    inner, product, table, diagonal = call(
+        interior_kernel, [extended, (1, 128), gather, block], late=[diagonal_far], near=[right, search, ya, yb]
     )
     sums, image, halo = call(
         part(operator_kernel, swapped, sizes),
@@ -620,7 +635,7 @@
     )
     sums = everywhere(sums)
     solved, ya, yb, fa, fb = call(
-        second_fine_kernel, [block, (BX, BZ), (BX, BZ), (BY, BZ), (BY, BZ)], late=fine, near=[image, sigma]
+        second_fine_kernel, [block, (BX, BZ), (BX, BZ), (BY, BZ), (BY, BZ)], late=fine, near=[image, sigma], first_wave=4
     )
     ya, yb = pair_swap(ya, yb, "narrow")
     fa, fb = pair_swap(fa, fb, "wide")

time: 71.1 us -> 71.8 us (level)
  Pallas kernels: 16.1 us -> 17.7 us
  starting transfers between devices: 25.8 us -> 24.9 us
  blocking collectives: 12 us -> 12.8 us
    pallas_call x11, Pallas kernels: 16.1 us -> 17.7 us  [call(): pl.pallas_call(run, out_shape=[shape_of(getattr(out, 'shape', out), getat...]
    all_to_all x2, starting transfers between devices: 15.8 us -> 14.9 us  [everywhere(): return lax.all_to_all(rows, AXES, split_axis=0, concat_axis=0, tiled=True)]
    all_to_all x1, blocking collectives: 12 us -> 12.8 us  [everywhere(): return lax.all_to_all(rows, AXES, split_axis=0, concat_axis=0, tiled=True)]
  transfers between devices with their start and end apart: 12 -> 12, of which waited for: 7 -> 6; matrix products, arithmetic and copies ran while one was open for 0% -> 0% of each run, Pallas kernels for 14% -> 16%
where the time goes in v7:
time: 71.8 us; the launch traced here: 71.3 us
  starting transfers between devices  24.9 us (35%)
  Pallas kernels  17.7 us (25%)
  waiting for transfers between devices  15.3 us (21%)
  blocking collectives  12.8 us (18%)
  between operations  0.79 us (1%)
    pallas_call x11, Pallas kernels, call(): pl.pallas_call(run, out_shape=[shape_of(getattr(out, 'shape', out), getat...  17.7 us
    all_to_all x2, starting transfers between devices, everywhere(): return lax.all_to_all(rows, AXES, split_axis=0, concat_axis=0, tiled=True)  14.9 us
    all_to_all x1, blocking collectives, everywhere(): return lax.all_to_all(rows, AXES, split_axis=0, concat_axis=0, tiled=True)  12.8 us
    ppermute x9, waiting for transfers between devices, pair_swap(): lax.ppermute(value, axis, perm)  8.27 us
    ppermute x9, starting transfers between devices, pair_swap(): lax.ppermute(value, axis, perm)  8.14 us
    all_to_all x2, waiting for transfers between devices, everywhere(): return lax.all_to_all(rows, AXES, split_axis=0, concat_axis=0, tiled=True)  6.98 us
    ppermute x1, starting transfers between devices, body(): lax.ppermute(sent, 'narrow', [(0, 1), (1, 0)])  1.83 us
  transfers between devices with their start and end apart: 12, of which 6 were waited for; matrix products, arithmetic and copies ran while one was open for 0% of the time, Pallas kernels for 16%

profile of v7, /device:TPU:0, one launch (start us, length us, event | category | flops | bytes accessed | tf_op | source)
XLA Modules:
  0.0 71.3 jit_solution(15988709190551435029)
XLA Ops:
  0.6 1.9 %shard_map.149 = (f32[1,128]{1,0:T(1,128)S(1)}, f32[3,8,512]{2,1,0:T(8,128)S(1)}, f32[3,8,512]{2,1,0:T(8,128)}, f32[8,16,512]{2,1,0:T(8,128)S(1)}, f32[8,16,512]...) custom-call(f32[8,16,512]{2,1,0:T(8,128)} %refs_0_.5, f32[8,16,512]{2,1,0:T(8,128)} %refs_0_.7, ...), custom_call_target="tpu_custom_call" | custom-call | tf_op jit(solution)/shard_map/pallas_call | solution.py:559
  2.6 3.0 %collective-permute-start = (f32[3,8,512]{2,1,0:T(8,128)S(1)}, f32[3,8,512]{2,1,0:T(8,128)S(1)}, u32[]{:S(2)}, u32[]{:S(2)}) collective-permute-start(f32[3,8,512]{2,1,0:T(8,128)S(1)} %get-tuple-element.50), channel_id=1, source_target_pairs={{0,1},{1,0},{2,3},{3,2},{4,5},{5,4},{6,7},{7,6},{8,9},{9,8},{10,11... | collective-permute-start | bytes 147464 | tf_op jit(solution)/shard_map/ppermute | solution.py:576
  5.6 1.5 %shard_map.150 = (f32[64,2048]{1,0:T(8,128)S(1)}, f32[64,2048]{1,0:T(8,128)S(1)}, f32[1,128]{1,0:T(1,128)S(1)}, f32[1,128]{1,0:T(1,128)S(1)}, bf16[208,240]{1,0:...) custom-call(f32[128,2048]{1,0:T(8,128)} %refs_0_.6, ...), custom_call_target="tpu_custom_call" | custom-call | tf_op jit(solution)/shard_map/pallas_call | solution.py:559
  7.1 0.5 collective-permute-done.refs_1_.refs_11_.refs_2_.refs_3_
  7.6 1.0 %shard_map.151 = (f32[32,1,2176]{2,1,0:T(1,128)}, f32[2,24,512]{2,1,0:T(8,128)S(1)}, f32[2,24,512]{2,1,0:T(8,128)S(1)}) custom-call(f32[1,128]{1,0:T(1,128)S(1)} %get-tuple-element.51.refs_0_, f32[3,8,512]{2,1,0:T(8,128)S(1)} %collective-permute-done.refs_1_.refs_11_.refs_2_.refs_3_, ...), custom_call_target="tpu_custom_call" | custom-call | tf_op jit(solution)/shard_map/pallas_call | solution.py:559
  8.6 6.4 %all-to-all-start = ((f32[32,1,2176]{2,1,0:T(1,128)}), f32[32,1,2176]{2,1,0:T(1,128)S(1)}, u32[]{:S(2)}, u32[]{:S(2)}) async-start(f32[32,1,2176]{2,1,0:T(1,128)} %get-tuple-element.58), calls=%async_computation | async-start | bytes 557056 | tf_op jit(solution)/shard_map/all_to_all | solution.py:581
  15.0 1.8 %collective-permute-start.4 = (f32[64,2048]{1,0:T(8,128)S(1)}, f32[64,2048]{1,0:T(8,128)S(1)}, u32[]{:S(2)}, u32[]{:S(2)}) collective-permute-start(f32[64,2048]{1,0:T(8,128)S(1)} %get-tuple-element.53.refs_6_.refs_4_), channel_id=1, source_target_pairs={{0,1},{1,0},{2,3},{3,2},{4,5},{5,4},{6,7},{7,6},{8,9},{9,8},{10,11... | collective-permute-start | bytes 1572872 | tf_op jit(solution)/shard_map/ppermute | solution.py:621
  16.9 0.0 collective-permute-start.1
  16.9 0.7 collective-permute-start.2
  17.5 0.6 collective-permute-done.1.refs_13_.refs_8_
  18.2 0.0 collective-permute-done.2.refs_14_.refs_9_
  18.2 2.7 %shard_map.152.refs_1_.refs_0_ = f32[8,16,512]{2,1,0:T(8,128)S(1)} custom-call(bf16[384,256]{1,0:T(8,128)(2,1)} %constant.29.clone.refs_0_.refs_6_, bf16[384,256]{1,0:T(8,128)(2,1)} %constant.30.clone.refs_1_.refs_7_, f32[208,128]{1,0:T(8,128)} %constant.31.clone.refs_2_.refs_8_, f32[8,384]{1,0:T(8,128)} %constant.32.clone.refs_3_.refs_9_, ...), custom_call_target="tpu_custom_call" | custom-call | tf_op jit(solution)/shard_map/pallas_call | solution.py:559
  20.9 5.1 %all-to-all-done.refs_0_ = f32[32,1,2176]{2,1,0:T(1,128)S(1)} async-done(((f32[32,1,2176]{2,1,0:T(1,128)}), f32[32,1,2176]{2,1,0:T(1,128)S(1)}, u32[]{:S(2)}, u32[]{:S(2)}) %all-to-all-start) | async-done | bytes 278560 | tf_op jit(solution)/shard_map/all_to_all | solution.py:581
  26.0 1.1 %shard_map.153 = (f32[3,8,512]{2,1,0:T(8,128)S(1)}, f32[3,8,512]{2,1,0:T(8,128)}) custom-call(f32[32,1,2176]{2,1,0:T(1,128)S(1)} %all-to-all-done.refs_0_, f32[8,16,512]{2,1,0:T(8,128)S(1)} %shard_map.152.refs_1_.refs_0_, f32[1,128]{1,0:T(1,128)S(1)} %get-tuple-element.57.refs_2_.refs_1_.refs_10_.refs_13_, ...), custom_call_target="tpu_custom_call" | custom-call | tf_op jit(solution)/shard_map/pallas_call | solution.py:559
  27.1 1.0 %collective-permute-start.3 = (f32[3,8,512]{2,1,0:T(8,128)S(1)}, f32[3,8,512]{2,1,0:T(8,128)S(1)}, u32[]{:S(2)}, u32[]{:S(2)}) collective-permute-start(f32[3,8,512]{2,1,0:T(8,128)S(1)} %get-tuple-element.59.refs_3_), channel_id=1, source_target_pairs={{0,1},{1,0},{2,3},{3,2},{4,5},{5,4},{6,7},{7,6},{8,9},{9,8},{10,11... | collective-permute-start | bytes 147464 | tf_op jit(solution)/shard_map/ppermute | solution.py:576
  28.1 5.0 %collective-permute-done.3.refs_4_ = f32[3,8,512]{2,1,0:T(8,128)S(1)} collective-permute-done((f32[3,8,512]{2,1,0:T(8,128)S(1)}, f32[3,8,512]{2,1,0:T(8,128)S(1)}, u32[]{:S(2)}, u32[]{:S(2)}) %collective-permute-start.3) | collective-permute-done | bytes 49184 | tf_op jit(solution)/shard_map/ppermute | solution.py:576
  33.2 0.4 shard_map.154
  33.6 0.1 collective-permute-start.5
  33.7 0.7 collective-permute-start.6
  34.3 1.5 %shard_map.155 = (f32[8,24,512]{2,1,0:T(8,128)S(1)}, f32[1,128]{1,0:T(1,128)S(1)}, bf16[512,256]{1,0:T(8,128)(2,1)S(1)}, f32[8,16,512]{2,1,0:T(8,128)S(1)}) custom-call(f32[8,16,512]{2,1,0:T(8,128)} %refs_0_.7, f32[8,16,512]{2,1,0:T(8,128)S(1)} %get-tuple-element.40.refs_3_.refs_10_.refs_1_.refs_0_, ...), custom_call_target="tpu_custom_call" | custom-call | tf_op jit(solution)/shard_map/pallas_call | solution.py:559
  35.9 0.0 collective-permute-done.4.refs_1_.refs_3_
  35.9 0.0 collective-permute-done.5.refs_6_
  35.9 0.0 collective-permute-done.6.refs_7_
  35.9 1.1 %shard_map.156 = (f32[32,1,2176]{2,1,0:T(1,128)}, f32[10,24,512]{2,1,0:T(8,128)S(1)}, f32[48,512]{1,0:T(8,128)S(1)}) custom-call(f32[64,2048]{1,0:T(8,128)S(1)} %get-tuple-element.52.refs_5_.refs_3_.refs_0_.refs_2_, f32[64,2048]{1,0:T(8,128)S(1)} %collective-permute-done.4.refs_1_.refs_3_, f32[8,24,512]{2,1,0:T(8,128)S(1)} %get-tuple-element.60.refs_2_.refs_10_.refs_3_, ...), custom_call_target="tpu_custom_call" | custom-call | tf_op jit(solution)/shard_map/pallas_call | solution.py:559
  37.0 8.5 %all-to-all-start.1 = ((f32[32,1,2176]{2,1,0:T(1,128)}), f32[32,1,2176]{2,1,0:T(1,128)S(1)}, u32[]{:S(2)}, u32[]{:S(2)}) async-start(f32[32,1,2176]{2,1,0:T(1,128)} %get-tuple-element.67), calls=%async_computation.1 | async-start | bytes 557056 | tf_op jit(solution)/shard_map/all_to_all | solution.py:581
  45.6 4.2 %shard_map.157 = (f32[8,16,512]{2,1,0:T(8,128)S(1)}, f32[8,512]{1,0:T(8,128)S(1)}, f32[8,512]{1,0:T(8,128)}, f32[16,512]{1,0:T(8,128)S(1)}, f32[16,512]{1,0:T(8,128)S(1)}) custom-call(bf16[208,240]{1,0:T(8,128)(2,1)} %constant.10.clone.refs_1_.refs_0_, bf16[208,240]{1,0:T(8,128)(2,1)} %constant.24.clone.refs_2_.refs_1_, ...), custom_call_target="tpu_custom_call" | custom-call | tf_op jit(solution)/shard_map/pallas_call | solution.py:559
  49.8 0.3 collective-permute-start.8
  50.1 0.7 collective-permute-start.9
  50.8 1.7 %collective-permute-start.7 = (f32[8,512]{1,0:T(8,128)S(1)}, f32[8,512]{1,0:T(8,128)S(1)}, u32[]{:S(2)}, u32[]{:S(2)}) collective-permute-start(f32[8,512]{1,0:T(8,128)S(1)} %get-tuple-element.70), channel_id=1, source_target_pairs={{0,1},{1,0},{2,3},{3,2},{4,5},{5,4},{6,7},{7,6},{8,9},{9,8},{10,11... | collective-permute-start | bytes 49160 | tf_op jit(solution)/shard_map/ppermute | solution.py:576
  52.5 2.1 %collective-permute-done.7.refs_6_ = f32[8,512]{1,0:T(8,128)S(1)} collective-permute-done((f32[8,512]{1,0:T(8,128)S(1)}, f32[8,512]{1,0:T(8,128)S(1)}, u32[]{:S(2)}, u32[]{:S(2)}) %collective-permute-start.7) | collective-permute-done | bytes 16416 | tf_op jit(solution)/shard_map/ppermute | solution.py:576
  54.6 0.0 collective-permute-done.8.refs_8_
  54.6 0.0 collective-permute-done.9.refs_9_
  54.6 1.9 %all-to-all-done.1.refs_4_ = f32[32,1,2176]{2,1,0:T(1,128)S(1)} async-done(((f32[32,1,2176]{2,1,0:T(1,128)}), f32[32,1,2176]{2,1,0:T(1,128)S(1)}, u32[]{:S(2)}, u32[]{:S(2)}) %all-to-all-start.1) | async-done | bytes 278560 | tf_op jit(solution)/shard_map/all_to_all | solution.py:581
  56.5 1.0 %shard_map.158 = (f32[8,16,512]{2,1,0:T(8,128)S(1)}, f32[8,16,512]{2,1,0:T(8,128)S(1)}, f32[32,1,256]{2,1,0:T(1,128)S(1)}, f32[1,128]{1,0:T(1,128)S(1)}) custom-call(f32[8,16,512]{2,1,0:T(8,128)S(1)} %get-tuple-element.40.refs_3_.refs_10_.refs_1_.refs_0_, f32[8,16,512]{2,1,0:T(8,128)S(1)} %get-tuple-element.61.refs_1_, ...), custom_call_target="tpu_custom_call" | custom-call | tf_op jit(solution)/shard_map/pallas_call | solution.py:559
  57.5 12.8 %all_to_all.15.refs_2_ = f32[32,1,256]{2,1,0:T(1,128)S(1)} all-to-all(f32[32,1,256]{2,1,0:T(1,128)S(1)} %get-tuple-element.75), channel_id=1, replica_groups=mesh['wide'=16,'narrow'=2] {'wide','narrow'}, dimensions={0} | all-to-all | bytes 65536 | tf_op jit(solution)/shard_map/all_to_all | solution.py:581
  70.2 1.1 %shard_map.159 = (f32[8,16,512]{2,1,0:T(8,128)}, f32[8,16,512]{2,1,0:T(8,128)}) custom-call(f32[8,16,512]{2,1,0:T(8,128)S(1)} %get-tuple-element.40.refs_3_.refs_10_.refs_1_.refs_0_, f32[1,128]{1,0:T(1,128)S(1)} %get-tuple-element.74.refs_1_, f32[32,1,256]{2,1,0:T(1,128)S(1)} %all_to_all.15.refs_2_, ...), custom_call_target="tpu_custom_call" | custom-call | tf_op jit(solution)/shard_map/pallas_call | solution.py:559
  (2 shorter events, 0.0 us)
Async XLA Ops:
  2.6 5.1 %collective-permute-start = (f32[3,8,512]{2,1,0:T(8,128)S(1)}, f32[3,8,512]{2,1,0:T(8,128)S(1)}, u32[]{:S(2)}, u32[]{:S(2)}) collective-permute-start(f32[3,8,512]{2,1,0:T(8,128)S(1)} %get-tuple-element.50), channel_id=1, source_target_pairs={{0,1},{1,0},{2,3},{3,2},{4,5},{5,4},{6,7},{7,6},{8,9},{9,8},{10,11... | collective-permute-start | bytes 147464 | tf_op jit(solution)/shard_map/ppermute | solution.py:576
  8.6 17.4 %all-to-all-start = ((f32[32,1,2176]{2,1,0:T(1,128)}), f32[32,1,2176]{2,1,0:T(1,128)S(1)}, u32[]{:S(2)}, u32[]{:S(2)}) async-start(f32[32,1,2176]{2,1,0:T(1,128)} %get-tuple-element.58), calls=%async_computation | async-start | bytes 557056 | tf_op jit(solution)/shard_map/all_to_all | solution.py:581
  15.0 20.8 %collective-permute-start.4 = (f32[64,2048]{1,0:T(8,128)S(1)}, f32[64,2048]{1,0:T(8,128)S(1)}, u32[]{:S(2)}, u32[]{:S(2)}) collective-permute-start(f32[64,2048]{1,0:T(8,128)S(1)} %get-tuple-element.53.refs_6_.refs_4_), channel_id=1, source_target_pairs={{0,1},{1,0},{2,3},{3,2},{4,5},{5,4},{6,7},{7,6},{8,9},{9,8},{10,11... | collective-permute-start | bytes 1572872 | tf_op jit(solution)/shard_map/ppermute | solution.py:621
  16.9 1.3 %collective-permute-start.1 = (f32[2,24,512]{2,1,0:T(8,128)S(1)}, f32[2,24,512]{2,1,0:T(8,128)S(1)}, u32[]{:S(2)}, u32[]{:S(2)}) collective-permute-start(f32[2,24,512]{2,1,0:T(8,128)S(1)} %get-tuple-element.54), channel_id=1, source_target_pairs={{0,2},{2,0},{4,6},{6,4},{8,10},{10,8},{12,14},{14,12},{16,18},{18,... | collective-permute-start | bytes 294920 | tf_op jit(solution)/shard_map/ppermute | solution.py:576
  16.9 1.3 %collective-permute-start.2 = (f32[2,24,512]{2,1,0:T(8,128)S(1)}, f32[2,24,512]{2,1,0:T(8,128)S(1)}, u32[]{:S(2)}, u32[]{:S(2)}) collective-permute-start(f32[2,24,512]{2,1,0:T(8,128)S(1)} %get-tuple-element.55), channel_id=1, source_target_pairs={{2,4},{4,2},{6,8},{8,6},{10,12},{12,10},{14,16},{16,14},{18,20},{2... | collective-permute-start | bytes 294920 | tf_op jit(solution)/shard_map/ppermute | solution.py:576
  27.1 6.1 %collective-permute-start.3 = (f32[3,8,512]{2,1,0:T(8,128)S(1)}, f32[3,8,512]{2,1,0:T(8,128)S(1)}, u32[]{:S(2)}, u32[]{:S(2)}) collective-permute-start(f32[3,8,512]{2,1,0:T(8,128)S(1)} %get-tuple-element.59.refs_3_), channel_id=1, source_target_pairs={{0,1},{1,0},{2,3},{3,2},{4,5},{5,4},{6,7},{7,6},{8,9},{9,8},{10,11... | collective-permute-start | bytes 147464 | tf_op jit(solution)/shard_map/ppermute | solution.py:576
  33.6 2.3 %collective-permute-start.5 = (f32[2,24,512]{2,1,0:T(8,128)S(1)}, f32[2,24,512]{2,1,0:T(8,128)S(1)}, u32[]{:S(2)}, u32[]{:S(2)}) collective-permute-start(f32[2,24,512]{2,1,0:T(8,128)S(1)} %get-tuple-element.65), channel_id=1, source_target_pairs={{0,2},{2,0},{4,6},{6,4},{8,10},{10,8},{12,14},{14,12},{16,18},{18,... | collective-permute-start | bytes 294920 | tf_op jit(solution)/shard_map/ppermute | solution.py:576
  33.7 2.2 %collective-permute-start.6 = (f32[2,24,512]{2,1,0:T(8,128)S(1)}, f32[2,24,512]{2,1,0:T(8,128)S(1)}, u32[]{:S(2)}, u32[]{:S(2)}) collective-permute-start(f32[2,24,512]{2,1,0:T(8,128)S(1)} %get-tuple-element.66), channel_id=1, source_target_pairs={{2,4},{4,2},{6,8},{8,6},{10,12},{12,10},{14,16},{16,14},{18,20},{2... | collective-permute-start | bytes 294920 | tf_op jit(solution)/shard_map/ppermute | solution.py:576
  37.0 19.5 %all-to-all-start.1 = ((f32[32,1,2176]{2,1,0:T(1,128)}), f32[32,1,2176]{2,1,0:T(1,128)S(1)}, u32[]{:S(2)}, u32[]{:S(2)}) async-start(f32[32,1,2176]{2,1,0:T(1,128)} %get-tuple-element.67), calls=%async_computation.1 | async-start | bytes 557056 | tf_op jit(solution)/shard_map/all_to_all | solution.py:581
  49.8 4.8 %collective-permute-start.8 = (f32[16,512]{1,0:T(8,128)S(1)}, f32[16,512]{1,0:T(8,128)S(1)}, u32[]{:S(2)}, u32[]{:S(2)}) collective-permute-start(f32[16,512]{1,0:T(8,128)S(1)} %get-tuple-element.71), channel_id=1, source_target_pairs={{0,2},{2,0},{4,6},{6,4},{8,10},{10,8},{12,14},{14,12},{16,18},{18,... | collective-permute-start | bytes 98312 | tf_op jit(solution)/shard_map/ppermute | solution.py:576
  50.1 4.5 %collective-permute-start.9 = (f32[16,512]{1,0:T(8,128)S(1)}, f32[16,512]{1,0:T(8,128)S(1)}, u32[]{:S(2)}, u32[]{:S(2)}) collective-permute-start(f32[16,512]{1,0:T(8,128)S(1)} %get-tuple-element.72), channel_id=1, source_target_pairs={{2,4},{4,2},{6,8},{8,6},{10,12},{12,10},{14,16},{16,14},{18,20},{2... | collective-permute-start | bytes 98312 | tf_op jit(solution)/shard_map/ppermute | solution.py:576
  50.8 3.8 %collective-permute-start.7 = (f32[8,512]{1,0:T(8,128)S(1)}, f32[8,512]{1,0:T(8,128)S(1)}, u32[]{:S(2)}, u32[]{:S(2)}) collective-permute-start(f32[8,512]{1,0:T(8,128)S(1)} %get-tuple-element.70), channel_id=1, source_target_pairs={{0,1},{1,0},{2,3},{3,2},{4,5},{5,4},{6,7},{7,6},{8,9},{9,8},{10,11... | collective-permute-start | bytes 49160 | tf_op jit(solution)/shard_map/ppermute | solution.py:576

commit v8 on v7

--- a/solution.py
+++ b/solution.py
@@ -60,8 +60,8 @@
             to_xy[:, e, :, :, y % YR] += basis.T[:, None, :] * basis[j][None, :, None]
             if 1 <= j <= 8:
                 from_xy[:, y, :, e, :] = basis[1:9, :, None] * basis[j][None, None, :]
-    to_xy = np.pad(to_xy.reshape(200, YW), ((0, AB - 200), (0, 0)))
-    from_xy = np.pad(from_xy.reshape(BX * BY, 200), ((0, 0), (0, AB - 200)))
+    to_xy = np.pad(to_xy.reshape(200, YW), ((0, AB - 200), (0, 256 - YW)))
+    from_xy = np.pad(from_xy.reshape(BX * BY, 200), ((0, 0), (0, 256 - 200)))
     column = np.zeros((AB, 128), np.float32)
     grid = np.zeros((10, EY, 10, 2))
     grid[..., 0] = values[:, None, None] + values[None, None, :]
@@ -226,6 +226,7 @@
     for table in tables:
         if isinstance(table, Loaded):
             table.begin()
+    rows = jnp.concatenate([rows, jnp.zeros((256 - YW, BZ), F32)], axis=0)
     spectra = dot3((high, low), split2(rows))
     th, tl, vh, vl, uh, ul, column, beyond = [value(table) for table in (th, tl, vh, vl, uh, ul, column, beyond)]
     nodal = []
@@ -235,6 +236,7 @@
         part = dot3(split2(part), (th, tl)) + edge * beyond[half : half + 1]
         sig = jnp.where(column[:, 1:2] == 0.0, repeat_lanes(sigma, half), repeat_lanes(sigma, 2 + half))
         part = part / (column[:, 0:1] + beyond[2:3] + sig)
+        part = jnp.concatenate([part, jnp.zeros((256 - AB, HW), F32)], axis=0)
         part = dot3((vh, vl), split2(part))
         nodal.append(dot3(split2(part), (uh, ul)).reshape(BX, BY, HZ))
     return jnp.concatenate(nodal, axis=2)
@@ -635,7 +637,7 @@
     )
     sums = everywhere(sums)
     solved, ya, yb, fa, fb = call(
-        second_fine_kernel, [block, (BX, BZ), (BX, BZ), (BY, BZ), (BY, BZ)], late=fine, near=[image, sigma], first_wave=4
+        second_fine_kernel, [block, (BX, BZ), (BX, BZ), (BY, BZ), (BY, BZ)], late=fine, near=[image, sigma]
     )
     ya, yb = pair_swap(ya, yb, "narrow")
     fa, fb = pair_swap(fa, fb, "wide")

time: 71.8 us -> 71.1 us (level)
  blocking collectives: 12.8 us -> 12 us
    all_to_all x1, blocking collectives: 12.8 us -> 12 us  [everywhere(): return lax.all_to_all(rows, AXES, split_axis=0, concat_axis=0, tiled=True)]
  transfers between devices with their start and end apart: 12 -> 12, of which waited for: 6 -> 6; matrix products, arithmetic and copies ran while one was open for 0% -> 0% of each run, Pallas kernels for 16% -> 15%
where the time goes in v8:
time: 71.1 us; the launch traced here: 70.7 us
  starting transfers between devices  24.9 us (35%)
  Pallas kernels  17 us (24%)
  waiting for transfers between devices  16 us (23%)
  blocking collectives  12 us (17%)
  between operations  0.79 us (1%)
    pallas_call x11, Pallas kernels, call(): pl.pallas_call(run, out_shape=[shape_of(getattr(out, 'shape', out), getat...  17 us
    all_to_all x2, starting transfers between devices, everywhere(): return lax.all_to_all(rows, AXES, split_axis=0, concat_axis=0, tiled=True)  14.9 us
    all_to_all x1, blocking collectives, everywhere(): return lax.all_to_all(rows, AXES, split_axis=0, concat_axis=0, tiled=True)  12 us
    ppermute x9, waiting for transfers between devices, pair_swap(): lax.ppermute(value, axis, perm)  8.33 us
    ppermute x9, starting transfers between devices, pair_swap(): lax.ppermute(value, axis, perm)  8.14 us
    all_to_all x2, waiting for transfers between devices, everywhere(): return lax.all_to_all(rows, AXES, split_axis=0, concat_axis=0, tiled=True)  7.65 us
    ppermute x1, starting transfers between devices, body(): lax.ppermute(sent, 'narrow', [(0, 1), (1, 0)])  1.83 us
  transfers between devices with their start and end apart: 12, of which 6 were waited for; matrix products, arithmetic and copies ran while one was open for 0% of the time, Pallas kernels for 15%

profile of v8, /device:TPU:0, one launch (start us, length us, event | category | flops | bytes accessed | tf_op | source)
XLA Modules:
  0.0 70.7 jit_solution(13522342716180769482)
XLA Ops:
  0.6 1.9 %shard_map.149 = (f32[1,128]{1,0:T(1,128)S(1)}, f32[3,8,512]{2,1,0:T(8,128)S(1)}, f32[3,8,512]{2,1,0:T(8,128)}, f32[8,16,512]{2,1,0:T(8,128)S(1)}, f32[8,16,512]...) custom-call(f32[8,16,512]{2,1,0:T(8,128)} %refs_0_.5, f32[8,16,512]{2,1,0:T(8,128)} %refs_0_.7, ...), custom_call_target="tpu_custom_call" | custom-call | tf_op jit(solution)/shard_map/pallas_call | solution.py:561
  2.6 3.0 %collective-permute-start = (f32[3,8,512]{2,1,0:T(8,128)S(1)}, f32[3,8,512]{2,1,0:T(8,128)S(1)}, u32[]{:S(2)}, u32[]{:S(2)}) collective-permute-start(f32[3,8,512]{2,1,0:T(8,128)S(1)} %get-tuple-element.50), channel_id=1, source_target_pairs={{0,1},{1,0},{2,3},{3,2},{4,5},{5,4},{6,7},{7,6},{8,9},{9,8},{10,11... | collective-permute-start | bytes 147464 | tf_op jit(solution)/shard_map/ppermute | solution.py:578
  5.6 1.5 %shard_map.150 = (f32[64,2048]{1,0:T(8,128)S(1)}, f32[64,2048]{1,0:T(8,128)S(1)}, f32[1,128]{1,0:T(1,128)S(1)}, f32[1,128]{1,0:T(1,128)S(1)}, bf16[208,256]{1,0:...) custom-call(f32[128,2048]{1,0:T(8,128)} %refs_0_.6, ...), custom_call_target="tpu_custom_call" | custom-call | tf_op jit(solution)/shard_map/pallas_call | solution.py:561
  7.1 0.5 collective-permute-done.refs_1_.refs_11_.refs_2_.refs_3_
  7.6 1.0 %shard_map.151 = (f32[32,1,2176]{2,1,0:T(1,128)}, f32[2,24,512]{2,1,0:T(8,128)S(1)}, f32[2,24,512]{2,1,0:T(8,128)S(1)}) custom-call(f32[1,128]{1,0:T(1,128)S(1)} %get-tuple-element.51.refs_0_, f32[3,8,512]{2,1,0:T(8,128)S(1)} %collective-permute-done.refs_1_.refs_11_.refs_2_.refs_3_, ...), custom_call_target="tpu_custom_call" | custom-call | tf_op jit(solution)/shard_map/pallas_call | solution.py:561
  8.6 6.4 %all-to-all-start = ((f32[32,1,2176]{2,1,0:T(1,128)}), f32[32,1,2176]{2,1,0:T(1,128)S(1)}, u32[]{:S(2)}, u32[]{:S(2)}) async-start(f32[32,1,2176]{2,1,0:T(1,128)} %get-tuple-element.58), calls=%async_computation | async-start | bytes 557056 | tf_op jit(solution)/shard_map/all_to_all | solution.py:583
  15.0 1.8 %collective-permute-start.4 = (f32[64,2048]{1,0:T(8,128)S(1)}, f32[64,2048]{1,0:T(8,128)S(1)}, u32[]{:S(2)}, u32[]{:S(2)}) collective-permute-start(f32[64,2048]{1,0:T(8,128)S(1)} %get-tuple-element.53.refs_6_.refs_4_), channel_id=1, source_target_pairs={{0,1},{1,0},{2,3},{3,2},{4,5},{5,4},{6,7},{7,6},{8,9},{9,8},{10,11... | collective-permute-start | bytes 1572872 | tf_op jit(solution)/shard_map/ppermute | solution.py:623
  16.9 0.0 collective-permute-start.1
  16.9 0.7 collective-permute-start.2
  17.5 0.6 collective-permute-done.1.refs_13_.refs_8_
  18.2 0.0 collective-permute-done.2.refs_14_.refs_9_
  18.2 2.8 %shard_map.152.refs_1_.refs_0_ = f32[8,16,512]{2,1,0:T(8,128)S(1)} custom-call(bf16[384,256]{1,0:T(8,128)(2,1)} %constant.29.clone.refs_0_.refs_6_, bf16[384,256]{1,0:T(8,128)(2,1)} %constant.30.clone.refs_1_.refs_7_, f32[208,128]{1,0:T(8,128)} %constant.31.clone.refs_2_.refs_8_, f32[8,384]{1,0:T(8,128)} %constant.32.clone.refs_3_.refs_9_, ...), custom_call_target="tpu_custom_call" | custom-call | tf_op jit(solution)/shard_map/pallas_call | solution.py:561
  20.9 5.1 %all-to-all-done.refs_0_ = f32[32,1,2176]{2,1,0:T(1,128)S(1)} async-done(((f32[32,1,2176]{2,1,0:T(1,128)}), f32[32,1,2176]{2,1,0:T(1,128)S(1)}, u32[]{:S(2)}, u32[]{:S(2)}) %all-to-all-start) | async-done | bytes 278560 | tf_op jit(solution)/shard_map/all_to_all | solution.py:583
  26.0 1.1 %shard_map.153 = (f32[3,8,512]{2,1,0:T(8,128)S(1)}, f32[3,8,512]{2,1,0:T(8,128)}) custom-call(f32[32,1,2176]{2,1,0:T(1,128)S(1)} %all-to-all-done.refs_0_, f32[8,16,512]{2,1,0:T(8,128)S(1)} %shard_map.152.refs_1_.refs_0_, f32[1,128]{1,0:T(1,128)S(1)} %get-tuple-element.57.refs_2_.refs_1_.refs_10_.refs_13_, ...), custom_call_target="tpu_custom_call" | custom-call | tf_op jit(solution)/shard_map/pallas_call | solution.py:561
  27.1 1.0 %collective-permute-start.3 = (f32[3,8,512]{2,1,0:T(8,128)S(1)}, f32[3,8,512]{2,1,0:T(8,128)S(1)}, u32[]{:S(2)}, u32[]{:S(2)}) collective-permute-start(f32[3,8,512]{2,1,0:T(8,128)S(1)} %get-tuple-element.59.refs_3_), channel_id=1, source_target_pairs={{0,1},{1,0},{2,3},{3,2},{4,5},{5,4},{6,7},{7,6},{8,9},{9,8},{10,11... | collective-permute-start | bytes 147464 | tf_op jit(solution)/shard_map/ppermute | solution.py:578
  28.1 5.0 %collective-permute-done.3.refs_4_ = f32[3,8,512]{2,1,0:T(8,128)S(1)} collective-permute-done((f32[3,8,512]{2,1,0:T(8,128)S(1)}, f32[3,8,512]{2,1,0:T(8,128)S(1)}, u32[]{:S(2)}, u32[]{:S(2)}) %collective-permute-start.3) | collective-permute-done | bytes 49184 | tf_op jit(solution)/shard_map/ppermute | solution.py:578
  33.2 0.4 shard_map.154
  33.6 0.1 collective-permute-start.5
  33.7 0.7 collective-permute-start.6
  34.3 1.5 %shard_map.155 = (f32[8,24,512]{2,1,0:T(8,128)S(1)}, f32[1,128]{1,0:T(1,128)S(1)}, bf16[512,256]{1,0:T(8,128)(2,1)S(1)}, f32[8,16,512]{2,1,0:T(8,128)S(1)}) custom-call(f32[8,16,512]{2,1,0:T(8,128)} %refs_0_.7, f32[8,16,512]{2,1,0:T(8,128)S(1)} %get-tuple-element.40.refs_3_.refs_10_.refs_1_.refs_0_, ...), custom_call_target="tpu_custom_call" | custom-call | tf_op jit(solution)/shard_map/pallas_call | solution.py:561
  35.9 0.0 collective-permute-done.4.refs_1_.refs_3_
  35.9 0.0 collective-permute-done.5.refs_6_
  35.9 0.0 collective-permute-done.6.refs_7_
  35.9 1.1 %shard_map.156 = (f32[32,1,2176]{2,1,0:T(1,128)}, f32[10,24,512]{2,1,0:T(8,128)S(1)}, f32[48,512]{1,0:T(8,128)S(1)}) custom-call(f32[64,2048]{1,0:T(8,128)S(1)} %get-tuple-element.52.refs_5_.refs_3_.refs_0_.refs_2_, f32[64,2048]{1,0:T(8,128)S(1)} %collective-permute-done.4.refs_1_.refs_3_, f32[8,24,512]{2,1,0:T(8,128)S(1)} %get-tuple-element.60.refs_2_.refs_10_.refs_3_, ...), custom_call_target="tpu_custom_call" | custom-call | tf_op jit(solution)/shard_map/pallas_call | solution.py:561
  37.0 8.5 %all-to-all-start.1 = ((f32[32,1,2176]{2,1,0:T(1,128)}), f32[32,1,2176]{2,1,0:T(1,128)S(1)}, u32[]{:S(2)}, u32[]{:S(2)}) async-start(f32[32,1,2176]{2,1,0:T(1,128)} %get-tuple-element.67), calls=%async_computation.1 | async-start | bytes 557056 | tf_op jit(solution)/shard_map/all_to_all | solution.py:583
  45.6 3.6 %shard_map.157 = (f32[8,16,512]{2,1,0:T(8,128)S(1)}, f32[8,512]{1,0:T(8,128)S(1)}, f32[8,512]{1,0:T(8,128)}, f32[16,512]{1,0:T(8,128)S(1)}, f32[16,512]{1,0:T(8,128)S(1)}) custom-call(bf16[208,256]{1,0:T(8,128)(2,1)} %constant.10.clone.refs_1_.refs_0_, bf16[208,256]{1,0:T(8,128)(2,1)} %constant.24.clone.refs_2_.refs_1_, ...), custom_call_target="tpu_custom_call" | custom-call | tf_op jit(solution)/shard_map/pallas_call | solution.py:561
  49.2 0.3 collective-permute-start.8
  49.5 0.7 collective-permute-start.9
  50.1 1.7 %collective-permute-start.7 = (f32[8,512]{1,0:T(8,128)S(1)}, f32[8,512]{1,0:T(8,128)S(1)}, u32[]{:S(2)}, u32[]{:S(2)}) collective-permute-start(f32[8,512]{1,0:T(8,128)S(1)} %get-tuple-element.70), channel_id=1, source_target_pairs={{0,1},{1,0},{2,3},{3,2},{4,5},{5,4},{6,7},{7,6},{8,9},{9,8},{10,11... | collective-permute-start | bytes 49160 | tf_op jit(solution)/shard_map/ppermute | solution.py:578
  51.9 2.1 %collective-permute-done.7.refs_6_ = f32[8,512]{1,0:T(8,128)S(1)} collective-permute-done((f32[8,512]{1,0:T(8,128)S(1)}, f32[8,512]{1,0:T(8,128)S(1)}, u32[]{:S(2)}, u32[]{:S(2)}) %collective-permute-start.7) | collective-permute-done | bytes 16416 | tf_op jit(solution)/shard_map/ppermute | solution.py:578
  54.0 0.0 collective-permute-done.8.refs_8_
  54.0 0.0 collective-permute-done.9.refs_9_
  54.0 2.6 %all-to-all-done.1.refs_4_ = f32[32,1,2176]{2,1,0:T(1,128)S(1)} async-done(((f32[32,1,2176]{2,1,0:T(1,128)}), f32[32,1,2176]{2,1,0:T(1,128)S(1)}, u32[]{:S(2)}, u32[]{:S(2)}) %all-to-all-start.1) | async-done | bytes 278560 | tf_op jit(solution)/shard_map/all_to_all | solution.py:583
  56.6 1.0 %shard_map.158 = (f32[8,16,512]{2,1,0:T(8,128)S(1)}, f32[8,16,512]{2,1,0:T(8,128)S(1)}, f32[32,1,256]{2,1,0:T(1,128)S(1)}, f32[1,128]{1,0:T(1,128)S(1)}) custom-call(f32[8,16,512]{2,1,0:T(8,128)S(1)} %get-tuple-element.40.refs_3_.refs_10_.refs_1_.refs_0_, f32[8,16,512]{2,1,0:T(8,128)S(1)} %get-tuple-element.61.refs_1_, ...), custom_call_target="tpu_custom_call" | custom-call | tf_op jit(solution)/shard_map/pallas_call | solution.py:561
  57.6 12.0 %all_to_all.15.refs_2_ = f32[32,1,256]{2,1,0:T(1,128)S(1)} all-to-all(f32[32,1,256]{2,1,0:T(1,128)S(1)} %get-tuple-element.75), channel_id=1, replica_groups=mesh['wide'=16,'narrow'=2] {'wide','narrow'}, dimensions={0} | all-to-all | bytes 65536 | tf_op jit(solution)/shard_map/all_to_all | solution.py:583
  69.6 1.1 %shard_map.159 = (f32[8,16,512]{2,1,0:T(8,128)}, f32[8,16,512]{2,1,0:T(8,128)}) custom-call(f32[8,16,512]{2,1,0:T(8,128)S(1)} %get-tuple-element.40.refs_3_.refs_10_.refs_1_.refs_0_, f32[1,128]{1,0:T(1,128)S(1)} %get-tuple-element.74.refs_1_, f32[32,1,256]{2,1,0:T(1,128)S(1)} %all_to_all.15.refs_2_, ...), custom_call_target="tpu_custom_call" | custom-call | tf_op jit(solution)/shard_map/pallas_call | solution.py:561
  (2 shorter events, 0.0 us)
Async XLA Ops:
  2.6 5.1 %collective-permute-start = (f32[3,8,512]{2,1,0:T(8,128)S(1)}, f32[3,8,512]{2,1,0:T(8,128)S(1)}, u32[]{:S(2)}, u32[]{:S(2)}) collective-permute-start(f32[3,8,512]{2,1,0:T(8,128)S(1)} %get-tuple-element.50), channel_id=1, source_target_pairs={{0,1},{1,0},{2,3},{3,2},{4,5},{5,4},{6,7},{7,6},{8,9},{9,8},{10,11... | collective-permute-start | bytes 147464 | tf_op jit(solution)/shard_map/ppermute | solution.py:578
  8.6 17.4 %all-to-all-start = ((f32[32,1,2176]{2,1,0:T(1,128)}), f32[32,1,2176]{2,1,0:T(1,128)S(1)}, u32[]{:S(2)}, u32[]{:S(2)}) async-start(f32[32,1,2176]{2,1,0:T(1,128)} %get-tuple-element.58), calls=%async_computation | async-start | bytes 557056 | tf_op jit(solution)/shard_map/all_to_all | solution.py:583
  15.0 20.8 %collective-permute-start.4 = (f32[64,2048]{1,0:T(8,128)S(1)}, f32[64,2048]{1,0:T(8,128)S(1)}, u32[]{:S(2)}, u32[]{:S(2)}) collective-permute-start(f32[64,2048]{1,0:T(8,128)S(1)} %get-tuple-element.53.refs_6_.refs_4_), channel_id=1, source_target_pairs={{0,1},{1,0},{2,3},{3,2},{4,5},{5,4},{6,7},{7,6},{8,9},{9,8},{10,11... | collective-permute-start | bytes 1572872 | tf_op jit(solution)/shard_map/ppermute | solution.py:623
  16.9 1.3 %collective-permute-start.1 = (f32[2,24,512]{2,1,0:T(8,128)S(1)}, f32[2,24,512]{2,1,0:T(8,128)S(1)}, u32[]{:S(2)}, u32[]{:S(2)}) collective-permute-start(f32[2,24,512]{2,1,0:T(8,128)S(1)} %get-tuple-element.54), channel_id=1, source_target_pairs={{0,2},{2,0},{4,6},{6,4},{8,10},{10,8},{12,14},{14,12},{16,18},{18,... | collective-permute-start | bytes 294920 | tf_op jit(solution)/shard_map/ppermute | solution.py:578
  16.9 1.3 %collective-permute-start.2 = (f32[2,24,512]{2,1,0:T(8,128)S(1)}, f32[2,24,512]{2,1,0:T(8,128)S(1)}, u32[]{:S(2)}, u32[]{:S(2)}) collective-permute-start(f32[2,24,512]{2,1,0:T(8,128)S(1)} %get-tuple-element.55), channel_id=1, source_target_pairs={{2,4},{4,2},{6,8},{8,6},{10,12},{12,10},{14,16},{16,14},{18,20},{2... | collective-permute-start | bytes 294920 | tf_op jit(solution)/shard_map/ppermute | solution.py:578
  27.1 6.1 %collective-permute-start.3 = (f32[3,8,512]{2,1,0:T(8,128)S(1)}, f32[3,8,512]{2,1,0:T(8,128)S(1)}, u32[]{:S(2)}, u32[]{:S(2)}) collective-permute-start(f32[3,8,512]{2,1,0:T(8,128)S(1)} %get-tuple-element.59.refs_3_), channel_id=1, source_target_pairs={{0,1},{1,0},{2,3},{3,2},{4,5},{5,4},{6,7},{7,6},{8,9},{9,8},{10,11... | collective-permute-start | bytes 147464 | tf_op jit(solution)/shard_map/ppermute | solution.py:578
  33.6 2.3 %collective-permute-start.5 = (f32[2,24,512]{2,1,0:T(8,128)S(1)}, f32[2,24,512]{2,1,0:T(8,128)S(1)}, u32[]{:S(2)}, u32[]{:S(2)}) collective-permute-start(f32[2,24,512]{2,1,0:T(8,128)S(1)} %get-tuple-element.65), channel_id=1, source_target_pairs={{0,2},{2,0},{4,6},{6,4},{8,10},{10,8},{12,14},{14,12},{16,18},{18,... | collective-permute-start | bytes 294920 | tf_op jit(solution)/shard_map/ppermute | solution.py:578
  33.7 2.2 %collective-permute-start.6 = (f32[2,24,512]{2,1,0:T(8,128)S(1)}, f32[2,24,512]{2,1,0:T(8,128)S(1)}, u32[]{:S(2)}, u32[]{:S(2)}) collective-permute-start(f32[2,24,512]{2,1,0:T(8,128)S(1)} %get-tuple-element.66), channel_id=1, source_target_pairs={{2,4},{4,2},{6,8},{8,6},{10,12},{12,10},{14,16},{16,14},{18,20},{2... | collective-permute-start | bytes 294920 | tf_op jit(solution)/shard_map/ppermute | solution.py:578
  37.0 19.6 %all-to-all-start.1 = ((f32[32,1,2176]{2,1,0:T(1,128)}), f32[32,1,2176]{2,1,0:T(1,128)S(1)}, u32[]{:S(2)}, u32[]{:S(2)}) async-start(f32[32,1,2176]{2,1,0:T(1,128)} %get-tuple-element.67), calls=%async_computation.1 | async-start | bytes 557056 | tf_op jit(solution)/shard_map/all_to_all | solution.py:583
  49.2 4.8 %collective-permute-start.8 = (f32[16,512]{1,0:T(8,128)S(1)}, f32[16,512]{1,0:T(8,128)S(1)}, u32[]{:S(2)}, u32[]{:S(2)}) collective-permute-start(f32[16,512]{1,0:T(8,128)S(1)} %get-tuple-element.71), channel_id=1, source_target_pairs={{0,2},{2,0},{4,6},{6,4},{8,10},{10,8},{12,14},{14,12},{16,18},{18,... | collective-permute-start | bytes 98312 | tf_op jit(solution)/shard_map/ppermute | solution.py:578
  49.5 4.5 %collective-permute-start.9 = (f32[16,512]{1,0:T(8,128)S(1)}, f32[16,512]{1,0:T(8,128)S(1)}, u32[]{:S(2)}, u32[]{:S(2)}) collective-permute-start(f32[16,512]{1,0:T(8,128)S(1)} %get-tuple-element.72), channel_id=1, source_target_pairs={{2,4},{4,2},{6,8},{8,6},{10,12},{12,10},{14,16},{16,14},{18,20},{2... | collective-permute-start | bytes 98312 | tf_op jit(solution)/shard_map/ppermute | solution.py:578
  50.1 3.9 %collective-permute-start.7 = (f32[8,512]{1,0:T(8,128)S(1)}, f32[8,512]{1,0:T(8,128)S(1)}, u32[]{:S(2)}, u32[]{:S(2)}) collective-permute-start(f32[8,512]{1,0:T(8,128)S(1)} %get-tuple-element.70), channel_id=1, source_target_pairs={{0,1},{1,0},{2,3},{3,2},{4,5},{5,4},{6,7},{7,6},{8,9},{9,8},{10,11... | collective-permute-start | bytes 49160 | tf_op jit(solution)/shard_map/ppermute | solution.py:578

commit v9 on v8

--- a/solution.py
+++ b/solution.py
@@ -19,6 +19,7 @@
 HZ = 256
 HW = 384
 STAGED = 6
+AGAIN = 2
 TABLES = 10
 KCOL = 2048
 WIDTH = KCOL + 128
@@ -384,7 +385,10 @@
     xa[...], xb[...] = pair_out(w, block[0:2], block[BX - 2 : BX])
 
 
-def interior_kernel(late, diagonal_late, right, search, ya, yb, image, product, table, diagonal):
+def interior_kernel(late, *refs):
+    for source, target in zip(refs[:AGAIN], refs[AGAIN + 9 :]):
+        late.start(source, target)
+    diagonal_late, right, search, ya, yb, image, product, table, diagonal = refs[AGAIN : AGAIN + 9]
     d = lax.axis_index("narrow")
     low, high = pair_in(d, ya[1], yb[1])
     centre = search[...]
@@ -426,7 +430,7 @@
 def second_fine_kernel(late, *rest):
     w, d = lax.axis_index("wide"), lax.axis_index("narrow")
     image, sigma, solved, ya, yb, xa, xb = rest[TABLES:]
-    out = fine_solve(image[...].reshape(YW, BZ), sigma[...], rest[:TABLES])
+    out = fine_solve(image[...].reshape(YW, BZ), sigma[...], rest[TABLES - AGAIN : TABLES] + rest[: TABLES - AGAIN])
     solved[...] = out
     ya[...], yb[...] = pair_out(d, solved[:, 0, :], solved[:, BY - 1, :])
     xa[...], xb[...] = pair_out(w, out[0], out[BX - 1])
@@ -627,8 +631,12 @@
         near=[solved, slots, ya, ta, ra, rb],
     )
     sa, sb = pair_swap(sa, sb, "wide")
-    inner, product, table, diagonal = call(
-        interior_kernel, [extended, (1, 128), gather, block], late=[diagonal_far], near=[right, search, ya, yb]
+    inner, product, table, diagonal, *near = call(
+        interior_kernel,
+        [extended, (1, 128), gather, block, *fine[:AGAIN]],
+        far=fine[:AGAIN],
+        late=[diagonal_far],
+        near=[right, search, ya, yb],
     )
     sums, image, halo = call(
         part(operator_kernel, swapped, sizes),
@@ -637,7 +645,7 @@
     )
     sums = everywhere(sums)
     solved, ya, yb, fa, fb = call(
-        second_fine_kernel, [block, (BX, BZ), (BX, BZ), (BY, BZ), (BY, BZ)], late=fine, near=[image, sigma]
+        second_fine_kernel, [block, (BX, BZ), (BX, BZ), (BY, BZ), (BY, BZ)], late=fine[AGAIN:], near=[*near, image, sigma]
     )
     ya, yb = pair_swap(ya, yb, "narrow")
     fa, fb = pair_swap(fa, fb, "wide")

time: 71.1 us -> 71.1 us (level)
  no operation moved by 1% of the time
where the time goes in v9:
time: 71.1 us; the launch traced here: 70.7 us
  starting transfers between devices  24.8 us (35%)
  Pallas kernels  17.1 us (24%)
  waiting for transfers between devices  16 us (23%)
  blocking collectives  12 us (17%)
  between operations  0.79 us (1%)
    pallas_call x11, Pallas kernels, call(): pl.pallas_call(run, out_shape=[shape_of(getattr(out, 'shape', out), getat...  17.1 us
    all_to_all x2, starting transfers between devices, everywhere(): return lax.all_to_all(rows, AXES, split_axis=0, concat_axis=0, tiled=True)  14.9 us
    all_to_all x1, blocking collectives, everywhere(): return lax.all_to_all(rows, AXES, split_axis=0, concat_axis=0, tiled=True)  12 us
    ppermute x9, waiting for transfers between devices, pair_swap(): lax.ppermute(value, axis, perm)  8.33 us
    ppermute x9, starting transfers between devices, pair_swap(): lax.ppermute(value, axis, perm)  8.14 us
    all_to_all x2, waiting for transfers between devices, everywhere(): return lax.all_to_all(rows, AXES, split_axis=0, concat_axis=0, tiled=True)  7.65 us
    ppermute x1, starting transfers between devices, body(): lax.ppermute(sent, 'narrow', [(0, 1), (1, 0)])  1.83 us
  transfers between devices with their start and end apart: 12, of which 6 were waited for; matrix products, arithmetic and copies ran while one was open for 0% of the time, Pallas kernels for 15%

profile of v9, /device:TPU:0, one launch (start us, length us, event | category | flops | bytes accessed | tf_op | source)
XLA Modules:
  0.0 70.7 jit_solution(2668450448401783287)
XLA Ops:
  0.6 1.9 %shard_map.149 = (f32[1,128]{1,0:T(1,128)S(1)}, f32[3,8,512]{2,1,0:T(8,128)S(1)}, f32[3,8,512]{2,1,0:T(8,128)}, f32[8,16,512]{2,1,0:T(8,128)S(1)}, f32[8,16,512]...) custom-call(f32[8,16,512]{2,1,0:T(8,128)} %refs_0_.5, f32[8,16,512]{2,1,0:T(8,128)} %refs_2_.4, ...), custom_call_target="tpu_custom_call" | custom-call | tf_op jit(solution)/shard_map/pallas_call | solution.py:565
  2.6 3.0 %collective-permute-start = (f32[3,8,512]{2,1,0:T(8,128)S(1)}, f32[3,8,512]{2,1,0:T(8,128)S(1)}, u32[]{:S(2)}, u32[]{:S(2)}) collective-permute-start(f32[3,8,512]{2,1,0:T(8,128)S(1)} %get-tuple-element.52), channel_id=1, source_target_pairs={{0,1},{1,0},{2,3},{3,2},{4,5},{5,4},{6,7},{7,6},{8,9},{9,8},{10,11... | collective-permute-start | bytes 147464 | tf_op jit(solution)/shard_map/ppermute | solution.py:582
  5.6 1.5 %shard_map.150 = (f32[64,2048]{1,0:T(8,128)S(1)}, f32[64,2048]{1,0:T(8,128)S(1)}, f32[1,128]{1,0:T(1,128)S(1)}, f32[1,128]{1,0:T(1,128)S(1)}, bf16[208,256]{1,0:...) custom-call(f32[128,2048]{1,0:T(8,128)} %refs_0_.6, ...), custom_call_target="tpu_custom_call" | custom-call | tf_op jit(solution)/shard_map/pallas_call | solution.py:565
  7.1 0.5 collective-permute-done.refs_1_.refs_11_.refs_2_.refs_5_
  7.6 1.0 %shard_map.151 = (f32[32,1,2176]{2,1,0:T(1,128)}, f32[2,24,512]{2,1,0:T(8,128)S(1)}, f32[2,24,512]{2,1,0:T(8,128)S(1)}) custom-call(f32[1,128]{1,0:T(1,128)S(1)} %get-tuple-element.53.refs_0_, f32[3,8,512]{2,1,0:T(8,128)S(1)} %collective-permute-done.refs_1_.refs_11_.refs_2_.refs_5_, ...), custom_call_target="tpu_custom_call" | custom-call | tf_op jit(solution)/shard_map/pallas_call | solution.py:565
  8.6 6.4 %all-to-all-start = ((f32[32,1,2176]{2,1,0:T(1,128)}), f32[32,1,2176]{2,1,0:T(1,128)S(1)}, u32[]{:S(2)}, u32[]{:S(2)}) async-start(f32[32,1,2176]{2,1,0:T(1,128)} %get-tuple-element.60), calls=%async_computation | async-start | bytes 557056 | tf_op jit(solution)/shard_map/all_to_all | solution.py:587
  15.0 1.8 %collective-permute-start.4 = (f32[64,2048]{1,0:T(8,128)S(1)}, f32[64,2048]{1,0:T(8,128)S(1)}, u32[]{:S(2)}, u32[]{:S(2)}) collective-permute-start(f32[64,2048]{1,0:T(8,128)S(1)} %get-tuple-element.55.refs_6_.refs_4_), channel_id=1, source_target_pairs={{0,1},{1,0},{2,3},{3,2},{4,5},{5,4},{6,7},{7,6},{8,9},{9,8},{10,11... | collective-permute-start | bytes 1572872 | tf_op jit(solution)/shard_map/ppermute | solution.py:627
  16.9 0.0 collective-permute-start.1
  16.9 0.7 collective-permute-start.2
  17.5 0.6 collective-permute-done.1.refs_13_.refs_8_
  18.2 0.0 collective-permute-done.2.refs_14_.refs_9_
  18.2 2.8 %shard_map.152.refs_1_.refs_0_ = f32[8,16,512]{2,1,0:T(8,128)S(1)} custom-call(bf16[384,256]{1,0:T(8,128)(2,1)} %constant.29.clone.refs_0_.refs_4_, bf16[384,256]{1,0:T(8,128)(2,1)} %constant.30.clone.refs_1_.refs_5_, f32[208,128]{1,0:T(8,128)} %constant.31.clone.refs_2_.refs_6_, f32[8,384]{1,0:T(8,128)} %constant.32.clone.refs_3_.refs_7_, ...), custom_call_target="tpu_custom_call" | custom-call | tf_op jit(solution)/shard_map/pallas_call | solution.py:565
  20.9 5.1 %all-to-all-done.refs_0_ = f32[32,1,2176]{2,1,0:T(1,128)S(1)} async-done(((f32[32,1,2176]{2,1,0:T(1,128)}), f32[32,1,2176]{2,1,0:T(1,128)S(1)}, u32[]{:S(2)}, u32[]{:S(2)}) %all-to-all-start) | async-done | bytes 278560 | tf_op jit(solution)/shard_map/all_to_all | solution.py:587
  26.0 1.1 %shard_map.153 = (f32[3,8,512]{2,1,0:T(8,128)S(1)}, f32[3,8,512]{2,1,0:T(8,128)}) custom-call(f32[32,1,2176]{2,1,0:T(1,128)S(1)} %all-to-all-done.refs_0_, f32[8,16,512]{2,1,0:T(8,128)S(1)} %shard_map.152.refs_1_.refs_0_, f32[1,128]{1,0:T(1,128)S(1)} %get-tuple-element.59.refs_2_.refs_1_.refs_10_.refs_13_, ...), custom_call_target="tpu_custom_call" | custom-call | tf_op jit(solution)/shard_map/pallas_call | solution.py:565
  27.1 1.0 %collective-permute-start.3 = (f32[3,8,512]{2,1,0:T(8,128)S(1)}, f32[3,8,512]{2,1,0:T(8,128)S(1)}, u32[]{:S(2)}, u32[]{:S(2)}) collective-permute-start(f32[3,8,512]{2,1,0:T(8,128)S(1)} %get-tuple-element.61.refs_3_), channel_id=1, source_target_pairs={{0,1},{1,0},{2,3},{3,2},{4,5},{5,4},{6,7},{7,6},{8,9},{9,8},{10,11... | collective-permute-start | bytes 147464 | tf_op jit(solution)/shard_map/ppermute | solution.py:582
  28.1 5.0 %collective-permute-done.3.refs_4_ = f32[3,8,512]{2,1,0:T(8,128)S(1)} collective-permute-done((f32[3,8,512]{2,1,0:T(8,128)S(1)}, f32[3,8,512]{2,1,0:T(8,128)S(1)}, u32[]{:S(2)}, u32[]{:S(2)}) %collective-permute-start.3) | collective-permute-done | bytes 49184 | tf_op jit(solution)/shard_map/ppermute | solution.py:582
  33.2 0.4 shard_map.154
  33.6 0.1 collective-permute-start.5
  33.7 0.7 collective-permute-start.6
  34.3 1.5 %shard_map.155 = (f32[8,24,512]{2,1,0:T(8,128)S(1)}, f32[1,128]{1,0:T(1,128)S(1)}, bf16[512,256]{1,0:T(8,128)(2,1)S(1)}, f32[8,16,512]{2,1,0:T(8,128)S(1)}, bf16...) custom-call(bf16[208,256]{1,0:T(8,128)(2,1)} %constant.10.clone.refs_1_.refs_0_, ...), custom_call_target="tpu_custom_call" | custom-call | tf_op jit(solution)/shard_map/pallas_call | solution.py:565
  35.9 0.0 collective-permute-done.4.refs_1_.refs_3_
  35.9 0.0 collective-permute-done.5.refs_6_
  35.9 0.0 collective-permute-done.6.refs_7_
  35.9 1.1 %shard_map.156 = (f32[32,1,2176]{2,1,0:T(1,128)}, f32[10,24,512]{2,1,0:T(8,128)S(1)}, f32[48,512]{1,0:T(8,128)S(1)}) custom-call(f32[64,2048]{1,0:T(8,128)S(1)} %get-tuple-element.54.refs_5_.refs_3_.refs_0_.refs_2_, f32[64,2048]{1,0:T(8,128)S(1)} %collective-permute-done.4.refs_1_.refs_3_, ...), custom_call_target="tpu_custom_call" | custom-call | tf_op jit(solution)/shard_map/pallas_call | solution.py:565
  37.1 8.5 %all-to-all-start.1 = ((f32[32,1,2176]{2,1,0:T(1,128)}), f32[32,1,2176]{2,1,0:T(1,128)S(1)}, u32[]{:S(2)}, u32[]{:S(2)}) async-start(f32[32,1,2176]{2,1,0:T(1,128)} %get-tuple-element.69), calls=%async_computation.1 | async-start | bytes 557056 | tf_op jit(solution)/shard_map/all_to_all | solution.py:587
  45.5 3.6 %shard_map.157 = (f32[8,16,512]{2,1,0:T(8,128)S(1)}, f32[8,512]{1,0:T(8,128)S(1)}, f32[8,512]{1,0:T(8,128)}, f32[16,512]{1,0:T(8,128)S(1)}, f32[16,512]{1,0:T(8,128)S(1)}) custom-call(bf16[256,384]{1,0:T(8,128)(2,1)} %constant.25.clone.refs_3_.refs_0_, bf16[256,384]{1,0:T(8,128)(2,1)} %constant.26.clone.refs_4_.refs_1_, ...), custom_call_target="tpu_custom_call" | custom-call | tf_op jit(solution)/shard_map/pallas_call | solution.py:565
  49.2 0.3 collective-permute-start.8
  49.5 0.7 collective-permute-start.9
  50.1 1.7 %collective-permute-start.7 = (f32[8,512]{1,0:T(8,128)S(1)}, f32[8,512]{1,0:T(8,128)S(1)}, u32[]{:S(2)}, u32[]{:S(2)}) collective-permute-start(f32[8,512]{1,0:T(8,128)S(1)} %get-tuple-element.74), channel_id=1, source_target_pairs={{0,1},{1,0},{2,3},{3,2},{4,5},{5,4},{6,7},{7,6},{8,9},{9,8},{10,11... | collective-permute-start | bytes 49160 | tf_op jit(solution)/shard_map/ppermute | solution.py:582
  51.9 2.1 %collective-permute-done.7.refs_6_ = f32[8,512]{1,0:T(8,128)S(1)} collective-permute-done((f32[8,512]{1,0:T(8,128)S(1)}, f32[8,512]{1,0:T(8,128)S(1)}, u32[]{:S(2)}, u32[]{:S(2)}) %collective-permute-start.7) | collective-permute-done | bytes 16416 | tf_op jit(solution)/shard_map/ppermute | solution.py:582
  54.0 0.0 collective-permute-done.8.refs_8_
  54.0 0.0 collective-permute-done.9.refs_9_
  54.0 2.6 %all-to-all-done.1.refs_4_ = f32[32,1,2176]{2,1,0:T(1,128)S(1)} async-done(((f32[32,1,2176]{2,1,0:T(1,128)}), f32[32,1,2176]{2,1,0:T(1,128)S(1)}, u32[]{:S(2)}, u32[]{:S(2)}) %all-to-all-start.1) | async-done | bytes 278560 | tf_op jit(solution)/shard_map/all_to_all | solution.py:587
  56.6 1.0 %shard_map.158 = (f32[8,16,512]{2,1,0:T(8,128)S(1)}, f32[8,16,512]{2,1,0:T(8,128)S(1)}, f32[32,1,256]{2,1,0:T(1,128)S(1)}, f32[1,128]{1,0:T(1,128)S(1)}) custom-call(f32[8,16,512]{2,1,0:T(8,128)S(1)} %get-tuple-element.42.refs_3_.refs_10_.refs_0_, f32[8,16,512]{2,1,0:T(8,128)S(1)} %get-tuple-element.63.refs_1_, ...), custom_call_target="tpu_custom_call" | custom-call | tf_op jit(solution)/shard_map/pallas_call | solution.py:565
  57.6 12.0 %all_to_all.15.refs_2_ = f32[32,1,256]{2,1,0:T(1,128)S(1)} all-to-all(f32[32,1,256]{2,1,0:T(1,128)S(1)} %get-tuple-element.79), channel_id=1, replica_groups=mesh['wide'=16,'narrow'=2] {'wide','narrow'}, dimensions={0} | all-to-all | bytes 65536 | tf_op jit(solution)/shard_map/all_to_all | solution.py:587
  69.6 1.1 %shard_map.159 = (f32[8,16,512]{2,1,0:T(8,128)}, f32[8,16,512]{2,1,0:T(8,128)}) custom-call(f32[8,16,512]{2,1,0:T(8,128)S(1)} %get-tuple-element.42.refs_3_.refs_10_.refs_0_, f32[1,128]{1,0:T(1,128)S(1)} %get-tuple-element.78.refs_1_, f32[32,1,256]{2,1,0:T(1,128)S(1)} %all_to_all.15.refs_2_, ...), custom_call_target="tpu_custom_call" | custom-call | tf_op jit(solution)/shard_map/pallas_call | solution.py:565
  (2 shorter events, 0.0 us)
Async XLA Ops:
  2.6 5.1 %collective-permute-start = (f32[3,8,512]{2,1,0:T(8,128)S(1)}, f32[3,8,512]{2,1,0:T(8,128)S(1)}, u32[]{:S(2)}, u32[]{:S(2)}) collective-permute-start(f32[3,8,512]{2,1,0:T(8,128)S(1)} %get-tuple-element.52), channel_id=1, source_target_pairs={{0,1},{1,0},{2,3},{3,2},{4,5},{5,4},{6,7},{7,6},{8,9},{9,8},{10,11... | collective-permute-start | bytes 147464 | tf_op jit(solution)/shard_map/ppermute | solution.py:582
  8.6 17.4 %all-to-all-start = ((f32[32,1,2176]{2,1,0:T(1,128)}), f32[32,1,2176]{2,1,0:T(1,128)S(1)}, u32[]{:S(2)}, u32[]{:S(2)}) async-start(f32[32,1,2176]{2,1,0:T(1,128)} %get-tuple-element.60), calls=%async_computation | async-start | bytes 557056 | tf_op jit(solution)/shard_map/all_to_all | solution.py:587
  15.0 20.9 %collective-permute-start.4 = (f32[64,2048]{1,0:T(8,128)S(1)}, f32[64,2048]{1,0:T(8,128)S(1)}, u32[]{:S(2)}, u32[]{:S(2)}) collective-permute-start(f32[64,2048]{1,0:T(8,128)S(1)} %get-tuple-element.55.refs_6_.refs_4_), channel_id=1, source_target_pairs={{0,1},{1,0},{2,3},{3,2},{4,5},{5,4},{6,7},{7,6},{8,9},{9,8},{10,11... | collective-permute-start | bytes 1572872 | tf_op jit(solution)/shard_map/ppermute | solution.py:627
  16.9 1.3 %collective-permute-start.1 = (f32[2,24,512]{2,1,0:T(8,128)S(1)}, f32[2,24,512]{2,1,0:T(8,128)S(1)}, u32[]{:S(2)}, u32[]{:S(2)}) collective-permute-start(f32[2,24,512]{2,1,0:T(8,128)S(1)} %get-tuple-element.56), channel_id=1, source_target_pairs={{0,2},{2,0},{4,6},{6,4},{8,10},{10,8},{12,14},{14,12},{16,18},{18,... | collective-permute-start | bytes 294920 | tf_op jit(solution)/shard_map/ppermute | solution.py:582
  16.9 1.3 %collective-permute-start.2 = (f32[2,24,512]{2,1,0:T(8,128)S(1)}, f32[2,24,512]{2,1,0:T(8,128)S(1)}, u32[]{:S(2)}, u32[]{:S(2)}) collective-permute-start(f32[2,24,512]{2,1,0:T(8,128)S(1)} %get-tuple-element.57), channel_id=1, source_target_pairs={{2,4},{4,2},{6,8},{8,6},{10,12},{12,10},{14,16},{16,14},{18,20},{2... | collective-permute-start | bytes 294920 | tf_op jit(solution)/shard_map/ppermute | solution.py:582
  27.1 6.1 %collective-permute-start.3 = (f32[3,8,512]{2,1,0:T(8,128)S(1)}, f32[3,8,512]{2,1,0:T(8,128)S(1)}, u32[]{:S(2)}, u32[]{:S(2)}) collective-permute-start(f32[3,8,512]{2,1,0:T(8,128)S(1)} %get-tuple-element.61.refs_3_), channel_id=1, source_target_pairs={{0,1},{1,0},{2,3},{3,2},{4,5},{5,4},{6,7},{7,6},{8,9},{9,8},{10,11... | collective-permute-start | bytes 147464 | tf_op jit(solution)/shard_map/ppermute | solution.py:582
  33.6 2.3 %collective-permute-start.5 = (f32[2,24,512]{2,1,0:T(8,128)S(1)}, f32[2,24,512]{2,1,0:T(8,128)S(1)}, u32[]{:S(2)}, u32[]{:S(2)}) collective-permute-start(f32[2,24,512]{2,1,0:T(8,128)S(1)} %get-tuple-element.67), channel_id=1, source_target_pairs={{0,2},{2,0},{4,6},{6,4},{8,10},{10,8},{12,14},{14,12},{16,18},{18,... | collective-permute-start | bytes 294920 | tf_op jit(solution)/shard_map/ppermute | solution.py:582
  33.7 2.2 %collective-permute-start.6 = (f32[2,24,512]{2,1,0:T(8,128)S(1)}, f32[2,24,512]{2,1,0:T(8,128)S(1)}, u32[]{:S(2)}, u32[]{:S(2)}) collective-permute-start(f32[2,24,512]{2,1,0:T(8,128)S(1)} %get-tuple-element.68), channel_id=1, source_target_pairs={{2,4},{4,2},{6,8},{8,6},{10,12},{12,10},{14,16},{16,14},{18,20},{2... | collective-permute-start | bytes 294920 | tf_op jit(solution)/shard_map/ppermute | solution.py:582
  37.1 19.5 %all-to-all-start.1 = ((f32[32,1,2176]{2,1,0:T(1,128)}), f32[32,1,2176]{2,1,0:T(1,128)S(1)}, u32[]{:S(2)}, u32[]{:S(2)}) async-start(f32[32,1,2176]{2,1,0:T(1,128)} %get-tuple-element.69), calls=%async_computation.1 | async-start | bytes 557056 | tf_op jit(solution)/shard_map/all_to_all | solution.py:587
  49.2 4.8 %collective-permute-start.8 = (f32[16,512]{1,0:T(8,128)S(1)}, f32[16,512]{1,0:T(8,128)S(1)}, u32[]{:S(2)}, u32[]{:S(2)}) collective-permute-start(f32[16,512]{1,0:T(8,128)S(1)} %get-tuple-element.75), channel_id=1, source_target_pairs={{0,2},{2,0},{4,6},{6,4},{8,10},{10,8},{12,14},{14,12},{16,18},{18,... | collective-permute-start | bytes 98312 | tf_op jit(solution)/shard_map/ppermute | solution.py:582
  49.5 4.5 %collective-permute-start.9 = (f32[16,512]{1,0:T(8,128)S(1)}, f32[16,512]{1,0:T(8,128)S(1)}, u32[]{:S(2)}, u32[]{:S(2)}) collective-permute-start(f32[16,512]{1,0:T(8,128)S(1)} %get-tuple-element.76), channel_id=1, source_target_pairs={{2,4},{4,2},{6,8},{8,6},{10,12},{12,10},{14,16},{16,14},{18,20},{2... | collective-permute-start | bytes 98312 | tf_op jit(solution)/shard_map/ppermute | solution.py:582
  50.1 3.9 %collective-permute-start.7 = (f32[8,512]{1,0:T(8,128)S(1)}, f32[8,512]{1,0:T(8,128)S(1)}, u32[]{:S(2)}, u32[]{:S(2)}) collective-permute-start(f32[8,512]{1,0:T(8,128)S(1)} %get-tuple-element.74), channel_id=1, source_target_pairs={{0,1},{1,0},{2,3},{3,2},{4,5},{5,4},{6,7},{7,6},{8,9},{9,8},{10,11... | collective-permute-start | bytes 49160 | tf_op jit(solution)/shard_map/ppermute | solution.py:582

commit v10 on v8

--- a/solution.py
+++ b/solution.py
@@ -317,7 +317,7 @@
         row = jnp.where(d == 0, row, pltpu.roll(row, half, 1))
         other = jnp.where(d == 0, pltpu.roll(other, half, 1), other)
         row = jnp.where(iota((1, ELEMS), 1) < half, row, other)
-    store_sum(sums, project(row_to_column(row), (kept, sent)), jnp.zeros((1, 128), F32))
+    sums[...] = jnp.broadcast_to(project(row_to_column(row), (kept, sent))[None], sums.shape)
     for i, ref in enumerate((right, diagonal)):
         low, high = pair_in(d, ra[i], rb[i])
         layers = [extend_y(ref[x : x + 1], [low[x : x + 1]], [high[x : x + 1]], 1)[0] for x in (0, BX - 1)]
@@ -613,7 +613,7 @@
         near=[c, diagonal, table],
     )
     sums, xa, xb = call(
-        part(project_kernel, swapped), [(count, 1, WIDTH), x_shape, x_shape], near=[c, ya, yb, right, diagonal, kept, sent]
+        part(project_kernel, swapped), [(count, 1, KCOL), x_shape, x_shape], near=[c, ya, yb, right, diagonal, kept, sent]
     )
     sums = everywhere(sums)
     xa, xb = pair_swap(xa, xb, "wide")

time: 71.1 us -> 70.9 us (level)
  no operation moved by 1% of the time
where the time goes in v10:
time: 70.9 us; the launch traced here: 70.5 us
  starting transfers between devices  24.7 us (35%)
  Pallas kernels  17 us (24%)
  waiting for transfers between devices  16 us (23%)
  blocking collectives  12 us (17%)
  between operations  0.79 us (1%)
    pallas_call x11, Pallas kernels, call(): pl.pallas_call(run, out_shape=[shape_of(getattr(out, 'shape', out), getat...  17 us
    all_to_all x2, starting transfers between devices, everywhere(): return lax.all_to_all(rows, AXES, split_axis=0, concat_axis=0, tiled=True)  14.9 us
    all_to_all x1, blocking collectives, everywhere(): return lax.all_to_all(rows, AXES, split_axis=0, concat_axis=0, tiled=True)  12 us
    ppermute x9, waiting for transfers between devices, pair_swap(): lax.ppermute(value, axis, perm)  8.58 us
    ppermute x9, starting transfers between devices, pair_swap(): lax.ppermute(value, axis, perm)  7.97 us
    all_to_all x2, waiting for transfers between devices, everywhere(): return lax.all_to_all(rows, AXES, split_axis=0, concat_axis=0, tiled=True)  7.38 us
    ppermute x1, starting transfers between devices, body(): lax.ppermute(sent, 'narrow', [(0, 1), (1, 0)])  1.83 us
  transfers between devices with their start and end apart: 12, of which 6 were waited for; matrix products, arithmetic and copies ran while one was open for 0% of the time, Pallas kernels for 15%

profile of v10, /device:TPU:0, one launch (start us, length us, event | category | flops | bytes accessed | tf_op | source)
XLA Modules:
  0.0 70.5 jit_solution(11826131078683840610)
XLA Ops:
  0.6 1.9 %shard_map.149 = (f32[1,128]{1,0:T(1,128)S(1)}, f32[3,8,512]{2,1,0:T(8,128)S(1)}, f32[3,8,512]{2,1,0:T(8,128)}, f32[8,16,512]{2,1,0:T(8,128)S(1)}, f32[8,16,512]...) custom-call(f32[8,16,512]{2,1,0:T(8,128)} %refs_0_.5, f32[8,16,512]{2,1,0:T(8,128)} %refs_0_.7, ...), custom_call_target="tpu_custom_call" | custom-call | tf_op jit(solution)/shard_map/pallas_call | solution.py:561
  2.6 3.0 %collective-permute-start = (f32[3,8,512]{2,1,0:T(8,128)S(1)}, f32[3,8,512]{2,1,0:T(8,128)S(1)}, u32[]{:S(2)}, u32[]{:S(2)}) collective-permute-start(f32[3,8,512]{2,1,0:T(8,128)S(1)} %get-tuple-element.50), channel_id=1, source_target_pairs={{0,1},{1,0},{2,3},{3,2},{4,5},{5,4},{6,7},{7,6},{8,9},{9,8},{10,11... | collective-permute-start | bytes 147464 | tf_op jit(solution)/shard_map/ppermute | solution.py:578
  5.6 1.5 %shard_map.150 = (f32[64,2048]{1,0:T(8,128)S(1)}, f32[64,2048]{1,0:T(8,128)S(1)}, f32[1,128]{1,0:T(1,128)S(1)}, f32[1,128]{1,0:T(1,128)S(1)}, bf16[208,256]{1,0:...) custom-call(f32[128,2048]{1,0:T(8,128)} %refs_0_.6, ...), custom_call_target="tpu_custom_call" | custom-call | tf_op jit(solution)/shard_map/pallas_call | solution.py:561
  7.1 0.5 collective-permute-done.refs_1_.refs_11_.refs_2_.refs_3_
  7.6 1.0 %shard_map.151 = (f32[32,1,2048]{2,1,0:T(1,128)}, f32[2,24,512]{2,1,0:T(8,128)S(1)}, f32[2,24,512]{2,1,0:T(8,128)S(1)}) custom-call(f32[1,128]{1,0:T(1,128)S(1)} %get-tuple-element.51.refs_0_, f32[3,8,512]{2,1,0:T(8,128)S(1)} %collective-permute-done.refs_1_.refs_11_.refs_2_.refs_3_, ...), custom_call_target="tpu_custom_call" | custom-call | tf_op jit(solution)/shard_map/pallas_call | solution.py:561
  8.6 6.4 %all-to-all-start = ((f32[32,1,2048]{2,1,0:T(1,128)}), f32[32,1,2048]{2,1,0:T(1,128)S(1)}, u32[]{:S(2)}, u32[]{:S(2)}) async-start(f32[32,1,2048]{2,1,0:T(1,128)} %get-tuple-element.58), calls=%async_computation | async-start | bytes 524288 | tf_op jit(solution)/shard_map/all_to_all | solution.py:583
  15.0 1.8 %collective-permute-start.4 = (f32[64,2048]{1,0:T(8,128)S(1)}, f32[64,2048]{1,0:T(8,128)S(1)}, u32[]{:S(2)}, u32[]{:S(2)}) collective-permute-start(f32[64,2048]{1,0:T(8,128)S(1)} %get-tuple-element.53.refs_6_.refs_4_), channel_id=1, source_target_pairs={{0,1},{1,0},{2,3},{3,2},{4,5},{5,4},{6,7},{7,6},{8,9},{9,8},{10,11... | collective-permute-start | bytes 1572872 | tf_op jit(solution)/shard_map/ppermute | solution.py:623
  16.9 0.0 collective-permute-start.1
  16.9 0.7 collective-permute-start.2
  17.5 0.6 collective-permute-done.1.refs_13_.refs_8_
  18.2 0.0 collective-permute-done.2.refs_14_.refs_9_
  18.2 2.8 %shard_map.152.refs_1_.refs_0_ = f32[8,16,512]{2,1,0:T(8,128)S(1)} custom-call(bf16[384,256]{1,0:T(8,128)(2,1)} %constant.29.clone.refs_0_.refs_6_, bf16[384,256]{1,0:T(8,128)(2,1)} %constant.30.clone.refs_1_.refs_7_, f32[208,128]{1,0:T(8,128)} %constant.31.clone.refs_2_.refs_8_, f32[8,384]{1,0:T(8,128)} %constant.32.clone.refs_3_.refs_9_, ...), custom_call_target="tpu_custom_call" | custom-call | tf_op jit(solution)/shard_map/pallas_call | solution.py:561
  20.9 4.8 %all-to-all-done.refs_0_ = f32[32,1,2048]{2,1,0:T(1,128)S(1)} async-done(((f32[32,1,2048]{2,1,0:T(1,128)}), f32[32,1,2048]{2,1,0:T(1,128)S(1)}, u32[]{:S(2)}, u32[]{:S(2)}) %all-to-all-start) | async-done | bytes 262176 | tf_op jit(solution)/shard_map/all_to_all | solution.py:583
  25.7 1.1 %shard_map.153 = (f32[3,8,512]{2,1,0:T(8,128)S(1)}, f32[3,8,512]{2,1,0:T(8,128)}) custom-call(f32[32,1,2048]{2,1,0:T(1,128)S(1)} %all-to-all-done.refs_0_, f32[8,16,512]{2,1,0:T(8,128)S(1)} %shard_map.152.refs_1_.refs_0_, f32[1,128]{1,0:T(1,128)S(1)} %get-tuple-element.57.refs_2_.refs_1_.refs_10_.refs_13_, ...), custom_call_target="tpu_custom_call" | custom-call | tf_op jit(solution)/shard_map/pallas_call | solution.py:561
  26.8 0.9 %collective-permute-start.3 = (f32[3,8,512]{2,1,0:T(8,128)S(1)}, f32[3,8,512]{2,1,0:T(8,128)S(1)}, u32[]{:S(2)}, u32[]{:S(2)}) collective-permute-start(f32[3,8,512]{2,1,0:T(8,128)S(1)} %get-tuple-element.59.refs_3_), channel_id=1, source_target_pairs={{0,1},{1,0},{2,3},{3,2},{4,5},{5,4},{6,7},{7,6},{8,9},{9,8},{10,11... | collective-permute-start | bytes 147464 | tf_op jit(solution)/shard_map/ppermute | solution.py:578
  27.7 5.3 %collective-permute-done.3.refs_4_ = f32[3,8,512]{2,1,0:T(8,128)S(1)} collective-permute-done((f32[3,8,512]{2,1,0:T(8,128)S(1)}, f32[3,8,512]{2,1,0:T(8,128)S(1)}, u32[]{:S(2)}, u32[]{:S(2)}) %collective-permute-start.3) | collective-permute-done | bytes 49184 | tf_op jit(solution)/shard_map/ppermute | solution.py:578
  33.0 0.4 shard_map.154
  33.4 0.1 collective-permute-start.5
  33.5 0.7 collective-permute-start.6
  34.2 1.5 %shard_map.155 = (f32[8,24,512]{2,1,0:T(8,128)S(1)}, f32[1,128]{1,0:T(1,128)S(1)}, bf16[512,256]{1,0:T(8,128)(2,1)S(1)}, f32[8,16,512]{2,1,0:T(8,128)S(1)}) custom-call(f32[8,16,512]{2,1,0:T(8,128)} %refs_0_.7, f32[8,16,512]{2,1,0:T(8,128)S(1)} %get-tuple-element.40.refs_3_.refs_10_.refs_1_.refs_0_, ...), custom_call_target="tpu_custom_call" | custom-call | tf_op jit(solution)/shard_map/pallas_call | solution.py:561
  35.7 0.0 collective-permute-done.4.refs_1_.refs_3_
  35.7 0.0 collective-permute-done.5.refs_6_
  35.7 0.0 collective-permute-done.6.refs_7_
  35.7 1.1 %shard_map.156 = (f32[32,1,2176]{2,1,0:T(1,128)}, f32[10,24,512]{2,1,0:T(8,128)S(1)}, f32[48,512]{1,0:T(8,128)S(1)}) custom-call(f32[64,2048]{1,0:T(8,128)S(1)} %get-tuple-element.52.refs_5_.refs_3_.refs_0_.refs_2_, f32[64,2048]{1,0:T(8,128)S(1)} %collective-permute-done.4.refs_1_.refs_3_, f32[8,24,512]{2,1,0:T(8,128)S(1)} %get-tuple-element.60.refs_2_.refs_10_.refs_3_, ...), custom_call_target="tpu_custom_call" | custom-call | tf_op jit(solution)/shard_map/pallas_call | solution.py:561
  36.9 8.5 %all-to-all-start.1 = ((f32[32,1,2176]{2,1,0:T(1,128)}), f32[32,1,2176]{2,1,0:T(1,128)S(1)}, u32[]{:S(2)}, u32[]{:S(2)}) async-start(f32[32,1,2176]{2,1,0:T(1,128)} %get-tuple-element.67), calls=%async_computation.1 | async-start | bytes 557056 | tf_op jit(solution)/shard_map/all_to_all | solution.py:583
  45.4 3.6 %shard_map.157 = (f32[8,16,512]{2,1,0:T(8,128)S(1)}, f32[8,512]{1,0:T(8,128)S(1)}, f32[8,512]{1,0:T(8,128)}, f32[16,512]{1,0:T(8,128)S(1)}, f32[16,512]{1,0:T(8,128)S(1)}) custom-call(bf16[208,256]{1,0:T(8,128)(2,1)} %constant.10.clone.refs_1_.refs_0_, bf16[208,256]{1,0:T(8,128)(2,1)} %constant.24.clone.refs_2_.refs_1_, ...), custom_call_target="tpu_custom_call" | custom-call | tf_op jit(solution)/shard_map/pallas_call | solution.py:561
  49.0 0.3 collective-permute-start.8
  49.3 0.7 collective-permute-start.9
  50.0 1.7 %collective-permute-start.7 = (f32[8,512]{1,0:T(8,128)S(1)}, f32[8,512]{1,0:T(8,128)S(1)}, u32[]{:S(2)}, u32[]{:S(2)}) collective-permute-start(f32[8,512]{1,0:T(8,128)S(1)} %get-tuple-element.70), channel_id=1, source_target_pairs={{0,1},{1,0},{2,3},{3,2},{4,5},{5,4},{6,7},{7,6},{8,9},{9,8},{10,11... | collective-permute-start | bytes 49160 | tf_op jit(solution)/shard_map/ppermute | solution.py:578
  51.7 2.1 %collective-permute-done.7.refs_6_ = f32[8,512]{1,0:T(8,128)S(1)} collective-permute-done((f32[8,512]{1,0:T(8,128)S(1)}, f32[8,512]{1,0:T(8,128)S(1)}, u32[]{:S(2)}, u32[]{:S(2)}) %collective-permute-start.7) | collective-permute-done | bytes 16416 | tf_op jit(solution)/shard_map/ppermute | solution.py:578
  53.8 0.0 collective-permute-done.8.refs_8_
  53.8 0.0 collective-permute-done.9.refs_9_
  53.8 2.6 %all-to-all-done.1.refs_4_ = f32[32,1,2176]{2,1,0:T(1,128)S(1)} async-done(((f32[32,1,2176]{2,1,0:T(1,128)}), f32[32,1,2176]{2,1,0:T(1,128)S(1)}, u32[]{:S(2)}, u32[]{:S(2)}) %all-to-all-start.1) | async-done | bytes 278560 | tf_op jit(solution)/shard_map/all_to_all | solution.py:583
  56.4 1.0 %shard_map.158 = (f32[8,16,512]{2,1,0:T(8,128)S(1)}, f32[8,16,512]{2,1,0:T(8,128)S(1)}, f32[32,1,256]{2,1,0:T(1,128)S(1)}, f32[1,128]{1,0:T(1,128)S(1)}) custom-call(f32[8,16,512]{2,1,0:T(8,128)S(1)} %get-tuple-element.40.refs_3_.refs_10_.refs_1_.refs_0_, f32[8,16,512]{2,1,0:T(8,128)S(1)} %get-tuple-element.61.refs_1_, ...), custom_call_target="tpu_custom_call" | custom-call | tf_op jit(solution)/shard_map/pallas_call | solution.py:561
  57.4 12.0 %all_to_all.15.refs_2_ = f32[32,1,256]{2,1,0:T(1,128)S(1)} all-to-all(f32[32,1,256]{2,1,0:T(1,128)S(1)} %get-tuple-element.75), channel_id=1, replica_groups=mesh['wide'=16,'narrow'=2] {'wide','narrow'}, dimensions={0} | all-to-all | bytes 65536 | tf_op jit(solution)/shard_map/all_to_all | solution.py:583
  69.4 1.1 %shard_map.159 = (f32[8,16,512]{2,1,0:T(8,128)}, f32[8,16,512]{2,1,0:T(8,128)}) custom-call(f32[8,16,512]{2,1,0:T(8,128)S(1)} %get-tuple-element.40.refs_3_.refs_10_.refs_1_.refs_0_, f32[1,128]{1,0:T(1,128)S(1)} %get-tuple-element.74.refs_1_, f32[32,1,256]{2,1,0:T(1,128)S(1)} %all_to_all.15.refs_2_, ...), custom_call_target="tpu_custom_call" | custom-call | tf_op jit(solution)/shard_map/pallas_call | solution.py:561
  (2 shorter events, 0.0 us)
Async XLA Ops:
  2.6 5.1 %collective-permute-start = (f32[3,8,512]{2,1,0:T(8,128)S(1)}, f32[3,8,512]{2,1,0:T(8,128)S(1)}, u32[]{:S(2)}, u32[]{:S(2)}) collective-permute-start(f32[3,8,512]{2,1,0:T(8,128)S(1)} %get-tuple-element.50), channel_id=1, source_target_pairs={{0,1},{1,0},{2,3},{3,2},{4,5},{5,4},{6,7},{7,6},{8,9},{9,8},{10,11... | collective-permute-start | bytes 147464 | tf_op jit(solution)/shard_map/ppermute | solution.py:578
  8.6 17.1 %all-to-all-start = ((f32[32,1,2048]{2,1,0:T(1,128)}), f32[32,1,2048]{2,1,0:T(1,128)S(1)}, u32[]{:S(2)}, u32[]{:S(2)}) async-start(f32[32,1,2048]{2,1,0:T(1,128)} %get-tuple-element.58), calls=%async_computation | async-start | bytes 524288 | tf_op jit(solution)/shard_map/all_to_all | solution.py:583
  15.0 20.7 %collective-permute-start.4 = (f32[64,2048]{1,0:T(8,128)S(1)}, f32[64,2048]{1,0:T(8,128)S(1)}, u32[]{:S(2)}, u32[]{:S(2)}) collective-permute-start(f32[64,2048]{1,0:T(8,128)S(1)} %get-tuple-element.53.refs_6_.refs_4_), channel_id=1, source_target_pairs={{0,1},{1,0},{2,3},{3,2},{4,5},{5,4},{6,7},{7,6},{8,9},{9,8},{10,11... | collective-permute-start | bytes 1572872 | tf_op jit(solution)/shard_map/ppermute | solution.py:623
  16.9 1.3 %collective-permute-start.1 = (f32[2,24,512]{2,1,0:T(8,128)S(1)}, f32[2,24,512]{2,1,0:T(8,128)S(1)}, u32[]{:S(2)}, u32[]{:S(2)}) collective-permute-start(f32[2,24,512]{2,1,0:T(8,128)S(1)} %get-tuple-element.54), channel_id=1, source_target_pairs={{0,2},{2,0},{4,6},{6,4},{8,10},{10,8},{12,14},{14,12},{16,18},{18,... | collective-permute-start | bytes 294920 | tf_op jit(solution)/shard_map/ppermute | solution.py:578
  16.9 1.3 %collective-permute-start.2 = (f32[2,24,512]{2,1,0:T(8,128)S(1)}, f32[2,24,512]{2,1,0:T(8,128)S(1)}, u32[]{:S(2)}, u32[]{:S(2)}) collective-permute-start(f32[2,24,512]{2,1,0:T(8,128)S(1)} %get-tuple-element.55), channel_id=1, source_target_pairs={{2,4},{4,2},{6,8},{8,6},{10,12},{12,10},{14,16},{16,14},{18,20},{2... | collective-permute-start | bytes 294920 | tf_op jit(solution)/shard_map/ppermute | solution.py:578
  26.8 6.1 %collective-permute-start.3 = (f32[3,8,512]{2,1,0:T(8,128)S(1)}, f32[3,8,512]{2,1,0:T(8,128)S(1)}, u32[]{:S(2)}, u32[]{:S(2)}) collective-permute-start(f32[3,8,512]{2,1,0:T(8,128)S(1)} %get-tuple-element.59.refs_3_), channel_id=1, source_target_pairs={{0,1},{1,0},{2,3},{3,2},{4,5},{5,4},{6,7},{7,6},{8,9},{9,8},{10,11... | collective-permute-start | bytes 147464 | tf_op jit(solution)/shard_map/ppermute | solution.py:578
  33.4 2.3 %collective-permute-start.5 = (f32[2,24,512]{2,1,0:T(8,128)S(1)}, f32[2,24,512]{2,1,0:T(8,128)S(1)}, u32[]{:S(2)}, u32[]{:S(2)}) collective-permute-start(f32[2,24,512]{2,1,0:T(8,128)S(1)} %get-tuple-element.65), channel_id=1, source_target_pairs={{0,2},{2,0},{4,6},{6,4},{8,10},{10,8},{12,14},{14,12},{16,18},{18,... | collective-permute-start | bytes 294920 | tf_op jit(solution)/shard_map/ppermute | solution.py:578
  33.5 2.2 %collective-permute-start.6 = (f32[2,24,512]{2,1,0:T(8,128)S(1)}, f32[2,24,512]{2,1,0:T(8,128)S(1)}, u32[]{:S(2)}, u32[]{:S(2)}) collective-permute-start(f32[2,24,512]{2,1,0:T(8,128)S(1)} %get-tuple-element.66), channel_id=1, source_target_pairs={{2,4},{4,2},{6,8},{8,6},{10,12},{12,10},{14,16},{16,14},{18,20},{2... | collective-permute-start | bytes 294920 | tf_op jit(solution)/shard_map/ppermute | solution.py:578
  36.9 19.6 %all-to-all-start.1 = ((f32[32,1,2176]{2,1,0:T(1,128)}), f32[32,1,2176]{2,1,0:T(1,128)S(1)}, u32[]{:S(2)}, u32[]{:S(2)}) async-start(f32[32,1,2176]{2,1,0:T(1,128)} %get-tuple-element.67), calls=%async_computation.1 | async-start | bytes 557056 | tf_op jit(solution)/shard_map/all_to_all | solution.py:583
  49.0 4.8 %collective-permute-start.8 = (f32[16,512]{1,0:T(8,128)S(1)}, f32[16,512]{1,0:T(8,128)S(1)}, u32[]{:S(2)}, u32[]{:S(2)}) collective-permute-start(f32[16,512]{1,0:T(8,128)S(1)} %get-tuple-element.71), channel_id=1, source_target_pairs={{0,2},{2,0},{4,6},{6,4},{8,10},{10,8},{12,14},{14,12},{16,18},{18,... | collective-permute-start | bytes 98312 | tf_op jit(solution)/shard_map/ppermute | solution.py:578
  49.3 4.5 %collective-permute-start.9 = (f32[16,512]{1,0:T(8,128)S(1)}, f32[16,512]{1,0:T(8,128)S(1)}, u32[]{:S(2)}, u32[]{:S(2)}) collective-permute-start(f32[16,512]{1,0:T(8,128)S(1)} %get-tuple-element.72), channel_id=1, source_target_pairs={{2,4},{4,2},{6,8},{8,6},{10,12},{12,10},{14,16},{16,14},{18,20},{2... | collective-permute-start | bytes 98312 | tf_op jit(solution)/shard_map/ppermute | solution.py:578
  50.0 3.9 %collective-permute-start.7 = (f32[8,512]{1,0:T(8,128)S(1)}, f32[8,512]{1,0:T(8,128)S(1)}, u32[]{:S(2)}, u32[]{:S(2)}) collective-permute-start(f32[8,512]{1,0:T(8,128)S(1)} %get-tuple-element.70), channel_id=1, source_target_pairs={{0,1},{1,0},{2,3},{3,2},{4,5},{5,4},{6,7},{7,6},{8,9},{9,8},{10,11... | collective-permute-start | bytes 49160 | tf_op jit(solution)/shard_map/ppermute | solution.py:578
